TPU v7x, 32 devices: a whole 2x2x4 slice. The times are simulated.
32 devices in a mesh: seq: 4 (over z), head: 8 (over y, x, core).
Axes of the slice: x: 2, y: 2, z: 4, core: 2. Of those that a mesh axis runs over, the one named last changes fastest.
Arguments:
- hidden_in: bfloat16 [4096, 2048], P(('seq', 'head')), may hold values from -6 to 6
- out_grad: bfloat16 [4096, 2048], P(('seq', 'head')), may hold values from -8 to 8
- decays: float32 [4096, 16], P('seq', 'head'), may hold values from 0.4 to 1
- strength: float32 [4096, 16], P('seq', 'head'), may hold values from 0.2 to 0.95
- mixer_in: float32 [2048, 16, 768], P('seq', 'head'), may hold values from -0.125 to 0.125
- mixer_in_rows: float32 [2048], P('seq'), may hold values from 204 to 819
- mixer_in_cols: float32 [16, 768], P('head'), may hold values from 204 to 819
- mixer_out: float32 [16, 256, 2048], P('head', None, 'seq'), may hold values from -0.125 to 0.125
- mixer_out_rows: float32 [16, 256], P('head'), may hold values from 341 to 1365
- mixer_out_cols: float32 [2048], P('seq'), may hold values from 341 to 1365
- feed_in: float32 [2048, 2, 5632], P('head', None, 'seq'), may hold values from -0.125 to 0.125
- feed_in_rows: float32 [2048], P('head'), may hold values from 68 to 273
- feed_in_cols: float32 [2, 5632], P(None, 'seq'), may hold values from 68 to 273
- feed_out: float32 [5632, 2048], P('seq', 'head'), may hold values from -0.078125 to 0.078125
- feed_out_rows: float32 [5632], P('seq'), may hold values from 292 to 1024
- feed_out_cols: float32 [2048], P('head'), may hold values from 292 to 1024
- conv_kernel: float32 [4, 16, 512], P(None, 'head', 'seq'), may hold values from -3 to 3
- conv_second: float32 [4, 16, 512], P(None, 'head', 'seq'), may hold values from 204 to 819
- norm_gains: float32 [2, 2048], replicated, may hold values from 0.35 to 2.8
- gains_second: float32 [2, 2048], replicated, may hold values from 819 to 3072
- head_gain: float32 [256], replicated, may hold values from 0.5 to 1.5
- head_gain_second: float32 [256], replicated, may hold values from 4681 to 16384
Outputs:
- block_out: bfloat16 [4096, 2048], P(('seq', 'head'))
- input_grad: float32 [4096, 2048], P(('seq', 'head'))
- mixer_in_grad: float32 [2048, 16, 768], P('seq', 'head')
- mixer_in_rows_new: float32 [2048], P('seq')
- mixer_in_cols_new: float32 [16, 768], P('head')
- mixer_in_new: float32 [2048, 16, 768], P('seq', 'head')
- mixer_out_grad: float32 [16, 256, 2048], P('head', None, 'seq')
- mixer_out_rows_new: float32 [16, 256], P('head')
- mixer_out_cols_new: float32 [2048], P('seq')
- mixer_out_new: float32 [16, 256, 2048], P('head', None, 'seq')
- feed_in_grad: float32 [2048, 2, 5632], P('head', None, 'seq')
- feed_in_rows_new: float32 [2048], P('head')
- feed_in_cols_new: float32 [2, 5632], P(None, 'seq')
- feed_in_new: float32 [2048, 2, 5632], P('head', None, 'seq')
- feed_out_grad: float32 [5632, 2048], P('seq', 'head')
- feed_out_rows_new: float32 [5632], P('seq')
- feed_out_cols_new: float32 [2048], P('head')
- feed_out_new: float32 [5632, 2048], P('seq', 'head')
- conv_grad: float32 [4, 16, 512], P(None, 'head', 'seq')
- conv_second_new: float32 [4, 16, 512], P(None, 'head', 'seq')
- conv_new: float32 [4, 16, 512], P(None, 'head', 'seq')
- gains_grad: float32 [2, 2048], replicated
- gains_second_new: float32 [2, 2048], replicated
- gains_new: float32 [2, 2048], replicated
- head_gain_grad: float32 [256], replicated
- head_gain_second_new: float32 [256], replicated
- head_gain_new: float32 [256], replicated
All inputs are finite; a program needn't handle non-finite values.
Results may differ from a plain program's by a relative error of at most 0.02.
Values may be sent and summed in bfloat16 or wider, within the bound.
No kernel may reach another device: no remote copies, remote signals or barrier semaphores. Data moves between devices by JAX's collectives and lax.ppermute only.
A program may use at most 256 MiB of HBM per device.

v0:
```python
import jax
import jax.numpy as jnp
from jax import lax
from jax.sharding import PartitionSpec as P

D = 2048
HEAD_TOTAL = 16
DK = 128
DV = 256
FF = 5632
KC = 4
BLOCK = 64
STEP = 10


HIGHEST = lax.Precision.HIGHEST


def passed_along(x, axis, by):
    count = lax.axis_size(axis)
    pairs = [(i, i + by) for i in range(count) if 0 <= i + by < count]
    return lax.ppermute(x, axis, pairs)


def norm_rows(entries, scale_row):
    return (
        entries * lax.rsqrt(jnp.mean(entries * entries, axis=-1, keepdims=True) + 1e-06) * scale_row
    )


def gate_norm(heads_rows, gate_part, gain_row):
    scaled = heads_rows * lax.rsqrt(
        jnp.mean(heads_rows * heads_rows, axis=-1, keepdims=True) + 1e-05
    )
    return scaled * gain_row * jax.nn.silu(gate_part)


def swiglu(gate_up):
    return jax.nn.silu(gate_up[:, 0]) * gate_up[:, 1]


def conv_piece(padded, kernel):
    length = padded.shape[0] - (KC - 1)
    summed = kernel[0] * padded[0:length]
    for offset in range(1, KC):
        summed = summed + kernel[offset] * padded[offset : offset + length]
    active = jax.nn.silu(summed)
    queries = active[..., :DK]
    key_rows = active[..., DK : 2 * DK]
    values = active[..., 2 * DK :]
    queries = (
        queries
        * lax.rsqrt(jnp.sum(queries * queries, axis=-1, keepdims=True) + 1e-06)
        * DK ** (-0.5)
    )
    key_rows = key_rows * lax.rsqrt(jnp.sum(key_rows * key_rows, axis=-1, keepdims=True) + 1e-06)
    return (queries, key_rows, values)


def block_parts(queries, key_rows, values, log_decay, write_gain):
    cumulated = jnp.cumsum(log_decay, axis=-1)
    block_len = cumulated.shape[-1]
    row_index = lax.broadcasted_iota(jnp.int32, (block_len, block_len), 0)
    col_index = lax.broadcasted_iota(jnp.int32, (block_len, block_len), 1)
    is_below = row_index > col_index
    within = row_index >= col_index
    spread = cumulated[..., :, None] - cumulated[..., None, :]
    decay_ratio = jnp.where(within, jnp.exp(jnp.where(within, spread, 0.0)), 0.0)
    key_dots = jnp.einsum("bncd,bnjd->bncj", key_rows, key_rows, precision=HIGHEST)
    strict_part = jnp.where(is_below, write_gain[..., :, None] * decay_ratio * key_dots, 0.0)
    system = strict_part + jnp.eye(block_len, dtype=strict_part.dtype)
    write_vals = lax.linalg.triangular_solve(
        system, write_gain[..., None] * values, left_side=True, lower=True, unit_diagonal=True
    )
    write_keys = lax.linalg.triangular_solve(
        system,
        (write_gain * jnp.exp(cumulated))[..., None] * key_rows,
        left_side=True,
        lower=True,
        unit_diagonal=True,
    )
    scores = jnp.where(
        within,
        decay_ratio * jnp.einsum("bncd,bnjd->bncj", queries, key_rows, precision=HIGHEST),
        0.0,
    )
    query_dec = queries * jnp.exp(cumulated)[..., None]
    key_dec = key_rows * jnp.exp(cumulated[..., -1:] - cumulated)[..., None]
    block_dec = jnp.exp(cumulated[..., -1])
    return (query_dec, key_dec, scores, write_keys, write_vals, block_dec)


def advance(state_now, pieces):
    update = pieces[4] - jnp.einsum("bcd,bde->bce", pieces[3], state_now, precision=HIGHEST)
    outputs = jnp.einsum("bcd,bde->bce", pieces[0], state_now, precision=HIGHEST) + jnp.einsum(
        "bcj,bje->bce", pieces[2], update, precision=HIGHEST
    )
    state_next = pieces[5][:, None, None] * state_now + jnp.einsum(
        "bcd,bce->bde", pieces[1], update, precision=HIGHEST
    )
    return (state_next, outputs)


def run_blocks(query_dec, key_dec, scores, write_keys, write_vals, block_dec, start_state):
    by_block = tuple(
        (
            jnp.moveaxis(member, 1, 0)
            for member in (query_dec, key_dec, scores, write_keys, write_vals, block_dec)
        )
    )
    last_state, outputs = lax.scan(advance, start_state, by_block)
    return (jnp.moveaxis(outputs, 0, 1), last_state)


def to_blocks(entries):
    return jnp.moveaxis(entries, 1, 0).reshape(
        entries.shape[1], entries.shape[0] // BLOCK, BLOCK, entries.shape[2]
    )


def from_blocks(entries):
    return jnp.moveaxis(entries.reshape(entries.shape[0], -1, entries.shape[3]), 0, 1)


def shift_rim(rim_rows, direction):
    return passed_along(rim_rows, "seq", direction)


def chain_maps(matrices, offsets, backward):
    direction = -1 if backward else 1
    state_now = jnp.zeros_like(offsets)
    for repeat in range(lax.axis_size("seq") - 1):
        moved_on = jnp.einsum("bij,bjk->bik", matrices, state_now, precision=HIGHEST) + offsets
        state_now = passed_along(moved_on, "seq", direction)
    return state_now


def placed(piece, full_shape, first_row, axis_dim):
    return lax.dynamic_update_slice_in_dim(
        jnp.zeros(full_shape, jnp.float32), piece, first_row, axis_dim
    )


def plain_update(weight, gradient, second_old, beta_two):
    second_new = beta_two * second_old + (1.0 - beta_two) * (gradient * gradient + 1e-30)
    update = gradient * lax.rsqrt(second_new)
    clipped = update / jnp.maximum(1.0, jnp.sqrt(jnp.mean(update * update, axis=-1, keepdims=True)))
    scale = 0.3 * jnp.maximum(0.001, jnp.sqrt(jnp.mean(weight * weight, axis=-1, keepdims=True)))
    return (second_new, weight - scale * clipped)


def factor_stats(
    rows_old, cols_old, row_sums, col_sums, total_sq, row_count, col_count, old_total, beta_two
):
    rows_new = beta_two * rows_old + (1.0 - beta_two) * (row_sums / col_count + 1e-30)
    cols_new = beta_two * cols_old + (1.0 - beta_two) * (col_sums / row_count + 1e-30)
    mean_rows = beta_two * old_total / row_count + (1.0 - beta_two) * (
        total_sq / (row_count * col_count) + 1e-30
    )
    return (rows_new, cols_new, mean_rows)


def finished(weight, update, weight_total, update_total, entry_count):
    scale = 0.3 * jnp.maximum(0.001, jnp.sqrt(weight_total / entry_count))
    return weight - scale * (update / jnp.maximum(1.0, jnp.sqrt(update_total / entry_count)))


def local(
    hidden_in,
    out_grad,
    decays,
    strength,
    mixer_in,
    mixer_in_rows,
    mixer_in_cols,
    mixer_out,
    mixer_out_rows,
    mixer_out_cols,
    feed_in,
    feed_in_rows,
    feed_in_cols,
    feed_out,
    feed_out_rows,
    feed_out_cols,
    conv_kernel,
    conv_second,
    norm_gains,
    gains_second,
    head_gain,
    head_gain_second,
):
    beta_two = 1.0 - STEP ** (-0.8)
    conv_width = 2 * DK + DV
    residual_in = hidden_in.astype(jnp.float32)
    in_weights, out_weights, kernel_low, grad_rows = (
        lax.all_gather(mixer_in.astype(jnp.bfloat16), "seq", axis=0, tiled=True),
        lax.all_gather(mixer_out.astype(jnp.bfloat16), "seq", axis=2, tiled=True),
        lax.all_gather(conv_kernel.astype(jnp.bfloat16), "seq", axis=2, tiled=True),
        lax.all_gather(out_grad, "seq", axis=0, tiled=True),
    )
    heads_here = in_weights.shape[1]
    head_cols = in_weights.shape[2]
    in_flat = in_weights.reshape(D, heads_here * head_cols)
    out_flat = out_weights.reshape(heads_here * DV, D)
    normed, norm_one_pull = jax.vjp(norm_rows, residual_in, norm_gains[0])
    block_rows, expand_low, shrink_low = (
        lax.all_gather(normed.astype(jnp.bfloat16), "head", axis=0, tiled=True),
        lax.all_gather(feed_in.astype(jnp.bfloat16), "head", axis=0, tiled=True),
        lax.all_gather(feed_out.astype(jnp.bfloat16), "head", axis=1, tiled=True),
    )
    mix_count = block_rows.shape[0]
    projected = jnp.dot(block_rows, in_flat, preferred_element_type=jnp.float32).reshape(
        mix_count, heads_here, head_cols
    )
    conv_in = projected[..., :conv_width]
    gate_in = projected[..., conv_width:]
    rim_rows = shift_rim(conv_in[mix_count - (KC - 1) :], 1)
    padded = jnp.concatenate([rim_rows, conv_in], 0)
    (queries, key_rows, values), conv_pull = jax.vjp(
        conv_piece, padded, kernel_low.astype(jnp.float32)
    )
    log_decay = to_blocks(jnp.log(decays)[..., None])[..., 0]
    write_gain = to_blocks(strength[..., None])[..., 0]

    def make_parts(query_part, key_part, value_part):
        return block_parts(query_part, key_part, value_part, log_decay, write_gain)

    block_data, parts_pull = jax.vjp(
        make_parts, to_blocks(queries), to_blocks(key_rows), to_blocks(values)
    )
    query_dec, key_dec, scores, write_keys, write_vals, block_dec = block_data
    eye_state = jnp.broadcast_to(jnp.eye(DK, dtype=jnp.float32), (heads_here, DK, DK))
    start_ext = jnp.concatenate([eye_state, jnp.zeros((heads_here, DK, DV), jnp.float32)], -1)
    vals_ext = jnp.concatenate(
        [jnp.zeros(write_vals.shape[:-1] + (DK,), jnp.float32), write_vals], -1
    )
    unused, carried = run_blocks(
        query_dec, key_dec, scores, write_keys, vals_ext, block_dec, start_ext
    )
    transfer = carried[..., :DK]
    start_state = chain_maps(transfer, carried[..., DK:], False)
    (mixer_heads, end_state), run_pull = jax.vjp(
        run_blocks, query_dec, key_dec, scores, write_keys, write_vals, block_dec, start_state
    )
    gated, gate_pull = jax.vjp(gate_norm, from_blocks(mixer_heads), gate_in, head_gain)
    gated_low = gated.astype(jnp.bfloat16).reshape(mix_count, heads_here * DV)
    row_block = gated_low
    mixed_rows = lax.psum_scatter(
        jnp.dot(row_block, out_flat, preferred_element_type=jnp.float32),
        "head",
        scatter_dimension=0,
        tiled=True,
    )
    residual = residual_in + mixed_rows
    normed_two, norm_two_pull = jax.vjp(norm_rows, residual, norm_gains[1])
    feed_rows = lax.all_gather(normed_two.astype(jnp.bfloat16), "seq", axis=0, tiled=True)
    gate_up = jnp.einsum("td,dkf->tkf", feed_rows, expand_low, preferred_element_type=jnp.float32)
    hidden, hidden_pull = jax.vjp(swiglu, gate_up)
    hidden_low = hidden.astype(jnp.bfloat16)
    row_block = hidden_low
    feed_sum = lax.psum_scatter(
        jnp.dot(row_block, shrink_low, preferred_element_type=jnp.float32).astype(jnp.bfloat16),
        "seq",
        scatter_dimension=0,
        tiled=True,
    ).astype(jnp.float32)
    block_out = (residual + feed_sum).astype(jnp.bfloat16)
    d_hidden = jnp.einsum("td,fd->tf", grad_rows, shrink_low, preferred_element_type=jnp.float32)
    shrink_grad_part = jnp.einsum(
        "tf,td->fd", hidden_low, grad_rows, preferred_element_type=jnp.float32
    )
    d_gate_up = hidden_pull(d_hidden)[0].astype(jnp.bfloat16)
    expand_grad_part = jnp.einsum(
        "td,tkf->dkf", feed_rows, d_gate_up, preferred_element_type=jnp.float32
    )
    row_block = d_gate_up
    d_normed_two = lax.psum_scatter(
        jnp.einsum("tkf,dkf->td", row_block, expand_low, preferred_element_type=jnp.float32).astype(
            jnp.bfloat16
        ),
        "seq",
        scatter_dimension=0,
        tiled=True,
    ).astype(jnp.float32)
    d_residual_part, d_gain_two = norm_two_pull(d_normed_two)
    d_residual = out_grad.astype(jnp.float32) + d_residual_part
    d_block = lax.all_gather(d_residual.astype(jnp.bfloat16), "head", axis=0, tiled=True)
    d_gated = jnp.einsum(
        "td,cd->tc", d_block, out_flat, preferred_element_type=jnp.float32
    ).reshape(mix_count, heads_here, DV)
    out_grad_part = jnp.einsum(
        "tc,td->cd", gated_low, d_block, preferred_element_type=jnp.float32
    ).reshape(heads_here, DV, D)
    d_heads, d_gate_in, d_head_gain = gate_pull(d_gated)
    d_heads_blocks = to_blocks(d_heads)
    first_pull = run_pull((d_heads_blocks, jnp.zeros_like(end_state)))
    state_grad = chain_maps(jnp.swapaxes(transfer, 1, 2), first_pull[6], True)
    second_pull = run_pull((jnp.zeros_like(d_heads_blocks), state_grad))
    d_data = tuple((first_pull[member] + second_pull[member] for member in range(6)))
    d_queries, d_keys, d_values = parts_pull(d_data)
    d_padded, d_kernel = conv_pull(
        (from_blocks(d_queries), from_blocks(d_keys), from_blocks(d_values))
    )
    rim_grad = shift_rim(d_padded[: KC - 1], -1)
    d_conv = d_padded[KC - 1 :]
    d_conv = jnp.concatenate(
        [d_conv[: mix_count - (KC - 1)], d_conv[mix_count - (KC - 1) :] + rim_grad], 0
    )
    d_projected = (
        jnp.concatenate([d_conv, d_gate_in], -1)
        .astype(jnp.bfloat16)
        .reshape(mix_count, heads_here * head_cols)
    )
    in_grad_part = jnp.einsum(
        "td,tc->dc", block_rows, d_projected, preferred_element_type=jnp.float32
    ).reshape(D, heads_here, head_cols)
    d_block_rows = jnp.einsum("tc,dc->td", d_projected, in_flat, preferred_element_type=jnp.float32)
    d_normed, expand_grad, shrink_grad = (
        lax.psum_scatter(
            d_block_rows.astype(jnp.bfloat16), "head", scatter_dimension=0, tiled=True
        ).astype(jnp.float32),
        lax.psum_scatter(
            expand_grad_part.astype(jnp.bfloat16), "head", scatter_dimension=0, tiled=True
        ).astype(jnp.float32),
        lax.psum_scatter(
            shrink_grad_part.astype(jnp.bfloat16), "head", scatter_dimension=1, tiled=True
        ).astype(jnp.float32),
    )
    d_residual_one, d_gain_one = norm_one_pull(d_normed)
    input_grad = d_residual + d_residual_one
    in_grad, mix_out_grad, kernel_grad = (
        lax.psum_scatter(
            in_grad_part.astype(jnp.bfloat16), "seq", scatter_dimension=0, tiled=True
        ).astype(jnp.float32),
        lax.psum_scatter(
            out_grad_part.astype(jnp.bfloat16), "seq", scatter_dimension=2, tiled=True
        ).astype(jnp.float32),
        lax.psum_scatter(
            d_kernel.astype(jnp.bfloat16), "seq", scatter_dimension=2, tiled=True
        ).astype(jnp.float32),
    )
    seq_pos = lax.axis_index("seq")
    head_pos = lax.axis_index("head")
    seq_count = lax.axis_size("seq")
    head_count = lax.axis_size("head")
    in_span = in_grad.shape[0]
    out_span = mix_out_grad.shape[2]
    expand_span = expand_grad.shape[0]
    hidden_span = shrink_grad.shape[0]
    in_sq = in_grad * in_grad
    out_sq = mix_out_grad * mix_out_grad
    expand_sq = expand_grad * expand_grad
    shrink_sq = shrink_grad * shrink_grad
    totals_part = jnp.stack(
        [
            jnp.sum(mixer_in * mixer_in),
            jnp.sum(mixer_out * mixer_out),
            jnp.sum(feed_in * feed_in),
            jnp.sum(feed_out * feed_out),
            jnp.sum(conv_kernel * conv_kernel),
            jnp.sum(mixer_in_rows) / head_count,
            jnp.sum(mixer_out_rows) / seq_count,
            jnp.sum(feed_in_rows) / seq_count,
            jnp.sum(feed_out_rows) / head_count,
        ]
    )
    summed = lax.psum(
        (
            jnp.stack([d_gain_one, d_gain_two]),
            d_head_gain,
            placed(jnp.sum(in_sq, axis=(1, 2)), (D,), seq_pos * in_span, 0),
            placed(jnp.sum(in_sq, axis=0), (HEAD_TOTAL, head_cols), head_pos * heads_here, 0),
            placed(jnp.sum(out_sq, axis=2), (HEAD_TOTAL, DV), head_pos * heads_here, 0),
            placed(jnp.sum(out_sq, axis=(0, 1)), (D,), seq_pos * out_span, 0),
            placed(jnp.sum(expand_sq, axis=(1, 2)), (D,), head_pos * expand_span, 0),
            placed(jnp.sum(expand_sq, axis=0), (2, FF), seq_pos * hidden_span, 1),
            placed(jnp.sum(shrink_sq, axis=1), (FF,), seq_pos * hidden_span, 0),
            placed(jnp.sum(shrink_sq, axis=0), (D,), head_pos * expand_span, 0),
            totals_part,
        ),
        ("seq", "head"),
    )
    (
        gains_grad,
        head_gain_grad,
        in_rows_full,
        in_cols_full,
        out_rows_full,
        out_cols_full,
        expand_rows_full,
        expand_cols_full,
        shrink_rows_full,
        shrink_cols_full,
        totals,
    ) = summed
    in_count = D * HEAD_TOTAL * head_cols
    out_count = HEAD_TOTAL * DV * D
    expand_count = D * 2 * FF
    shrink_count = FF * D
    conv_count = KC * HEAD_TOTAL * conv_width
    in_rows_new, in_cols_new, in_mean = factor_stats(
        mixer_in_rows,
        mixer_in_cols,
        lax.dynamic_slice_in_dim(in_rows_full, seq_pos * in_span, in_span, 0),
        lax.dynamic_slice_in_dim(in_cols_full, head_pos * heads_here, heads_here, 0),
        jnp.sum(in_rows_full),
        D,
        HEAD_TOTAL * head_cols,
        totals[5],
        beta_two,
    )
    out_rows_new, out_cols_new, out_mean = factor_stats(
        mixer_out_rows,
        mixer_out_cols,
        lax.dynamic_slice_in_dim(out_rows_full, head_pos * heads_here, heads_here, 0),
        lax.dynamic_slice_in_dim(out_cols_full, seq_pos * out_span, out_span, 0),
        jnp.sum(out_rows_full),
        HEAD_TOTAL * DV,
        D,
        totals[6],
        beta_two,
    )
    expand_rows_new, expand_cols_new, expand_mean = factor_stats(
        feed_in_rows,
        feed_in_cols,
        lax.dynamic_slice_in_dim(expand_rows_full, head_pos * expand_span, expand_span, 0),
        lax.dynamic_slice_in_dim(expand_cols_full, seq_pos * hidden_span, hidden_span, 1),
        jnp.sum(expand_rows_full),
        D,
        2 * FF,
        totals[7],
        beta_two,
    )
    shrink_rows_new, shrink_cols_new, shrink_mean = factor_stats(
        feed_out_rows,
        feed_out_cols,
        lax.dynamic_slice_in_dim(shrink_rows_full, seq_pos * hidden_span, hidden_span, 0),
        lax.dynamic_slice_in_dim(shrink_cols_full, head_pos * expand_span, expand_span, 0),
        jnp.sum(shrink_rows_full),
        FF,
        D,
        totals[8],
        beta_two,
    )
    in_update = in_grad * lax.rsqrt(in_rows_new[:, None, None] * in_cols_new[None] / in_mean)
    out_update = mix_out_grad * lax.rsqrt(
        out_rows_new[:, :, None] * out_cols_new[None, None, :] / out_mean
    )
    expand_update = expand_grad * lax.rsqrt(
        expand_rows_new[:, None, None] * expand_cols_new[None] / expand_mean
    )
    shrink_update = shrink_grad * lax.rsqrt(
        shrink_rows_new[:, None] * shrink_cols_new[None, :] / shrink_mean
    )
    conv_second_new = beta_two * conv_second + (1.0 - beta_two) * (
        kernel_grad * kernel_grad + 1e-30
    )
    conv_update = kernel_grad * lax.rsqrt(conv_second_new)
    update_totals = lax.psum(
        jnp.stack(
            [
                jnp.sum(in_update * in_update),
                jnp.sum(out_update * out_update),
                jnp.sum(expand_update * expand_update),
                jnp.sum(shrink_update * shrink_update),
                jnp.sum(conv_update * conv_update),
            ]
        ),
        ("seq", "head"),
    )
    in_new = finished(mixer_in, in_update, totals[0], update_totals[0], in_count)
    out_new = finished(mixer_out, out_update, totals[1], update_totals[1], out_count)
    expand_new = finished(feed_in, expand_update, totals[2], update_totals[2], expand_count)
    shrink_new = finished(feed_out, shrink_update, totals[3], update_totals[3], shrink_count)
    conv_new = finished(conv_kernel, conv_update, totals[4], update_totals[4], conv_count)
    gains_second_new, gains_new = plain_update(norm_gains, gains_grad, gains_second, beta_two)
    head_second_new, head_new = plain_update(
        head_gain[None], head_gain_grad[None], head_gain_second[None], beta_two
    )
    return (
        block_out,
        input_grad,
        in_grad,
        in_rows_new,
        in_cols_new,
        in_new,
        mix_out_grad,
        out_rows_new,
        out_cols_new,
        out_new,
        expand_grad,
        expand_rows_new,
        expand_cols_new,
        expand_new,
        shrink_grad,
        shrink_rows_new,
        shrink_cols_new,
        shrink_new,
        kernel_grad,
        conv_second_new,
        conv_new,
        gains_grad,
        gains_second_new,
        gains_new,
        head_gain_grad,
        head_second_new[0],
        head_new[0],
    )


def solution(mesh):
    return jax.shard_map(
        local,
        mesh=mesh,
        in_specs=(
            P(("seq", "head"), None),
            P(("seq", "head"), None),
            P("seq", "head"),
            P("seq", "head"),
            P("seq", "head", None),
            P("seq"),
            P("head", None),
            P("head", None, "seq"),
            P("head", None),
            P("seq"),
            P("head", None, "seq"),
            P("head"),
            P(None, "seq"),
            P("seq", "head"),
            P("seq"),
            P("head"),
            P(None, "head", "seq"),
            P(None, "head", "seq"),
            P(),
            P(),
            P(),
            P(),
        ),
        out_specs=(
            P(("seq", "head"), None),
            P(("seq", "head"), None),
            P("seq", "head", None),
            P("seq"),
            P("head", None),
            P("seq", "head", None),
            P("head", None, "seq"),
            P("head", None),
            P("seq"),
            P("head", None, "seq"),
            P("head", None, "seq"),
            P("head"),
            P(None, "seq"),
            P("head", None, "seq"),
            P("seq", "head"),
            P("seq"),
            P("head"),
            P("seq", "head"),
            P(None, "head", "seq"),
            P(None, "head", "seq"),
            P(None, "head", "seq"),
            P(),
            P(),
            P(),
            P(),
            P(),
            P(),
        ),
        check_vma=False,
    )
```

profile of v0, /device:TPU:0, one launch (start us, length us, event | category | flops | bytes accessed | tf_op | source)
XLA Modules:
  0.0 2146.4 jit_solution(1601265064099040305)
XLA Ops:
  13.8 12.8 all_gather.27
  30.5 98.2 %all-gather.11.cloned.1.call-done = bf16[2048,2,768]{2,0,1:T(8,128)(2,1)} async-done(((bf16[512,2,768]{2,0,1:T(8,128)(2,1)}), bf16[2048,2,768]{2,0,1:T(8,128)(2,1)}) %all-gather.11.cloned.1.call-update) | async-done | bytes 6291472 | tf_op jit(solution)/shard_map/all_gather | solution.py:196
  128.8 8.7 copy.147
  137.5 28.6 %all-gather.9.cloned.1.call-done = bf16[1024,2048]{1,0:T(8,128)(2,1)} async-done(((bf16[128,2048]{1,0:T(8,128)(2,1)}), bf16[1024,2048]{1,0:T(8,128)(2,1)}) %all-gather.9.cloned.1.call-update) | async-done | bytes 4194320 | tf_op jit(solution)/shard_map/all_gather | solution.py:207
  166.2 10.1 fusion.111
  198.3 158.0 %custom-call.12 = f32[2,16,1,64,64]{3,4,2,1,0:T(8,128)S(1)} custom-call(f32[2,16,1,64,64]{4,3,2,1,0:T(8,128)} %fusion.157), custom_call_target="InvertDiagBlocksLowerTriangular" | custom-call | tf_op jit(solution)/shard_map/jvp()/triangular_solve | solution.py:75
  366.2 55.2 %while.77 = (s32[]{:T(128)}, f32[2,128,384]{2,1,0:T(8,128)S(1)}, f32[16,2]{1,0:T(8,128)}, f32[16,2,64,128]{3,2,1,0:T(8,128)}, f32[16,2,64,384]{3,2,0,1:T(8,128)}, /*index=5*/f32[16,2,64,128]{3,2,1,0:T(8,128)S(1)}, s32[]{:T(128)}) while((s32[]{:T(128)}, f32[2,128,384]{2,1,0:T(8,128)S(1)}, f32[16,2]{1,0:T(8,128)}, f32[16,2,64,128]{3,2,1,0:T(8,128)}, ...), condition=%wide.region_4.5_spmd, body=%wide.region_3.4_spmd.sunk | while | flops 151240704 | bytes 1901685 | solution.py:111
  439.9 9.3 collective-permute-done.2
  449.5 8.8 collective-permute-start.3
  472.5 138.7 %while.78 = (s32[]{:T(128)}, f32[2,128,256]{2,1,0:T(8,128)S(1)}, f32[16,2,64,256]{3,2,1,0:T(8,128)}, f32[16,2,128,256]{3,2,1,0:T(8,128)}, f32[16,2,64,256]{3,2,1...) while((s32[]{:T(128)}, f32[2,128,256]{2,1,0:T(8,128)S(1)}, ...), condition=%wide.region_7.8_spmd, body=%wide.region_6.7_spmd.sunk | while | flops 176357376 | bytes 2886833 | solution.py:111
  627.7 77.2 %reduce-scatter.12.cloned.1.call-done = f32[128,2048]{1,0:T(8,128)} async-done(((f32[1024,2048]{1,0:T(8,128)}), f32[128,2048]{1,0:T(8,128)}) %reduce-scatter.12.cloned.1.call-update) | async-done | bytes 1048592 | tf_op jit(solution)/shard_map/reduce_scatter | solution.py:248
  714.0 61.0 %all-gather.17.cloned.1.call-done = bf16[2048,2,1408]{2,0,1:T(8,128)(2,1)} async-done(((bf16[256,2,1408]{2,0,1:T(8,128)(2,1)}), bf16[2048,2,1408]{2,0,1:T(8,128)(2,1)}) %all-gather.17.cloned.1.call-update) | async-done | bytes 11534352 | tf_op jit(solution)/shard_map/all_gather | solution.py:208
  775.1 48.0 %all-gather.15.cloned.1.call-done = bf16[512,2048]{1,0:T(8,128)(2,1)} async-done(((bf16[128,2048]{1,0:T(8,128)(2,1)}), bf16[512,2048]{1,0:T(8,128)(2,1)}) %all-gather.15.cloned.1.call-update) | async-done | bytes 2097168 | tf_op jit(solution)/shard_map/all_gather | solution.py:256
  823.1 12.5 fusion.135
  835.6 33.9 %all-gather.21.cloned.1.call-done = bf16[512,2048]{1,0:T(8,128)(2,1)} async-done(((bf16[128,2048]{1,0:T(8,128)(2,1)}), bf16[512,2048]{1,0:T(8,128)(2,1)}) %all-gather.21.cloned.1.call-update) | async-done | bytes 2097168 | tf_op jit(solution)/shard_map/all_gather | solution.py:199
  869.5 45.7 %all-gather.19.cloned.1.call-done = bf16[1408,2048]{1,0:T(8,128)(2,1)} async-done(((bf16[1408,256]{1,0:T(8,128)(2,1)}), bf16[1408,2048]{1,0:T(8,128)(2,1)}) %all-gather.19.cloned.1.call-update) | async-done | bytes 5767184 | tf_op jit(solution)/shard_map/all_gather | solution.py:209
  915.2 10.4 multiply_bitcast_fusion
  928.1 10.1 bitcast_convert_fusion.1
  938.2 44.0 %reduce-scatter.16.cloned.1.call-done = bf16[128,2048]{1,0:T(8,128)(2,1)} async-done(((bf16[512,2048]{1,0:T(8,128)(2,1)}), bf16[128,2048]{1,0:T(8,128)(2,1)}) %reduce-scatter.16.cloned.1.call-update) | async-done | bytes 524304 | tf_op jit(solution)/shard_map/reduce_scatter | solution.py:277
  990.5 33.5 %all-gather.23.cloned.1.call-done = bf16[1024,2048]{1,0:T(8,128)(2,1)} async-done(((bf16[128,2048]{1,0:T(8,128)(2,1)}), bf16[1024,2048]{1,0:T(8,128)(2,1)}) %all-gather.23.cloned.1.call-update) | async-done | bytes 4194320 | tf_op jit(solution)/shard_map/all_gather | solution.py:287
  1042.9 214.5 %while.80 = (s32[]{:T(128)}, f32[2,128,256]{2,1,0:T(8,128)S(1)}, f32[16,2,64,128]{3,2,0,1:T(8,128)}, f32[16,2,64,128]{3,2,0,1:T(8,128)}, f32[16,2,64,64]{3,2,0,1...) while((s32[]{:T(128)}, f32[2,128,256]{2,1,0:T(8,128)S(1)}, ...), condition=%wide.region_16.17_spmd.clone, body=%wide.region_15.16_spmd.clone.sunk | while | flops 352813056 | bytes 4203239 | solution.py:111
  1259.1 9.1 collective-permute-done.4
  1292.7 207.8 %while.79 = (s32[]{:T(128)}, f32[2,128,256]{2,1,0:T(8,128)S(1)}, f32[16,2,64,128]{3,2,0,1:T(8,128)}, f32[16,2,64,128]{3,2,0,1:T(8,128)}, f32[16,2,64,64]{3,2,0,1...) while((s32[]{:T(128)}, f32[2,128,256]{2,1,0:T(8,128)S(1)}, ...), condition=%wide.region_18.19_spmd, body=%wide.region_17.18_spmd.sunk | while | flops 352616448 | bytes 3675345 | solution.py:111
  1538.0 12.2 convolution_convert_fusion
  1569.1 11.1 bitcast_convert_fusion
  1591.3 11.5 convolution_convert_fusion.2
  1632.4 55.2 %reduce-scatter.24.cloned.1.call-done = bf16[256,2,1408]{2,0,1:T(8,128)(2,1)} async-done(((bf16[2048,2,1408]{2,0,1:T(8,128)(2,1)}), bf16[256,2,1408]{2,0,1:T(8,128)(2,1)}) %reduce-scatter.24.cloned.1.call-update) | async-done | bytes 1441808 | tf_op jit(solution)/shard_map/reduce_scatter | solution.py:322
  1694.3 48.2 %reduce-scatter.18.cloned.1.call-done = bf16[128,2048]{1,0:T(8,128)(2,1)} async-done(((bf16[1024,2048]{1,0:T(8,128)(2,1)}), bf16[128,2048]{1,0:T(8,128)(2,1)}) %reduce-scatter.18.cloned.1.call-update) | async-done | bytes 524304 | tf_op jit(solution)/shard_map/reduce_scatter | solution.py:319
  1744.3 44.8 %reduce-scatter.14.cloned.1.call-done = bf16[128,2048]{1,0:T(8,128)(2,1)} async-done(((bf16[512,2048]{1,0:T(8,128)(2,1)}), bf16[128,2048]{1,0:T(8,128)(2,1)}) %reduce-scatter.14.cloned.1.call-update) | async-done | bytes 524304 | tf_op jit(solution)/shard_map/reduce_scatter | solution.py:261
  1792.8 108.7 %reduce-scatter.20.cloned.1.call-done = bf16[512,2,768]{2,0,1:T(8,128)(2,1)} async-done(((bf16[2048,2,768]{2,0,1:T(8,128)(2,1)}), bf16[512,2,768]{2,0,1:T(8,128)(2,1)}) %reduce-scatter.20.cloned.1.call-update) | async-done | bytes 1572880 | tf_op jit(solution)/shard_map/reduce_scatter | solution.py:332
  1909.1 129.4 %all-reduce.19.cloned.1.call-done = (f32[2048]{0:T(1024)}, f32[16,768]{1,0:T(8,128)}, f32[9]{0:T(128)}, f32[16,256]{1,0:T(8,128)}, f32[2048]{0:T(1024)}, /*index...) async-done(((f32[2048]{0:T(1024)}, f32[16,768]{1,0:T(8,128)}, f32[9]{0:T(128)}, f32[16,256]{1,0:T(8,128)}, f32[2048]{0:T(1024)}, ...) | async-done | bytes 165940 | tf_op jit(solution)/shard_map/psum | solution.py:367
  2069.7 41.9 %all-reduce.15 = (f32[5]{0:T(128)S(1)}, f32[2,2048]{1,0:T(2,128)}, f32[256]{0:T(256)}) all-reduce(f32[5]{0:T(128)S(1)} %stack.68, f32[2,2048]{1,0:T(2,128)S(1)} %pad_maximum_fusion.1, f32[256]{0:T(256)S(1)} %get-tuple-element.987), channel_id=1, replica_groups=mesh['seq'=4,'head'=8] {'seq','head'}, use_global_device_ids=true, to_apply=%region_67.69 | all-reduce | flops 4357 | bytes 34856 | tf_op jit(solution)/shard_map/psum | solution.py:459
  (970 shorter events, 929.0 us)
Async XLA Ops:
  7.2 121.5 %all-gather.11.cloned.1.call-start = ((), (), s32[]{:S(2)}) async-start(), calls=%async_computation.10 | async-start | bytes 7864320 | tf_op jit(solution)/shard_map/all_gather | solution.py:196
  10.6 155.6 %all-gather.9.cloned.1.call-start = ((), (), s32[]{:S(2)}) async-start(), calls=%async_computation.9 | async-start | bytes 4718592 | tf_op jit(solution)/shard_map/all_gather | solution.py:207
  13.0 603.9 %all-gather.13.cloned.1.call-start = ((), (), s32[]{:S(2)}) async-start(), calls=%async_computation.11 | async-start | bytes 2621440 | tf_op jit(solution)/shard_map/all_gather | solution.py:197
  29.8 156.6 %copy-start.88 = (f32[2,512]{1,0:T(2,128)}, f32[2,512]{1,0:T(2,128)S(1)}, u32[]{:S(2)}) copy-start(f32[2,512]{1,0:T(2,128)S(1)} %get-tuple-element.1160) | copy-start | bytes 12292
  178.8 7.5 collective-permute-start
  193.8 264.6 %copy-start.3 = (f32[1024,2,128]{2,0,1:T(8,128)}, f32[1024,2,128]{2,0,1:T(8,128)S(1)}, u32[]{:S(2)}) copy-start(f32[1024,2,128]{2,0,1:T(8,128)S(1)} %get-tuple-element.1145) | copy-start | bytes 3145732
  193.8 264.6 %copy-start.20 = (f32[1024,2,128]{2,0,1:T(8,128)}, f32[1024,2,128]{2,0,1:T(8,128)S(1)}, u32[]{:S(2)}) copy-start(f32[1024,2,128]{2,0,1:T(8,128)S(1)} %get-tuple-element.1144) | copy-start | bytes 3145732
  422.4 9.4 collective-permute-start.1
  429.7 275.2 %reduce-scatter.12.cloned.1.call-start = ((), (), s32[]{:S(2)}) async-start(), calls=%async_computation.12 | async-start | bytes 9437184 | tf_op jit(solution)/shard_map/reduce_scatter | solution.py:248
  433.1 16.0 collective-permute-start.2
  449.5 19.9 collective-permute-start.3
  624.5 150.6 %all-gather.17.cloned.1.call-start = ((), (), s32[]{:S(2)}) async-start(), calls=%async_computation.14 | async-start | bytes 12976128 | tf_op jit(solution)/shard_map/all_gather | solution.py:208
  627.6 195.5 %all-gather.15.cloned.1.call-start = ((), (), s32[]{:S(2)}) async-start(), calls=%async_computation.13 | async-start | bytes 2621440 | tf_op jit(solution)/shard_map/all_gather | solution.py:256
  706.5 278.3 %copy-start.11 = (f32[128,2048]{1,0:T(8,128)}, f32[128,2048]{1,0:T(8,128)S(1)}, u32[]{:S(2)}) copy-start(f32[128,2048]{1,0:T(8,128)S(1)} %get-tuple-element.1126) | copy-start | bytes 3145732
  709.2 160.3 %all-gather.21.cloned.1.call-start = ((), (), s32[]{:S(2)}) async-start(), calls=%async_computation.17 | async-start | bytes 2621440 | tf_op jit(solution)/shard_map/all_gather | solution.py:199
  709.9 205.3 %all-gather.19.cloned.1.call-start = ((), (), s32[]{:S(2)}) async-start(), calls=%async_computation.15 | async-start | bytes 6488064 | tf_op jit(solution)/shard_map/all_gather | solution.py:209
  713.6 268.6 %reduce-scatter.16.cloned.1.call-start = ((), (), s32[]{:S(2)}) async-start(), calls=%async_computation.18 | async-start | bytes 2621440 | tf_op jit(solution)/shard_map/reduce_scatter | solution.py:277
  938.1 85.8 %all-gather.23.cloned.1.call-start = ((), (), s32[]{:S(2)}) async-start(), calls=%async_computation.19 | async-start | bytes 4718592 | tf_op jit(solution)/shard_map/all_gather | solution.py:287
  987.7 636.7 %reduce-scatter.26.cloned.1.call-start = ((), (), s32[]{:S(2)}) async-start(), calls=%async_computation.24 | async-start | bytes 6488064 | tf_op jit(solution)/shard_map/reduce_scatter | solution.py:325
  1257.8 10.4 collective-permute-start.4
  1268.6 9.5 collective-permute-start.5
  1278.6 9.1 collective-permute-start.6
  1287.6 340.2 %reduce-scatter.28.cloned.1.call-start = ((), (), s32[]{:S(2)}) async-start(), calls=%async_computation.25 | async-start | bytes 163840
  1292.7 207.8 %copy-start.16 = (f32[16,2,64,256]{3,2,0,1:T(8,128)S(1)}, f32[16,2,64,256]{3,2,0,1:T(8,128)}, u32[]{:S(2)}) copy-start(f32[16,2,64,256]{3,2,0,1:T(8,128)} %get-tuple-element.1681) | copy-start | bytes 6291460
  1532.0 98.0 %reduce-scatter.22.cloned.1.call-start = ((), (), s32[]{:S(2)}) async-start(), calls=%async_computation.22 | async-start | bytes 2621440 | tf_op jit(solution)/shard_map/reduce_scatter | solution.py:335
  1537.9 149.7 %reduce-scatter.24.cloned.1.call-start = ((), (), s32[]{:S(2)}) async-start(), calls=%async_computation.23 | async-start | bytes 12976128 | tf_op jit(solution)/shard_map/reduce_scatter | solution.py:322
  1550.2 192.3 %reduce-scatter.18.cloned.1.call-start = ((), (), s32[]{:S(2)}) async-start(), calls=%async_computation.20 | async-start | bytes 4718592 | tf_op jit(solution)/shard_map/reduce_scatter | solution.py:319
  1558.2 9.4 collective-permute-start.7
  1580.2 208.9 %reduce-scatter.14.cloned.1.call-start = ((), (), s32[]{:S(2)}) async-start(), calls=%async_computation.16 | async-start | bytes 2621440 | tf_op jit(solution)/shard_map/reduce_scatter | solution.py:261
  1588.3 313.2 %reduce-scatter.20.cloned.1.call-start = ((), (), s32[]{:S(2)}) async-start(), calls=%async_computation.21 | async-start | bytes 7864320 | tf_op jit(solution)/shard_map/reduce_scatter | solution.py:332
  1602.8 435.8 %all-reduce.19.cloned.1.call-start = ((), (), s32[]{:S(2)}) async-start(), calls=%async_computation.26 | async-start | bytes 336896 | tf_op jit(solution)/shard_map/psum | solution.py:367
  1744.3 160.1 %copy-start.92 = (f32[2048]{0:T(1024)S(1)}, f32[2048]{0:T(1024)}, u32[]{:S(2)}) copy-start(f32[2048]{0:T(1024)} %get-tuple-element.997) | copy-start | bytes 24580
  (137 other events, 3214.4 us)
Sparse Core Ops, SparseCore 0:
  10.7 118.0 all-gather.10
  131.2 34.8 all-gather.8
  429.8 51.0 all-gather.12
  624.6 80.2 reduce-scatter.11
  707.4 67.6 all-gather.16
  777.1 45.9 all-gather.14
  824.8 44.6 all-gather.20
  872.1 43.0 all-gather.18
  938.3 43.8 reduce-scatter.15
  987.8 36.0 all-gather.22
  1287.7 60.2 reduce-scatter.25
  1532.1 20.5 reduce-scatter.27
  1555.5 42.3 reduce-scatter.21
  1601.6 85.9 reduce-scatter.23
  1691.2 51.2 reduce-scatter.17
  1745.3 43.8 reduce-scatter.13
  1791.4 110.0 reduce-scatter.19
  1910.6 127.9 all-reduce.18
where the time goes:
time: 2170 us; the launch traced here: 2150 us
  waiting for transfers between devices  892 us (41%)
  matrix products  691 us (32%)
  other arithmetic  274 us (13%)
  local copies, waits for them, and re-layouts  172 us (8%)
  blocking collectives  54.7 us (3%)
  between operations  32.7 us (2%)
  starting transfers between devices  27.8 us (1%)
    another operation x4, other arithmetic, block_parts(): lax.linalg.triangular_solve(system, (write_gain * jnp.exp(cumulated))[......  159 us
    dot_general x96, matrix products, advance(): jnp.einsum('bcd,bde->bce', pieces[3], state_now, precision=HIGHEST)  154 us
    dot_general x96, matrix products, advance(): jnp.einsum('bcd,bce->bde', pieces[1], update, precision=HIGHEST)  140 us
    psum x1, waiting for transfers between devices, local(): lax.psum((jnp.stack([d_gain_one, d_gain_two]), d_head_gain, placed(jnp.su...  129 us
    dot_general x80, matrix products, advance(): jnp.einsum('bcd,bde->bce', pieces[0], state_now, precision=HIGHEST)  123 us
    dot_general x80, matrix products, advance(): jnp.einsum('bcj,bje->bce', pieces[2], update, precision=HIGHEST)  123 us
    reduce_scatter x1, waiting for transfers between devices, local(): lax.psum_scatter(in_grad_part.astype(jnp.bfloat16), 'seq', scatter_dimens...  109 us
    all_gather x1, waiting for transfers between devices, local(): lax.all_gather(mixer_in.astype(jnp.bfloat16), 'seq', axis=0, tiled=True)  98.2 us
  transfers between devices with their start and end apart: 26, of which 19 were waited for; matrix products, arithmetic and copies ran while one was open for 26% of the time, Pallas kernels for 0%

commit v1 on v0

v1 whole, which is shorter than its diff:
```python
import functools
import jax
import jax.numpy as jnp
from jax import lax
from jax.experimental import pallas as pl
from jax.experimental.pallas import tpu as pltpu
from jax.sharding import PartitionSpec as P

DK = 128
DV = 256
KC = 4
D = 2048
HEAD_TOTAL = 16
FF = 5632
STEP = 10
CH = 128
HC = 2 * DK + 2 * DV
CW = 2 * DK + DV
F32 = jnp.float32
BF = jnp.bfloat16


def mm(a, b, dims=((1,), (0,))):
    return lax.dot_general(a.astype(BF), b.astype(BF), (dims, ((), ())), preferred_element_type=F32)


def mm3(a, b, dims=((1,), (0,))):
    ah, bh = a.astype(BF), b.astype(BF)
    al, bl = (a - ah.astype(F32)).astype(BF), (b - bh.astype(F32)).astype(BF)
    one = functools.partial(lax.dot_general, dimension_numbers=(dims, ((), ())), preferred_element_type=F32)
    return one(ah, bh) + (one(ah, bl) + one(al, bh))


TT = ((1,), (1,))
TL = ((0,), (0,))


def sigmoid(v):
    return 1.0 / (1.0 + jnp.exp(-v))


def masks():
    rows = lax.broadcasted_iota(jnp.int32, (CH, CH), 0)
    cols = lax.broadcasted_iota(jnp.int32, (CH, CH), 1)
    return rows, cols


def invert(strict, rows, cols):
    x = jnp.where(rows == cols, 1.0, 0.0) - jnp.where((rows ^ cols) == 1, strict, 0.0)
    size = 2
    while size < CH:
        below = ((rows ^ cols) >= size) & ((rows ^ cols) < 2 * size)
        part = jnp.where(below, strict, 0.0)
        x = x - mm3(mm3(x, part), x)
        size *= 2
    return x


def k1(heads, proj_ref, halo_ref, taps_ref, gcol_ref, grow_ref,
       sum_ref, q_ref, k_ref, tinv_ref, a_ref, w_ref, uv_ref, qe_ref, oz_ref, m_ref, pre_ref, last_ref, x_ref):
    c = pl.program_id(0)
    rows, cols = masks()

    @pl.when(c == 0)
    def _():
        eye = jnp.where(rows == cols, 1.0, 0.0)
        for h in range(heads):
            x_ref[h] = jnp.concatenate([eye, jnp.zeros((CH, DV), F32)], 1)

    for h in range(heads):
        at = h * HC
        ext = jnp.concatenate([halo_ref[:, at:at + CW], proj_ref[:, at:at + CW]], 0)
        summed = taps_ref[0:1, h * CW:(h + 1) * CW] * ext[5:5 + CH]
        for j in range(1, KC):
            summed = summed + taps_ref[j:j + 1, h * CW:(h + 1) * CW] * ext[5 + j:5 + j + CH]
        sum_ref[:, h * CW:(h + 1) * CW] = summed
        act = summed * sigmoid(summed)
        q = act[:, :DK]
        k = act[:, DK:2 * DK]
        v = act[:, 2 * DK:]
        q = q * (lax.rsqrt(jnp.sum(q * q, axis=-1, keepdims=True) + 1e-6) * DK ** -0.5)
        k = k * lax.rsqrt(jnp.sum(k * k, axis=-1, keepdims=True) + 1e-6)
        gcol = gcol_ref[:, h:h + 1]
        beta = gcol_ref[:, heads + h:heads + h + 1]
        grow = grow_ref[0, h:h + 1, :]
        glast = grow[:, CH - 1:CH]
        ratio = jnp.exp(jnp.where(rows >= cols, gcol - grow, -1e30))
        kk = mm3(k, k, TT)
        strict = jnp.where(rows > cols, beta * ratio * kk, 0.0)
        tinv = invert(strict, rows, cols)
        a = ratio * mm(q, k, TT)
        eg = jnp.exp(gcol)
        kd = k * jnp.exp(glast - gcol)
        w = mm3(tinv, (beta * eg) * k)
        uv = mm3(tinv, beta * v)
        qe = q * eg - mm(a, w)
        oz = mm(a, uv)
        m = jnp.where(rows == cols, jnp.exp(glast), 0.0) - mm(kd, w, TL)
        b = mm(kd, uv, TL)
        x = x_ref[h]
        pre_ref[0, h] = x
        x = mm(m, x) + jnp.concatenate([jnp.zeros((CH, DK), F32), b], 1)
        x_ref[h] = x
        last_ref[h] = x
        q_ref[:, h * DK:(h + 1) * DK] = q.astype(BF)
        k_ref[:, h * DK:(h + 1) * DK] = k.astype(BF)
        tinv_ref[0, h] = tinv.astype(BF)
        a_ref[0, h] = a.astype(BF)
        w_ref[:, h * DK:(h + 1) * DK] = w.astype(BF)
        uv_ref[:, h * DV:(h + 1) * DV] = uv
        qe_ref[:, h * DK:(h + 1) * DK] = qe.astype(BF)
        oz_ref[:, h * DV:(h + 1) * DV] = oz
        m_ref[0, h] = m.astype(BF)


def whole(shape):
    return pl.BlockSpec(shape, lambda c: (0,) * len(shape))


def by_rows(width, n, back=False):
    return pl.BlockSpec((CH, width), (lambda c: (n - 1 - c, 0)) if back else (lambda c: (c, 0)))


def by_chunk(shape, n, back=False):
    tail = (0,) * len(shape)
    return pl.BlockSpec((1,) + shape, (lambda c: (n - 1 - c,) + tail) if back else (lambda c: (c,) + tail))


def sds(shape, dt=F32):
    return jax.ShapeDtypeStruct(shape, dt)


PARAMS = pltpu.CompilerParams(vmem_limit_bytes=48 * 1024 * 1024, dimension_semantics=("arbitrary",))


def forward_parts(proj, taps, gcol, grow, tokens, heads):
    n = tokens // CH
    extra = proj.shape[0] // 8 - 1
    halo = pl.BlockSpec((8, heads * HC), lambda c: (jnp.where(c == 0, extra, c * (CH // 8) - 1), 0))
    return pl.pallas_call(
        functools.partial(k1, heads),
        grid=(n,),
        in_specs=[by_rows(heads * HC, n), halo, whole(taps.shape), by_rows(gcol.shape[1], n),
                  by_chunk(grow.shape[1:], n)],
        out_specs=[by_rows(heads * CW, n), by_rows(heads * DK, n), by_rows(heads * DK, n),
                   by_chunk((heads, CH, CH), n), by_chunk((heads, CH, CH), n),
                   by_rows(heads * DK, n), by_rows(heads * DV, n), by_rows(heads * DK, n), by_rows(heads * DV, n),
                   by_chunk((heads, DK, DK), n), by_chunk((heads, DK, DK + DV), n), whole((heads, DK, DK + DV))],
        out_shape=[sds((tokens, heads * CW)), sds((tokens, heads * DK), BF), sds((tokens, heads * DK), BF),
                   sds((n, heads, CH, CH), BF), sds((n, heads, CH, CH), BF),
                   sds((tokens, heads * DK), BF), sds((tokens, heads * DV)), sds((tokens, heads * DK), BF),
                   sds((tokens, heads * DV)), sds((n, heads, DK, DK), BF), sds((n, heads, DK, DK + DV)),
                   sds((heads, DK, DK + DV))],
        scratch_shapes=[pltpu.VMEM((heads, DK, DK + DV), F32)],
        compiler_params=PARAMS,
        name="delta_forward_parts",
    )(proj, proj, taps, gcol, grow)


def k2(heads, start_ref, pre_ref, qe_ref, oz_ref, proj_ref, gain_ref, s_ref, o_ref, gated_ref):
    for h in range(heads):
        pre = pre_ref[0, h]
        s = mm(pre[:, :DK], start_ref[h]) + pre[:, DK:]
        s_ref[0, h] = s.astype(BF)
        o = mm(qe_ref[:, h * DK:(h + 1) * DK], s) + oz_ref[:, h * DV:(h + 1) * DV]
        o_ref[:, h * DV:(h + 1) * DV] = o
        gate = proj_ref[:, h * HC + CW:(h + 1) * HC]
        n = o * lax.rsqrt(jnp.mean(o * o, axis=-1, keepdims=True) + 1e-5)
        gated_ref[:, h * DV:(h + 1) * DV] = (n * gain_ref[...] * (gate * sigmoid(gate))).astype(BF)


def forward_outputs(start, pre, qe, oz, proj, gain, tokens, heads):
    n = tokens // CH
    return pl.pallas_call(
        functools.partial(k2, heads),
        grid=(n,),
        in_specs=[whole(start.shape), by_chunk((heads, DK, DK + DV), n), by_rows(heads * DK, n), by_rows(heads * DV, n),
                  by_rows(heads * HC, n), whole((1, DV))],
        out_specs=[by_chunk((heads, DK, DV), n), by_rows(heads * DV, n), by_rows(heads * DV, n)],
        out_shape=[sds((n, heads, DK, DV), BF), sds((tokens, heads * DV)), sds((tokens, heads * DV), BF)],
        compiler_params=PARAMS,
        name="delta_forward_outputs",
    )(start, pre, qe, oz, proj, gain)


def k3(heads, dg_ref, o_ref, proj_ref, gain_ref, qe_ref, m_ref, do_ref, dgate_ref, dc_ref, last_ref, dgain_ref, d_ref):
    c = pl.program_id(0)

    @pl.when(c == 0)
    def _():
        d_ref[...] = jnp.zeros_like(d_ref)
        dgain_ref[...] = jnp.zeros_like(dgain_ref)

    for h in range(heads):
        o = o_ref[:, h * DV:(h + 1) * DV]
        gate = proj_ref[:, h * HC + CW:(h + 1) * HC]
        dg = dg_ref[:, h * DV:(h + 1) * DV]
        gain = gain_ref[...]
        rstd = lax.rsqrt(jnp.mean(o * o, axis=-1, keepdims=True) + 1e-5)
        n = o * rstd
        sg = sigmoid(gate)
        act = gate * sg
        dgain_ref[...] += jnp.sum(dg * n * act, axis=0, keepdims=True)
        dgate_ref[:, h * DV:(h + 1) * DV] = (dg * n * gain * (sg * (1.0 + gate * (1.0 - sg)))).astype(BF)
        dn = dg * gain * act
        do = rstd * (dn - n * jnp.mean(dn * n, axis=-1, keepdims=True))
        do_ref[:, h * DV:(h + 1) * DV] = do.astype(BF)
        dc = mm(qe_ref[:, h * DK:(h + 1) * DK], do, TL)
        dc_ref[0, h] = dc
        d = mm(m_ref[0, h], d_ref[h], TL) + dc
        d_ref[h] = d
        last_ref[h] = d


def backward_states(dgated, o, proj, gain, qe, m, tokens, heads):
    n = tokens // CH
    return pl.pallas_call(
        functools.partial(k3, heads),
        grid=(n,),
        in_specs=[by_rows(heads * DV, n, True), by_rows(heads * DV, n, True), by_rows(heads * HC, n, True),
                  whole((1, DV)), by_rows(heads * DK, n, True), by_chunk((heads, DK, DK), n, True)],
        out_specs=[by_rows(heads * DV, n, True), by_rows(heads * DV, n, True), by_chunk((heads, DK, DV), n, True),
                   whole((heads, DK, DV)), whole((1, DV))],
        out_shape=[sds((tokens, heads * DV), BF), sds((tokens, heads * DV), BF), sds((n, heads, DK, DV)),
                   sds((heads, DK, DV)), sds((1, DV))],
        scratch_shapes=[pltpu.VMEM((heads, DK, DV), F32)],
        compiler_params=PARAMS,
        name="delta_backward_states",
    )(dgated, o, proj, gain, qe, m)


def normed_pull(raw, grad, scale):
    r = lax.rsqrt(jnp.sum(raw * raw, axis=-1, keepdims=True) + 1e-6)
    n = raw * r
    return (scale * r) * (grad - n * jnp.sum(grad * n, axis=-1, keepdims=True))


def k4(heads, end_ref, dc_ref, m_ref, s_ref, do_ref, uv_ref, w_ref, a_ref, tinv_ref, q_ref, k_ref, sum_ref, proj_ref,
       dgate_ref, halo_ref, taps_ref, gcol_ref, grow_ref, dproj_ref, dhalo_ref, dtaps_ref, ds_ref, rim_ref):
    c = pl.program_id(0)
    last = pl.num_programs(0) - 1
    rows, cols = masks()

    @pl.when(c == 0)
    def _():
        ds_ref[...] = end_ref[...]
        rim_ref[...] = jnp.zeros_like(rim_ref)
        dtaps_ref[...] = jnp.zeros_like(dtaps_ref)

    for h in range(heads):
        ds = ds_ref[h]
        s = s_ref[0, h]
        do = do_ref[:, h * DV:(h + 1) * DV]
        q = q_ref[:, h * DK:(h + 1) * DK]
        k = k_ref[:, h * DK:(h + 1) * DK]
        a = a_ref[0, h]
        gcol = gcol_ref[:, h:h + 1]
        beta = gcol_ref[:, heads + h:heads + h + 1]
        grow = grow_ref[0, h:h + 1, :]
        glast = grow[:, CH - 1:CH]
        ratio = jnp.exp(jnp.where(rows >= cols, gcol - grow, -1e30))
        eg = jnp.exp(gcol)
        el = jnp.exp(glast - gcol)
        u = uv_ref[:, h * DV:(h + 1) * DV] - mm(w_ref[:, h * DK:(h + 1) * DK], s)
        du = mm(a, do, TL) + el * mm(k, ds)
        da = ratio * mm(do, u, TT)
        drv = mm(tinv_ref[0, h], du, TL)
        drk = mm(drv, s, TT)
        dl = jnp.where(rows > cols, (-beta) * ratio * mm(drv, u, TT), 0.0)
        dq = eg * mm(do, s, TT) + mm(da, k)
        dk = el * mm(u, ds, TT) + mm(da, q, TL) - (beta * eg) * drk + mm(dl, k) + mm(dl, k, TL)
        dv = beta * drv
        ds_ref[h] = mm(m_ref[0, h], ds, TL) + dc_ref[0, h]
        summed = sum_ref[:, h * CW:(h + 1) * CW]
        sg = sigmoid(summed)
        act = summed * sg
        dact = jnp.concatenate(
            [normed_pull(act[:, :DK], dq, DK ** -0.5), normed_pull(act[:, DK:2 * DK], dk, 1.0), dv], 1)
        dsum = dact * (sg * (1.0 + summed * (1.0 - sg)))
        rim = rim_ref[:, h * CW:(h + 1) * CW]
        ext = jnp.concatenate([dsum, rim], 0)
        rim_ref[:, h * CW:(h + 1) * CW] = dsum[:8]
        conv_in = proj_ref[:, h * HC:h * HC + CW]
        dconv = jnp.zeros((CH, CW), F32)
        for j in range(KC):
            moved = ext[3 - j:3 - j + CH]
            dconv = dconv + taps_ref[j:j + 1, h * CW:(h + 1) * CW] * moved
            dtaps_ref[j:j + 1, h * CW:(h + 1) * CW] += jnp.sum(moved * conv_in, axis=0, keepdims=True)
        dproj_ref[:, h * HC:h * HC + CW] = dconv.astype(BF)
        dproj_ref[:, h * HC + CW:(h + 1) * HC] = dgate_ref[:, h * DV:(h + 1) * DV]

        @pl.when(c == last)
        def _():
            before = jnp.concatenate([jnp.zeros((8, CW), F32), dsum[:8]], 0)
            conv_halo = halo_ref[:, h * HC:h * HC + CW]
            dhalo = jnp.zeros((8, CW), F32)
            for j in range(KC):
                moved = before[3 - j:3 - j + 8]
                dhalo = dhalo + taps_ref[j:j + 1, h * CW:(h + 1) * CW] * moved
                dtaps_ref[j:j + 1, h * CW:(h + 1) * CW] += jnp.sum(moved * conv_halo, axis=0, keepdims=True)
            dhalo_ref[:, h * HC:h * HC + CW] = jnp.concatenate([jnp.zeros((8, CW), F32), dhalo], 0).astype(BF)
            dhalo_ref[:, h * HC + CW:(h + 1) * HC] = jnp.zeros((16, DV), BF)


def backward_inputs(end, dc, m, s, do, uv, w, a, tinv, q, k, summed, proj, dgate, taps, gcol, grow, tokens, heads):
    n = tokens // CH
    extra = proj.shape[0] // 8 - 1
    rows = functools.partial(by_rows, n=n, back=True)
    chunk = functools.partial(by_chunk, n=n, back=True)
    return pl.pallas_call(
        functools.partial(k4, heads),
        grid=(n,),
        in_specs=[whole((heads, DK, DV)), chunk((heads, DK, DV)), chunk((heads, DK, DK)), chunk((heads, DK, DV)),
                  rows(heads * DV), rows(heads * DV), rows(heads * DK), chunk((heads, CH, CH)), chunk((heads, CH, CH)),
                  rows(heads * DK), rows(heads * DK), rows(heads * CW), rows(heads * HC), rows(heads * DV),
                  pl.BlockSpec((8, heads * HC), lambda c: (extra, 0)), whole(taps.shape),
                  rows(gcol.shape[1]), chunk(grow.shape[1:])],
        out_specs=[rows(heads * HC), whole((16, heads * HC)), whole(taps.shape)],
        out_shape=[sds((tokens, heads * HC), BF), sds((16, heads * HC), BF), sds(taps.shape)],
        scratch_shapes=[pltpu.VMEM((heads, DK, DV), F32), pltpu.VMEM((8, heads * CW), F32)],
        compiler_params=PARAMS,
        name="delta_backward_inputs",
    )(end, dc, m, s, do, uv, w, a, tinv, q, k, summed, proj, dgate, proj, taps, gcol, grow)


def passed_along(x, by):
    count = lax.axis_size("seq")
    return lax.ppermute(x, "seq", [(i, i + by) for i in range(count) if 0 <= i + by < count])


def gather_seq(x, axis=0):
    return lax.all_gather(x, "seq", axis=axis, tiled=True)


def gather_head(x, axis=0):
    return lax.all_gather(x, "head", axis=axis, tiled=True)


def scatter_seq(x, axis=0):
    return lax.psum_scatter(x, "seq", scatter_dimension=axis, tiled=True).astype(F32)


def scatter_head(x, axis=0):
    return lax.psum_scatter(x, "head", scatter_dimension=axis, tiled=True).astype(F32)


def dot(a, b, dims=((1,), (0,)), out=F32):
    return lax.dot_general(a, b, (dims, ((), ())), preferred_element_type=out)


def norm_rows(entries, scale_row):
    return entries * lax.rsqrt(jnp.mean(entries * entries, axis=-1, keepdims=True) + 1e-06) * scale_row


def chain(first, offsets, maps, backward):
    count = lax.axis_size("seq")
    here = lax.axis_index("seq")
    state = jnp.zeros(offsets[0].shape, F32)
    found = state
    order = range(count - 1, 0, -1) if backward else range(count - 1)
    for i in order:
        dims = ((1,), (1,)) if backward else ((2,), (1,))
        moved = lax.dot_general(maps[i], state.astype(BF), (dims, ((0,), (0,))), preferred_element_type=F32)
        state = moved + offsets[i].astype(F32)
        found = jnp.where(here == (i - 1 if backward else i + 1), state, found)
    return found


def plain_update(weight, gradient, second_old, beta_two):
    second_new = beta_two * second_old + (1.0 - beta_two) * (gradient * gradient + 1e-30)
    update = gradient * lax.rsqrt(second_new)
    clipped = update / jnp.maximum(1.0, jnp.sqrt(jnp.mean(update * update, axis=-1, keepdims=True)))
    scale = 0.3 * jnp.maximum(0.001, jnp.sqrt(jnp.mean(weight * weight, axis=-1, keepdims=True)))
    return (second_new, weight - scale * clipped)


def finished(weight, update, weight_total, update_total, entry_count):
    scale = 0.3 * jnp.maximum(0.001, jnp.sqrt(weight_total / entry_count))
    return weight - update * (scale / jnp.maximum(1.0, jnp.sqrt(update_total / entry_count)))


def local(
    hidden_in,
    out_grad,
    decays,
    strength,
    mixer_in,
    mixer_in_rows,
    mixer_in_cols,
    mixer_out,
    mixer_out_rows,
    mixer_out_cols,
    feed_in,
    feed_in_rows,
    feed_in_cols,
    feed_out,
    feed_out_rows,
    feed_out_cols,
    conv_kernel,
    conv_second,
    norm_gains,
    gains_second,
    head_gain,
    head_gain_second,
):
    beta_two = 1.0 - STEP ** (-0.8)
    tokens, heads = decays.shape
    blocks = tokens // CH
    in_span, in_width = mixer_in.shape[0], heads * HC
    out_span = mixer_out.shape[2]
    feed_span, hidden_span = feed_in.shape[0], feed_in.shape[2]
    x = hidden_in.astype(F32)

    taps = gather_seq(conv_kernel.astype(BF), 2).astype(F32).reshape(KC, heads * CW)
    in_w = gather_seq(mixer_in.astype(BF).reshape(in_span, in_width))
    rows_all = gather_head(norm_rows(x, norm_gains[0]).astype(BF))
    out_w = gather_seq(mixer_out.astype(BF).reshape(heads * DV, out_span), 1)
    grad_rows = gather_seq(out_grad)
    expand = gather_head(feed_in.astype(BF).reshape(feed_span, 2 * hidden_span))
    shrink = gather_head(feed_out.astype(BF), 1)

    log_sum = jnp.cumsum(jnp.log(decays).reshape(blocks, CH, heads), axis=1)
    gcol = jnp.concatenate([log_sum.reshape(tokens, heads), strength, jnp.zeros((tokens, 8 - 2 * heads), F32)], 1)
    grow = jnp.concatenate([jnp.swapaxes(log_sum, 1, 2), jnp.zeros((blocks, 8 - heads, CH), F32)], 1)
    gain_row = head_gain[None]
    rows_more = jnp.concatenate([rows_all, passed_along(rows_all[tokens - 16 :], 1)], 0)
    proj = dot(rows_more, in_w)
    (summed, q, k, tinv, scores, w, uv, qe, oz, m, pre, last) = forward_parts(proj, taps, gcol, grow, tokens, heads)
    all_last = lax.all_gather(last.astype(BF), "seq", axis=0)
    maps, offsets = all_last[..., :DK], all_last[..., DK:]
    start = chain(0, offsets, maps, False)
    states, o, gated = forward_outputs(start, pre, qe, oz, proj, gain_row, tokens, heads)
    mixed = scatter_head(dot(gated, out_w, out=BF))
    residual = x + mixed

    normed_two, norm_two_pull = jax.vjp(norm_rows, residual, norm_gains[1])
    feed_rows = gather_seq(normed_two.astype(BF))
    gate_up = dot(feed_rows, expand)
    gate, up = gate_up[:, :hidden_span], gate_up[:, hidden_span:]
    sig = 1.0 / (1.0 + jnp.exp(-gate))
    silu = gate * sig
    hidden = (silu * up).astype(BF)
    d_hidden = dot(grad_rows, shrink, ((1,), (1,)))
    d_gate_up = jnp.concatenate(
        [d_hidden * up * (sig * (1.0 + gate * (1.0 - sig))), d_hidden * silu], 1
    ).astype(BF)
    d_normed_two = scatter_seq(dot(d_gate_up, expand, ((1,), (1,)), BF))
    d_residual_part, d_gain_two = norm_two_pull(d_normed_two)
    d_residual = out_grad.astype(F32) + d_residual_part
    d_rows = gather_head(d_residual.astype(BF))

    d_gated = dot(d_rows, out_w, ((1,), (1,)))
    do, d_gate, dc, d_last, d_head_gain = backward_states(d_gated, o, proj, gain_row, qe, m, tokens, heads)
    end = chain(0, lax.all_gather(d_last.astype(BF), "seq", axis=0), maps, True)
    d_proj, d_halo, d_taps = backward_inputs(
        end, dc, m, states, do, uv, w, scores, tinv, q, k, summed, proj, d_gate, taps, gcol, grow, tokens, heads
    )
    d_proj_more = jnp.concatenate([d_proj, d_halo], 0)
    in_grad = scatter_seq(dot(rows_more, d_proj_more, ((0,), (0,)), BF))
    d_rows_more = dot(d_proj_more, in_w, ((1,), (1,)), BF)
    rim = passed_along(d_rows_more[tokens:], -1)
    d_rows_in = jnp.concatenate([d_rows_more[: tokens - 16], d_rows_more[tokens - 16 : tokens] + rim], 0)
    d_normed = scatter_head(d_rows_in)
    feed_sum = scatter_seq(dot(hidden, shrink, out=BF))
    block_out = (residual + feed_sum).astype(BF)
    out_g = scatter_seq(dot(gated, d_rows, ((0,), (0,)), BF), 1)
    expand_g = scatter_head(dot(feed_rows, d_gate_up, ((0,), (0,)), BF))
    shrink_g = scatter_head(dot(hidden, grad_rows, ((0,), (0,)), BF), 1)
    kernel_grad = scatter_seq(d_taps.reshape(KC, heads, CW).astype(BF), 2)

    _, norm_one_pull = jax.vjp(norm_rows, x, norm_gains[0])
    d_residual_one, d_gain_one = norm_one_pull(d_normed)
    input_grad = d_residual + d_residual_one

    in_sq, out_sq, expand_sq, shrink_sq = in_grad * in_grad, out_g * out_g, expand_g * expand_g, shrink_g * shrink_g
    over_head = jnp.concatenate(
        [
            jnp.sum(in_sq, 1),
            jnp.sum(out_sq, 0),
            jnp.sum(expand_sq, 0),
            jnp.sum(shrink_sq, 1),
        ]
    )
    over_seq = jnp.concatenate(
        [
            jnp.sum(in_sq, 0),
            jnp.sum(out_sq, 1),
            jnp.sum(expand_sq, 1),
            jnp.sum(shrink_sq, 0),
        ]
    )
    over_head = lax.psum(over_head, "head")
    over_seq = lax.psum(over_seq, "seq")

    def cut(vector, sizes):
        at = 0
        pieces = []
        for size in sizes:
            pieces.append(vector[at : at + size])
            at += size
        return pieces

    in_rows_sq, out_cols_sq, expand_cols_sq, shrink_rows_sq = cut(
        over_head, (in_span, out_span, 2 * hidden_span, hidden_span)
    )
    in_cols_sq, out_rows_sq, expand_rows_sq, shrink_cols_sq = cut(
        over_seq, (in_width, heads * DV, feed_span, feed_span)
    )
    in_count = (D, HEAD_TOTAL * HC)
    out_count = (HEAD_TOTAL * DV, D)
    expand_count = (D, 2 * FF)
    shrink_count = (FF, D)

    def moment(old, squares, over):
        return beta_two * old.reshape(-1) + (1.0 - beta_two) * (squares / over + 1e-30)

    in_rows_new = moment(mixer_in_rows, in_rows_sq, in_count[1])
    in_cols_new = moment(mixer_in_cols, in_cols_sq, in_count[0])
    out_rows_new = moment(mixer_out_rows, out_rows_sq, out_count[1])
    out_cols_new = moment(mixer_out_cols, out_cols_sq, out_count[0])
    expand_rows_new = moment(feed_in_rows, expand_rows_sq, expand_count[1])
    expand_cols_new = moment(feed_in_cols, expand_cols_sq, expand_count[0])
    shrink_rows_new = moment(feed_out_rows, shrink_rows_sq, shrink_count[1])
    shrink_cols_new = moment(feed_out_cols, shrink_cols_sq, shrink_count[0])
    in_upd = in_grad * (lax.rsqrt(in_rows_new)[:, None] * lax.rsqrt(in_cols_new)[None])
    out_upd = out_g * (lax.rsqrt(out_rows_new)[:, None] * lax.rsqrt(out_cols_new)[None])
    expand_upd = expand_g * (lax.rsqrt(expand_rows_new)[:, None] * lax.rsqrt(expand_cols_new)[None])
    shrink_upd = shrink_g * (lax.rsqrt(shrink_rows_new)[:, None] * lax.rsqrt(shrink_cols_new)[None])
    conv_second_new = beta_two * conv_second + (1.0 - beta_two) * (kernel_grad * kernel_grad + 1e-30)
    conv_update = kernel_grad * lax.rsqrt(conv_second_new)
    seq_count, head_count = lax.axis_size("seq"), lax.axis_size("head")
    scalars = jnp.stack(
        [
            jnp.sum(in_upd * in_upd),
            jnp.sum(out_upd * out_upd),
            jnp.sum(expand_upd * expand_upd),
            jnp.sum(shrink_upd * shrink_upd),
            jnp.sum(conv_update * conv_update),
            jnp.sum(mixer_in * mixer_in),
            jnp.sum(mixer_out * mixer_out),
            jnp.sum(feed_in * feed_in),
            jnp.sum(feed_out * feed_out),
            jnp.sum(conv_kernel * conv_kernel),
            jnp.sum(in_rows_new) / head_count,
            jnp.sum(out_rows_new) / seq_count,
            jnp.sum(expand_rows_new) / seq_count,
            jnp.sum(shrink_rows_new) / head_count,
        ]
    )
    late = jnp.concatenate([d_gain_one, d_gain_two, d_head_gain[0], scalars])
    late = lax.psum(lax.psum(late, "head"), "seq")
    gains_grad = late[: 2 * D].reshape(2, D)
    head_gain_grad = late[2 * D : 2 * D + DV]
    totals = late[2 * D + DV :]

    def stepped(weight, update, count, slot, shape):
        mean = totals[10 + slot] / count[0]
        entries = count[0] * count[1]
        scale = 0.3 * jnp.maximum(0.001, jnp.sqrt(totals[5 + slot] / entries))
        scale = scale * jnp.sqrt(mean) / jnp.maximum(1.0, jnp.sqrt(totals[slot] * mean / entries))
        return weight - scale * update.reshape(shape)

    in_new = stepped(mixer_in, in_upd, in_count, 0, mixer_in.shape)
    out_new = stepped(mixer_out, out_upd, out_count, 1, mixer_out.shape)
    expand_new = stepped(feed_in, expand_upd, expand_count, 2, feed_in.shape)
    shrink_new = stepped(feed_out, shrink_upd, shrink_count, 3, feed_out.shape)
    conv_new = finished(conv_kernel, conv_update, totals[9], totals[4], KC * HEAD_TOTAL * CW)
    gains_second_new, gains_new = plain_update(norm_gains, gains_grad, gains_second, beta_two)
    head_second_new, head_new = plain_update(
        head_gain[None], head_gain_grad[None], head_gain_second[None], beta_two
    )
    return (
        block_out,
        input_grad,
        in_grad.reshape(mixer_in.shape),
        in_rows_new,
        in_cols_new.reshape(mixer_in_cols.shape),
        in_new,
        out_g.reshape(mixer_out.shape),
        out_rows_new.reshape(mixer_out_rows.shape),
        out_cols_new,
        out_new,
        expand_g.reshape(feed_in.shape),
        expand_rows_new,
        expand_cols_new.reshape(feed_in_cols.shape),
        expand_new,
        shrink_g,
        shrink_rows_new,
        shrink_cols_new,
        shrink_new,
        kernel_grad,
        conv_second_new,
        conv_new,
        gains_grad,
        gains_second_new,
        gains_new,
        head_gain_grad,
        head_second_new[0],
        head_new[0],
    )


def solution(mesh):
    return jax.shard_map(
        local,
        mesh=mesh,
        in_specs=(
            P(("seq", "head"), None),
            P(("seq", "head"), None),
            P("seq", "head"),
            P("seq", "head"),
            P("seq", "head", None),
            P("seq"),
            P("head", None),
            P("head", None, "seq"),
            P("head", None),
            P("seq"),
            P("head", None, "seq"),
            P("head"),
            P(None, "seq"),
            P("seq", "head"),
            P("seq"),
            P("head"),
            P(None, "head", "seq"),
            P(None, "head", "seq"),
            P(),
            P(),
            P(),
            P(),
        ),
        out_specs=(
            P(("seq", "head"), None),
            P(("seq", "head"), None),
            P("seq", "head", None),
            P("seq"),
            P("head", None),
            P("seq", "head", None),
            P("head", None, "seq"),
            P("head", None),
            P("seq"),
            P("head", None, "seq"),
            P("head", None, "seq"),
            P("head"),
            P(None, "seq"),
            P("head", None, "seq"),
            P("seq", "head"),
            P("seq"),
            P("head"),
            P("seq", "head"),
            P(None, "head", "seq"),
            P(None, "head", "seq"),
            P(None, "head", "seq"),
            P(),
            P(),
            P(),
            P(),
            P(),
            P(),
        ),
        check_vma=False,
    )
```

time: 2170 us -> 1260 us (0.58)
  matrix products: 691 us -> 114 us
  waiting for transfers between devices: 892 us -> 702 us
  other arithmetic: 274 us -> 123 us
  local copies, waits for them, and re-layouts: 172 us -> 58.3 us
  Pallas kernels: 0 us -> 84.4 us
  blocking collectives: 54.7 us -> 132 us
  starting transfers between devices: 27.8 us -> 4.38 us
    dot_general x378 -> x18, matrix products: 678 us -> 114 us  [the longest x12 111 us: dot(): return lax.dot_general(a, b, (dims, ((), ())), preferred_element_type=out)]
    another operation x6 -> x1, other arithmetic: 160 us -> 23.3 us  [local(): log_sum = jnp.cumsum(jnp.log(decays).reshape(blocks, CH, heads), axis=1)]
    psum x1 -> x0, waiting for transfers between devices: 129 us -> none  [local(): lax.psum((jnp.stack([d_gain_one, d_gain_two]), d_head_gain, placed(jnp.su...]
    pallas_call x0 -> x4, Pallas kernels: none -> 84.4 us  [the longest x1 46.5 us: forward_parts(): pl.pallas_call(functools.partial(k1, heads), grid=(n,), in_specs=[by_rows...]
    psum x1 -> x4, blocking collectives: 41.9 us -> 85.3 us  [the longest x2 40.6 us: local(): late = lax.psum(lax.psum(late, 'head'), 'seq')]
    all_gather x8, waiting for transfers between devices: 349 us -> 313 us  [the longest x4 170 us: gather_seq(): return lax.all_gather(x, 'seq', axis=axis, tiled=True)]
    all_gather x1 -> x3, blocking collectives: 12.8 us -> 47 us  [the longest x1 17.9 us: local(): all_last = lax.all_gather(last.astype(BF), 'seq', axis=0)]
    dynamic_update_slice x40 -> x0, local copies, waits for them, and re-layouts: 33 us -> none  [the longest x32 31.2 us: run_blocks(): last_state, outputs = lax.scan(advance, start_state, by_block)]
  transfers between devices with their start and end apart: 26 -> 19, of which waited for: 19 -> 13; matrix products, arithmetic and copies ran while one was open for 26% -> 14% of each run, Pallas kernels for 0% -> 7%
where the time goes in v1:
time: 1260 us; the launch traced here: 1250 us
  waiting for transfers between devices  702 us (56%)
  blocking collectives  132 us (10%)
  other arithmetic  123 us (10%)
  matrix products  114 us (9%)
  Pallas kernels  84.4 us (7%)
  local copies, waits for them, and re-layouts  58.3 us (5%)
  between operations  28.8 us (2%)
    reduce_scatter x4, waiting for transfers between devices, scatter_seq(): lax.psum_scatter(x, 'seq', scatter_dimension=axis, tiled=True).astype(F32)  196 us
    reduce_scatter x4, waiting for transfers between devices, scatter_head(): lax.psum_scatter(x, 'head', scatter_dimension=axis, tiled=True).astype(F32)  185 us
    all_gather x4, waiting for transfers between devices, gather_seq(): return lax.all_gather(x, 'seq', axis=axis, tiled=True)  170 us
    all_gather x4, waiting for transfers between devices, gather_head(): return lax.all_gather(x, 'head', axis=axis, tiled=True)  143 us
    dot_general x12, matrix products, dot(): return lax.dot_general(a, b, (dims, ((), ())), preferred_element_type=out)  111 us
    pallas_call x1, Pallas kernels, forward_parts(): pl.pallas_call(functools.partial(k1, heads), grid=(n,), in_specs=[by_rows...  46.5 us
    psum x2, blocking collectives, local(): late = lax.psum(lax.psum(late, 'head'), 'seq')  40.6 us
    psum x1, blocking collectives, local(): over_head = lax.psum(over_head, 'head')  25.3 us
  transfers between devices with their start and end apart: 19, of which 13 were waited for; matrix products, arithmetic and copies ran while one was open for 14% of the time, Pallas kernels for 7%

profile of v1, /device:TPU:0, one launch (start us, length us, event | category | flops | bytes accessed | tf_op | source)
XLA Modules:
  0.0 1247.4 jit_solution(14137280986434946465)
XLA Ops:
  22.1 23.3 %fusion.69 = f32[8,128,2]{2,0,1:T(8,128)S(1)} fusion(f32[8,128,2]{2,0,1:T(8,128)S(1)} %copy.63), kind=kOutput, calls=%fused_computation.166 | output fusion | flops 260096 | bytes 16384 | tf_op jit(solution)/shard_map/jit(cumsum)/reduce_window_sum | solution.py:422
  46.5 12.7 %all_gather.41 = bf16[4,2,512]{2,1,0:T(2,128)(2,1)S(1)} all-gather(bf16[4,2,128]{2,1,0:T(2,128)(2,1)S(1)} %get-tuple-element.146), channel_id=1, replica_groups=mesh['seq'=4,'head'=8] {'seq'}, dimensions={2}, use_global_device_ids=true | all-gather | bytes 10240 | tf_op jit(solution)/shard_map/all_gather | solution.py:332
  67.5 101.5 %all-gather.13.cloned.1.call-done = bf16[2048,1536]{1,0:T(8,128)(2,1)} async-done(((bf16[512,1536]{1,0:T(8,128)(2,1)}), bf16[2048,1536]{1,0:T(8,128)(2,1)}) %all-gather.13.cloned.1.call-update) | async-done | bytes 6291472 | tf_op jit(solution)/shard_map/all_gather | solution.py:332
  169.0 12.0 fusion.70.proj_ref.halo_ref
  181.0 46.5 %delta_forward_parts.1 = (f32[1024,1024]{1,0:T(8,128)}, bf16[1024,256]{1,0:T(8,128)(2,1)S(1)}, bf16[1024,256]{1,0:T(8,128)(2,1)S(1)}, bf16[8,2,128,128]{3,2,1,0:...) custom-call(f32[1040,1536]{1,0:T(8,128)} %fusion.70.proj_ref.halo_re, ...), custom_call_target="tpu_custom_call" | custom-call | tf_op jit(solution)/shard_map/delta_forward_parts/pallas_call | solution.py:140
  227.6 17.9 %all-gather = bf16[8,128,384]{2,1,0:T(8,128)(2,1)S(1)} all-gather(bf16[2,128,384]{2,1,0:T(8,128)(2,1)S(1)} %convert_element_type.129), channel_id=2, replica_groups=mesh['seq'=4,'head'=8] {'seq'}, dimensions={0}, use_global_device_ids=true | all-gather | bytes 983040 | tf_op jit(solution)/shard_map/all_gather | solution.py:429
  246.4 8.0 delta_forward_outputs.1
  263.0 51.1 %reduce-scatter.12.cloned.1.call-done = bf16[128,2048]{1,0:T(8,128)(2,1)} async-done(((bf16[1024,2048]{1,0:T(8,128)(2,1)}), bf16[128,2048]{1,0:T(8,128)(2,1)}) %reduce-scatter.12.cloned.1.call-update) | async-done | bytes 524304 | tf_op jit(solution)/shard_map/reduce_scatter | solution.py:344
  330.1 33.7 %all-gather.17.cloned.1.call-done = bf16[512,2048]{1,0:T(8,128)(2,1)} async-done(((bf16[128,2048]{1,0:T(8,128)(2,1)}), bf16[512,2048]{1,0:T(8,128)(2,1)}) %all-gather.17.cloned.1.call-update) | async-done | bytes 2097168 | tf_op jit(solution)/shard_map/all_gather | solution.py:332
  363.8 68.9 %all-gather.19.cloned.1.call-done = bf16[2048,2816]{1,0:T(8,128)(2,1)} async-done(((bf16[256,2816]{1,0:T(8,128)(2,1)}), bf16[2048,2816]{1,0:T(8,128)(2,1)}) %all-gather.19.cloned.1.call-update) | async-done | bytes 11534352 | tf_op jit(solution)/shard_map/all_gather | solution.py:336
  432.7 12.6 %fusion.72 = f32[512,2816]{1,0:T(8,128)} fusion(bf16[512,2048]{1,0:T(8,128)(2,1)} %all-gather.17.cloned.1.call-done, bf16[2048,2816]{1,0:T(8,128)(2,1)} %all-gather.19.cloned.1.call-done), kind=kOutput, calls=%fused_computation.169 | convolution fusion | flops 5905580032 | bytes 19398656 | tf_op jit(solution)/shard_map/dot_general | solution.py:348
  445.3 35.0 %all-gather.23.cloned.1.call-done = bf16[512,2048]{1,0:T(8,128)(2,1)} async-done(((bf16[128,2048]{1,0:T(8,128)(2,1)}), bf16[512,2048]{1,0:T(8,128)(2,1)}) %all-gather.23.cloned.1.call-update) | async-done | bytes 2097168 | tf_op jit(solution)/shard_map/all_gather | solution.py:332
  480.4 45.7 %all-gather.21.cloned.1.call-done = bf16[1408,2048]{1,0:T(8,128)(2,1)} async-done(((bf16[1408,256]{1,0:T(8,128)(2,1)}), bf16[1408,2048]{1,0:T(8,128)(2,1)}) %all-gather.21.cloned.1.call-update) | async-done | bytes 5767184 | tf_op jit(solution)/shard_map/all_gather | solution.py:336
  526.1 10.5 multiply_convert_fusion.1
  545.5 44.0 %reduce-scatter.16.cloned.1.call-done = bf16[128,2048]{1,0:T(8,128)(2,1)} async-done(((bf16[512,2048]{1,0:T(8,128)(2,1)}), bf16[128,2048]{1,0:T(8,128)(2,1)}) %reduce-scatter.16.cloned.1.call-update) | async-done | bytes 524304 | tf_op jit(solution)/shard_map/reduce_scatter | solution.py:340
  595.0 7.8 fusion.78
  602.9 28.1 %all-gather.25.cloned.1.call-done = bf16[1024,2048]{1,0:T(8,128)(2,1)} async-done(((bf16[128,2048]{1,0:T(8,128)(2,1)}), bf16[1024,2048]{1,0:T(8,128)(2,1)}) %all-gather.25.cloned.1.call-update) | async-done | bytes 4194320 | tf_op jit(solution)/shard_map/all_gather | solution.py:336
  637.5 8.5 delta_backward_states.1
  648.3 16.5 %all-gather.1 = bf16[8,128,256]{2,1,0:T(8,128)(2,1)S(1)} all-gather(bf16[2,128,256]{2,1,0:T(8,128)(2,1)S(1)} %convert_element_type.149), channel_id=3, replica_groups=mesh['seq'=4,'head'=8] {'seq'}, dimensions={0}, use_global_device_ids=true | all-gather | bytes 655360 | tf_op jit(solution)/shard_map/all_gather | solution.py:454
  668.1 21.4 %delta_backward_inputs.1 = (bf16[1024,1536]{1,0:T(8,128)(2,1)}, bf16[16,1536]{1,0:T(8,128)(2,1)S(1)}, f32[4,1024]{1,0:T(4,128)S(1)}) custom-call(f32[2,128,256]{2,1,0:T(8,128)S(1)} %fusion.9.end_ref, f32[8,2,128,256]{3,2,1,0:T(8,128)} %copy-done.1, bf16[8,2,128,128]{3,2,1,0:T(8,128)(2,1)S(1)} %get-tuple-element.56.m_ref, ...), custom_call_target="tpu_custom_call" | custom-call | tf_op jit(solution)/shard_map/delta_backward_inputs/pallas_call | solution.py:310
  697.8 10.8 fusion.3
  710.8 10.1 fusion.75
  732.4 8.0 fusion.73
  740.6 12.4 fusion.76
  766.7 84.1 %reduce-scatter.24.cloned.1.call-done = bf16[256,2816]{1,0:T(8,128)(2,1)} async-done(((bf16[2048,2816]{1,0:T(8,128)(2,1)}), bf16[256,2816]{1,0:T(8,128)(2,1)}) %reduce-scatter.24.cloned.1.call-update) | async-done | bytes 1441808 | tf_op jit(solution)/shard_map/reduce_scatter | solution.py:344
  856.3 49.4 %reduce-scatter.18.cloned.1.call-done = bf16[128,2048]{1,0:T(8,128)(2,1)} async-done(((bf16[1024,2048]{1,0:T(8,128)(2,1)}), bf16[128,2048]{1,0:T(8,128)(2,1)}) %reduce-scatter.18.cloned.1.call-update) | async-done | bytes 524304 | tf_op jit(solution)/shard_map/reduce_scatter | solution.py:344
  909.1 43.2 %reduce-scatter.14.cloned.1.call-done = bf16[128,2048]{1,0:T(8,128)(2,1)} async-done(((bf16[512,2048]{1,0:T(8,128)(2,1)}), bf16[128,2048]{1,0:T(8,128)(2,1)}) %reduce-scatter.14.cloned.1.call-update) | async-done | bytes 524304 | tf_op jit(solution)/shard_map/reduce_scatter | solution.py:340
  955.6 109.1 %reduce-scatter.20.cloned.1.call-done = bf16[512,1536]{1,0:T(8,128)(2,1)} async-done(((bf16[2048,1536]{1,0:T(8,128)(2,1)}), bf16[512,1536]{1,0:T(8,128)(2,1)}) %reduce-scatter.20.cloned.1.call-update) | async-done | bytes 1572880 | tf_op jit(solution)/shard_map/reduce_scatter | solution.py:340
  1068.0 25.3 %psum.28 = f32[5248]{0:T(1024)} all-reduce(f32[5248]{0:T(1024)} %pad_maximum_fusion.4), channel_id=1, replica_groups=mesh['seq'=4,'head'=8] {'head'}, use_global_device_ids=true, to_apply=%region_17.18 | all-reduce | flops 5248 | bytes 41984 | tf_op jit(solution)/shard_map/psum | solution.py:492
  1094.7 19.4 %psum.29 = f32[2560]{0:T(1024)} all-reduce(f32[2560]{0:T(1024)} %pad_maximum_fusion.5), channel_id=1, replica_groups=mesh['seq'=4,'head'=8] {'seq'}, use_global_device_ids=true, to_apply=%region_22.23 | all-reduce | flops 2560 | bytes 20480 | tf_op jit(solution)/shard_map/psum | solution.py:493
  1146.6 23.5 %psum.30 = f32[4366]{0:T(1024)} all-reduce(f32[4366]{0:T(1024)} %concatenate.36), channel_id=1, replica_groups=mesh['seq'=4,'head'=8] {'head'}, use_global_device_ids=true, to_apply=%region_40.41 | all-reduce | flops 4366 | bytes 34928 | tf_op jit(solution)/shard_map/psum | solution.py:551
  1170.1 17.1 %psum.31 = f32[4366]{0:T(1024)} all-reduce(f32[4366]{0:T(1024)} %psum.30), channel_id=1, replica_groups=mesh['seq'=4,'head'=8] {'seq'}, use_global_device_ids=true, to_apply=%region_41.42 | all-reduce | flops 4366 | bytes 34928 | tf_op jit(solution)/shard_map/psum | solution.py:551
  (295 shorter events, 200.7 us)
Async XLA Ops:
  7.2 52.4 %all-gather.11.cloned.1.call-start = ((), (), s32[]{:S(2)}) async-start(), calls=%async_computation.9 | async-start | bytes 4718592 | tf_op jit(solution)/shard_map/all_gather | solution.py:336
  11.9 157.1 %all-gather.13.cloned.1.call-start = ((), (), s32[]{:S(2)}) async-start(), calls=%async_computation.10 | async-start | bytes 7864320 | tf_op jit(solution)/shard_map/all_gather | solution.py:332
  20.1 25.8 %copy-start.42 = (f32[4,2,128]{2,1,0:T(2,128)S(1)}, f32[4,2,128]{2,1,0:T(2,128)}, u32[]{:S(2)}) copy-start(f32[4,2,128]{2,1,0:T(2,128)} %param.38) | copy-start | bytes 12292
  20.1 39.2 %copy-start.50 = (f32[1024,2]{0,1:T(2,128)S(1)}, f32[1024,2]{0,1:T(2,128)}, u32[]{:S(2)}) copy-start(f32[1024,2]{0,1:T(2,128)} %param.25) | copy-start | bytes 24580
  20.1 236.6 %all-gather.15.cloned.1.call-start = ((), (), s32[]{:S(2)}) async-start(), calls=%async_computation.11 | async-start | bytes 2621440 | tf_op jit(solution)/shard_map/all_gather | solution.py:332
  21.8 292.2 %reduce-scatter.12.cloned.1.call-start = ((), (), s32[]{:S(2)}) async-start(), calls=%async_computation.12 | async-start | bytes 4718592 | tf_op jit(solution)/shard_map/reduce_scatter | solution.py:344
  60.5 6.3 collective-permute-start
  262.9 100.9 %all-gather.17.cloned.1.call-start = ((), (), s32[]{:S(2)}) async-start(), calls=%async_computation.13 | async-start | bytes 2621440 | tf_op jit(solution)/shard_map/all_gather | solution.py:332
  315.5 276.4 %copy-start.49 = (f32[128]{0:T(128)}, f32[128]{0:T(128)S(1)}, u32[]{:S(2)}) copy-start(f32[128]{0:T(128)S(1)} %fusion.48) | copy-start | bytes 1540
  317.7 115.0 %all-gather.19.cloned.1.call-start = ((), (), s32[]{:S(2)}) async-start(), calls=%async_computation.14 | async-start | bytes 12976128 | tf_op jit(solution)/shard_map/all_gather | solution.py:336
  325.3 155.0 %all-gather.23.cloned.1.call-start = ((), (), s32[]{:S(2)}) async-start(), calls=%async_computation.17 | async-start | bytes 2621440 | tf_op jit(solution)/shard_map/all_gather | solution.py:332
  326.1 200.0 %all-gather.21.cloned.1.call-start = ((), (), s32[]{:S(2)}) async-start(), calls=%async_computation.15 | async-start | bytes 6488064 | tf_op jit(solution)/shard_map/all_gather | solution.py:336
  329.8 259.7 %reduce-scatter.16.cloned.1.call-start = ((), (), s32[]{:S(2)}) async-start(), calls=%async_computation.18 | async-start | bytes 2621440 | tf_op jit(solution)/shard_map/reduce_scatter | solution.py:340
  545.5 85.5 %all-gather.25.cloned.1.call-start = ((), (), s32[]{:S(2)}) async-start(), calls=%async_computation.19 | async-start | bytes 4718592 | tf_op jit(solution)/shard_map/all_gather | solution.py:336
  594.7 162.8 %reduce-scatter.26.cloned.1.call-start = ((), (), s32[]{:S(2)}) async-start(), calls=%async_computation.24 | async-start | bytes 6488064 | tf_op jit(solution)/shard_map/reduce_scatter | solution.py:344
  602.8 157.7 %reduce-scatter.28.cloned.1.call-start = ((), (), s32[]{:S(2)}) async-start(), calls=%async_computation.25 | async-start | bytes 163840
  648.3 19.7 %copy-start.4 = (bf16[1024,256]{1,0:T(8,128)(2,1)S(1)}, bf16[1024,256]{1,0:T(8,128)(2,1)}, u32[]{:S(2)}) copy-start(bf16[1024,256]{1,0:T(8,128)(2,1)} %copy-done.3) | copy-start | bytes 1572868
  648.3 19.8 %copy-start.6 = (bf16[8,2,128,128]{3,2,1,0:T(8,128)(2,1)S(1)}, bf16[8,2,128,128]{3,2,1,0:T(8,128)(2,1)}, u32[]{:S(2)}) copy-start(bf16[8,2,128,128]{3,2,1,0:T(8,128)(2,1)} %copy-done.5) | copy-start | bytes 1572868
  648.3 19.8 %copy-start.8 = (bf16[8,2,128,128]{3,2,1,0:T(8,128)(2,1)S(1)}, bf16[8,2,128,128]{3,2,1,0:T(8,128)(2,1)}, u32[]{:S(2)}) copy-start(bf16[8,2,128,128]{3,2,1,0:T(8,128)(2,1)} %copy-done.7) | copy-start | bytes 1572868
  648.3 19.8 %copy-start.10 = (bf16[1024,256]{1,0:T(8,128)(2,1)S(1)}, bf16[1024,256]{1,0:T(8,128)(2,1)}, u32[]{:S(2)}) copy-start(bf16[1024,256]{1,0:T(8,128)(2,1)} %copy-done.9) | copy-start | bytes 1572868
  690.8 71.9 %reduce-scatter.22.cloned.1.call-start = ((), (), s32[]{:S(2)}) async-start(), calls=%async_computation.22 | async-start | bytes 2621440 | tf_op jit(solution)/shard_map/reduce_scatter | solution.py:340
  697.3 153.5 %reduce-scatter.24.cloned.1.call-start = ((), (), s32[]{:S(2)}) async-start(), calls=%async_computation.23 | async-start | bytes 12976128 | tf_op jit(solution)/shard_map/reduce_scatter | solution.py:344
  708.7 197.0 %reduce-scatter.18.cloned.1.call-start = ((), (), s32[]{:S(2)}) async-start(), calls=%async_computation.20 | async-start | bytes 4718592 | tf_op jit(solution)/shard_map/reduce_scatter | solution.py:344
  721.0 9.1 collective-permute-start.1
  732.4 219.9 %reduce-scatter.14.cloned.1.call-start = ((), (), s32[]{:S(2)}) async-start(), calls=%async_computation.16 | async-start | bytes 2621440 | tf_op jit(solution)/shard_map/reduce_scatter | solution.py:340
  740.4 324.2 %reduce-scatter.20.cloned.1.call-start = ((), (), s32[]{:S(2)}) async-start(), calls=%async_computation.21 | async-start | bytes 7864320 | tf_op jit(solution)/shard_map/reduce_scatter | solution.py:340
  766.7 139.0 %copy-start.13 = (bf16[128,2048]{1,0:T(8,128)(2,1)S(1)}, bf16[128,2048]{1,0:T(8,128)(2,1)}, u32[]{:S(2)}) copy-start(bf16[128,2048]{1,0:T(8,128)(2,1)} %param.22) | copy-start | bytes 1572868
  766.7 185.6 %copy-start.16 = (bf16[128,2048]{1,0:T(8,128)(2,1)S(1)}, bf16[128,2048]{1,0:T(8,128)(2,1)}, u32[]{:S(2)}) copy-start(bf16[128,2048]{1,0:T(8,128)(2,1)} %reduce-scatter.12.cloned.1.call-done) | copy-start | bytes 1572868
  766.7 185.6 %copy-start.20 = (bf16[128,2048]{1,0:T(8,128)(2,1)S(1)}, bf16[128,2048]{1,0:T(8,128)(2,1)}, u32[]{:S(2)}) copy-start(bf16[128,2048]{1,0:T(8,128)(2,1)} %param.23) | copy-start | bytes 1572868
  766.7 185.6 %copy-start.21 = (bf16[128,2048]{1,0:T(8,128)(2,1)S(1)}, bf16[128,2048]{1,0:T(8,128)(2,1)}, u32[]{:S(2)}) copy-start(bf16[128,2048]{1,0:T(8,128)(2,1)} %reduce-scatter.16.cloned.1.call-done) | copy-start | bytes 1572868
  955.6 180.8 %copy-start.18 = (bf16[512,512]{1,0:T(8,128)(2,1)S(1)}, bf16[512,512]{1,0:T(8,128)(2,1)}, u32[]{:S(2)}) copy-start(bf16[512,512]{1,0:T(8,128)(2,1)} %reduce-scatter.22.cloned.1.call-done) | copy-start | bytes 1572868
  1064.7 69.3 %copy-start.14 = (bf16[512,1536]{1,0:T(8,128)(2,1)S(1)}, bf16[512,1536]{1,0:T(8,128)(2,1)}, u32[]{:S(2)}) copy-start(bf16[512,1536]{1,0:T(8,128)(2,1)} %reduce-scatter.20.cloned.1.call-done) | copy-start | bytes 4718596
  (55 other events, 351.4 us)
Sparse Core Ops, SparseCore 0:
  12.0 39.4 all-gather.10
  53.6 115.3 all-gather.12
  171.1 44.3 all-gather.14
  263.0 50.9 reduce-scatter.11
  317.9 45.9 all-gather.16
  366.3 66.3 all-gather.18
  434.4 45.9 all-gather.22
  483.0 43.0 all-gather.20
  545.6 43.8 reduce-scatter.15
  594.8 36.0 all-gather.24
  634.4 59.0 reduce-scatter.25
  696.2 19.1 reduce-scatter.27
  718.3 42.7 reduce-scatter.21
  764.9 85.8 reduce-scatter.23
  854.3 51.3 reduce-scatter.17
  908.4 43.8 reduce-scatter.13
  954.6 110.0 reduce-scatter.19

commit v2 on v1

v2 whole, which is shorter than its diff:
```python
import functools
import jax
import jax.numpy as jnp
import numpy as np
from jax import lax
from jax.experimental import pallas as pl
from jax.experimental.pallas import tpu as pltpu
from jax.sharding import PartitionSpec as P

D = 2048
HEAD_TOTAL = 16
DK = 128
DV = 256
FF = 5632
KC = 4
STEP = 10
CH = 128
RIM = 16
HC = 2 * DK + 2 * DV
CW = 2 * DK + DV
F32 = jnp.float32
BF = jnp.bfloat16
TT = ((1,), (1,))
TL = ((0,), (0,))


def mm(a, b, dims=((1,), (0,))):
    return lax.dot_general(a.astype(BF), b.astype(BF), (dims, ((), ())), preferred_element_type=F32)


def mm3(a, b, dims=((1,), (0,))):
    ah, bh = a.astype(BF), b.astype(BF)
    al, bl = (a - ah.astype(F32)).astype(BF), (b - bh.astype(F32)).astype(BF)
    one = functools.partial(lax.dot_general, dimension_numbers=(dims, ((), ())), preferred_element_type=F32)
    return one(ah, bh) + (one(ah, bl) + one(al, bh))


def sigmoid(v):
    return 1.0 / (1.0 + jnp.exp(-v))


def square_index():
    rows = lax.broadcasted_iota(jnp.int32, (CH, CH), 0)
    cols = lax.broadcasted_iota(jnp.int32, (CH, CH), 1)
    return rows, cols


def invert(strict, rows, cols):
    apart = rows ^ cols
    xs = [jnp.where(rows == cols, 1.0, 0.0) - jnp.where(apart == 1, s, 0.0) for s in strict]
    size = 2
    while size < CH:
        here = (apart >= size) & (apart < 2 * size)
        left = [mm3(x, jnp.where(here, s, 0.0)) for x, s in zip(xs, strict)]
        xs = [x - mm3(y, x) for x, y in zip(xs, left)]
        size *= 2
    return xs


PER = 2


def parts_kernel(heads, p_ref, halo_ref, first_ref, taps_ref, gcol_ref, grow_ref,
                 sum_ref, q_ref, k_ref, tinv_ref, a_ref, w_ref, uv_ref, qe_ref, oz_ref, m_ref, pre_ref, last_ref, x_ref):
    rows, cols = square_index()
    eye = jnp.where(rows == cols, 1.0, 0.0)
    width = heads * DV

    @pl.when(pl.program_id(0) == 0)
    def _():
        for h in range(heads):
            x_ref[h] = jnp.concatenate([eye, jnp.zeros((DK, DV), F32)], 1)

    def convolved(at, size):
        before = jnp.where(pl.program_id(0) == 0, first_ref[RIM - 8:, at:at + size], halo_ref[:, at:at + size])
        ext = jnp.concatenate([before, p_ref[:, at:at + size]], 0)
        summed = taps_ref[0:1, at:at + size] * ext[5:5 + PER * CH]
        for j in range(1, KC):
            summed = summed + taps_ref[j:j + 1, at:at + size] * ext[5 + j:5 + j + PER * CH]
        sum_ref[:, at:at + size] = summed
        return summed * sigmoid(summed)

    stricts, held = [], []
    for h in range(heads):
        act = convolved(2 * h * DK, 2 * DK)
        values = convolved(width + h * DV, DV)
        for c in range(PER):
            at = slice(c * CH, (c + 1) * CH)
            q, k = act[at, :DK], act[at, DK:]
            q = q * (lax.rsqrt(jnp.sum(q * q, axis=-1, keepdims=True) + 1e-6) * DK ** -0.5)
            k = k * lax.rsqrt(jnp.sum(k * k, axis=-1, keepdims=True) + 1e-6)
            gcol, beta = gcol_ref[at, h:h + 1], gcol_ref[at, heads + h:heads + h + 1]
            grow = grow_ref[c, h:h + 1, :]
            ratio = jnp.exp(jnp.where(rows >= cols, gcol - grow, -1e30))
            stricts.append(jnp.where(rows > cols, beta * ratio * mm3(k, k, TT), 0.0))
            held.append((h, c, q, k, values[at], ratio, gcol, beta, grow[:, CH - 1:CH]))
    for (h, c, q, k, v, ratio, gcol, beta, glast), tinv in zip(held, invert(stricts, rows, cols)):
        at, key, val = slice(c * CH, (c + 1) * CH), slice(h * DK, (h + 1) * DK), slice(h * DV, (h + 1) * DV)
        eg = jnp.exp(gcol)
        kd = k * jnp.exp(glast - gcol)
        a = ratio * mm(q, k, TT)
        w = mm3(tinv, (beta * eg) * k)
        uv = mm3(tinv, beta * v)
        m = jnp.exp(glast) * eye - mm(kd, w, TL)
        x = x_ref[h]
        pre_ref[c, h] = x
        x = mm(m, x) + jnp.concatenate([jnp.zeros((DK, DK), F32), mm(kd, uv, TL)], 1)
        x_ref[h] = x
        last_ref[h] = x.astype(BF)
        q_ref[at, key] = q.astype(BF)
        k_ref[at, key] = k.astype(BF)
        tinv_ref[c, h] = tinv.astype(BF)
        a_ref[c, h] = a.astype(BF)
        w_ref[at, key] = w.astype(BF)
        uv_ref[at, val] = uv
        qe_ref[at, key] = (q * eg - mm(a, w)).astype(BF)
        oz_ref[at, val] = mm(a, uv)
        m_ref[c, h] = m.astype(BF)


def whole(shape):
    return pl.BlockSpec(shape, lambda c: (0,) * len(shape))


def by_rows(width, n, back=False):
    return pl.BlockSpec((CH, width), (lambda c: (n - 1 - c, 0)) if back else (lambda c: (c, 0)))


def by_chunk(shape, n, back=False):
    tail = (0,) * len(shape)
    return pl.BlockSpec((1,) + shape, (lambda c: (n - 1 - c,) + tail) if back else (lambda c: (c,) + tail))


def sds(shape, dt=F32):
    return jax.ShapeDtypeStruct(shape, dt)


def call(kernel, name, n, micros, ins, outs, scratch, *operands, room=48):
    return pl.pallas_call(
        kernel,
        grid=(n,),
        in_specs=ins,
        out_specs=[spec for spec, _ in outs],
        out_shape=[shape for _, shape in outs],
        scratch_shapes=scratch,
        compiler_params=pltpu.CompilerParams(
            vmem_limit_bytes=room * 1024 * 1024, dimension_semantics=("arbitrary",)
        ),
        cost_estimate=pl.CostEstimate(flops=micros * 10**5, bytes_accessed=micros * 10**3, transcendentals=0),
        name=name,
    )(*operands)


def delta_parts(p, first, taps, gcol, grow, tokens, heads):
    n, span, width = tokens // CH, PER * CH, heads * DV

    def rows(size, dt=F32):
        return pl.BlockSpec((span, size), lambda c: (c, 0)), sds((tokens, size), dt)

    def chunk(shape, dt=F32):
        tail = (0,) * len(shape)
        return pl.BlockSpec((PER,) + shape, lambda c: (c,) + tail), sds((n,) + shape, dt)

    halo = pl.BlockSpec((8, 2 * width), lambda c: (jnp.maximum(c * (span // 8) - 1, 0), 0))
    return call(
        functools.partial(parts_kernel, heads), "delta_parts", n // PER, 35 * tokens // 1024,
        [rows(2 * width)[0], halo, whole(first.shape), whole(taps.shape), rows(gcol.shape[1])[0], chunk(grow.shape[1:])[0]],
        [rows(2 * width), rows(heads * DK, BF), rows(heads * DK, BF), chunk((heads, CH, CH), BF), chunk((heads, CH, CH), BF),
         rows(heads * DK, BF), rows(width), rows(heads * DK, BF), rows(width), chunk((heads, DK, DK), BF),
         chunk((heads, DK, DK + DV)), (whole((heads, DK, DK + DV)), sds((heads, DK, DK + DV), BF))],
        [pltpu.VMEM((heads, DK, DK + DV), F32)],
        p, p, first, taps, gcol, grow,
    )


def entering(near, h, dims):
    state = near[-1][h].astype(F32)
    for found in near[-2::-1]:
        state = mm(found[h, :, :DK], state, dims) + found[h, :, DK:].astype(F32)
    return state


def outputs_kernel(heads, count, rows_before, pre_ref, qe_ref, oz_ref, gate_ref, gain_ref, *refs):
    near, slots, (s_ref, o_ref, gated_ref, mixed_ref, start_ref) = refs[:count], refs[count:-5], refs[-5:]

    @pl.when(pl.program_id(0) == 0)
    def _():
        for h in range(heads):
            start_ref[h] = entering(near, h, ((1,), (0,)))

    for h in range(heads):
        at = slice(h * DV, (h + 1) * DV)
        pre = pre_ref[0, h]
        s = mm(pre[:, :DK], start_ref[h]) + pre[:, DK:]
        s_ref[0, h] = s.astype(BF)
        o = mm(qe_ref[:, h * DK:(h + 1) * DK], s) + oz_ref[:, at]
        o_ref[:, at] = o
        gate = gate_ref[:, at]
        n = o * lax.rsqrt(jnp.mean(o * o, axis=-1, keepdims=True) + 1e-5)
        gated_ref[:, at] = (n * gain_ref[...] * (gate * sigmoid(gate))).astype(BF)
    gated = gated_ref[...]
    size = slots[0].shape[0] - rows_before
    for i, slot in enumerate(slots):
        mixed_ref[:, i * size:(i + 1) * size] = mm(gated, slot[rows_before:], TT).astype(BF)


def delta_outputs(near, slots, pre, qe, oz, gate, gain, rows_before, tokens, heads):
    n = tokens // CH
    wide = by_rows(heads * DV, n)
    size = len(slots) * (slots[0].shape[0] - rows_before)
    return call(
        functools.partial(outputs_kernel, heads, len(near), rows_before), "delta_outputs", n, 7 * tokens // 1024,
        [by_chunk((heads, DK, DK + DV), n), by_rows(heads * DK, n), wide, wide, whole((1, DV))]
        + [whole(a.shape) for a in (*near, *slots)],
        [(by_chunk((heads, DK, DV), n), sds((n, heads, DK, DV), BF)), (wide, sds((tokens, heads * DV))),
         (wide, sds((tokens, heads * DV), BF)), (by_rows(size, n), sds((tokens, size), BF))],
        [pltpu.VMEM((heads, DK, DV), F32)],
        pre, qe, oz, gate, gain, *near, *slots,
    )


def states_back_kernel(heads, drows_ref, out_ref, o_ref, gate_ref, gain_ref, qe_ref, m_ref, map_ref,
                       do_ref, dgate_ref, dc_ref, last_ref, dgain_ref, d_ref):
    @pl.when(pl.program_id(0) == 0)
    def _():
        d_ref[...] = jnp.zeros_like(d_ref)
        dgain_ref[...] = jnp.zeros_like(dgain_ref)
        last_ref[:, :, :DK] = map_ref[:, :, :DK]

    dgated = mm(drows_ref[...], out_ref[...])
    for h in range(heads):
        at = slice(h * DV, (h + 1) * DV)
        o, gate, dg, gain = o_ref[:, at], gate_ref[:, at], dgated[:, at], gain_ref[...]
        rstd = lax.rsqrt(jnp.mean(o * o, axis=-1, keepdims=True) + 1e-5)
        n = o * rstd
        sg = sigmoid(gate)
        act = gate * sg
        dgain_ref[...] += jnp.sum(dg * n * act, axis=0, keepdims=True)
        dgate_ref[:, at] = (dg * n * gain * (sg * (1.0 + gate * (1.0 - sg)))).astype(BF)
        dn = dg * gain * act
        do = rstd * (dn - n * jnp.mean(dn * n, axis=-1, keepdims=True))
        do_ref[:, at] = do.astype(BF)
        dc = mm(qe_ref[:, h * DK:(h + 1) * DK], do, TL)
        dc_ref[0, h] = dc
        d = mm(m_ref[0, h], d_ref[h], TL) + dc
        d_ref[h] = d
        last_ref[h, :, DK:] = d.astype(BF)


def delta_states_back(drows, out_t, o, gate, gain, qe, m, last, tokens, heads):
    n = tokens // CH
    wide = by_rows(heads * DV, n, True)
    return call(
        functools.partial(states_back_kernel, heads), "delta_states_back", n, 7 * tokens // 1024,
        [by_rows(drows.shape[1], n, True), whole(out_t.shape), wide, wide, whole((1, DV)), by_rows(heads * DK, n, True), by_chunk((heads, DK, DK), n, True),
         whole(last.shape)],
        [(wide, sds((tokens, heads * DV), BF)), (wide, sds((tokens, heads * DV), BF)),
         (by_chunk((heads, DK, DV), n, True), sds((n, heads, DK, DV))),
         (whole(last.shape), sds(last.shape, BF)), (whole((1, DV)), sds((1, DV)))],
        [pltpu.VMEM((heads, DK, DV), F32)],
        drows, out_t, o, gate, gain, qe, m, last,
    )


def normed_pull(raw, grad, scale):
    r = lax.rsqrt(jnp.sum(raw * raw, axis=-1, keepdims=True) + 1e-6)
    n = raw * r
    return (scale * r) * (grad - n * jnp.sum(grad * n, axis=-1, keepdims=True))


def conv_back(dact, at, width, sum_ref, in_ref, taps_ref, out_ref, dtaps_ref, rim_ref):
    where = slice(at, at + width)
    summed = sum_ref[:, where]
    sg = sigmoid(summed)
    dsum = dact * (sg * (1.0 + summed * (1.0 - sg)))
    ext = jnp.concatenate([dsum, rim_ref[:, where]], 0)
    rim_ref[:, where] = dsum[:8]
    conv_in = in_ref[:, where]
    dconv = jnp.zeros((CH, width), F32)
    for j in range(KC):
        moved = ext[3 - j:3 - j + CH]
        dconv = dconv + taps_ref[j:j + 1, where] * moved
        dtaps_ref[j:j + 1, where] += jnp.sum(moved * conv_in, axis=0, keepdims=True)
    out_ref[:, where] = dconv.astype(BF)


def rim_back(first_ref, taps_ref, out_ref, out_at, dtaps_ref, rim_ref):
    before = jnp.concatenate([jnp.zeros_like(rim_ref), rim_ref[...]], 0)
    conv_in = first_ref[RIM - 8:]
    drim = jnp.zeros(rim_ref.shape, F32)
    for j in range(KC):
        moved = before[3 - j:3 - j + 8]
        drim = drim + taps_ref[j:j + 1] * moved
        dtaps_ref[j:j + 1] += jnp.sum(moved * conv_in, axis=0, keepdims=True)
    width = rim_ref.shape[1]
    out_ref[:RIM, out_at:out_at + width] = jnp.concatenate([jnp.zeros_like(drim), drim], 0).astype(BF)


def inputs_back_kernel(heads, dc_ref, m_ref, s_ref, do_ref, uv_ref, w_ref, a_ref, tinv_ref, q_ref, k_ref,
                       sum_ref, p_ref, dgate_ref, first_ref, taps_ref, gcol_ref, grow_ref, *refs):
    near, (dall_ref, dtaps_ref, ds_ref, rim_ref) = refs[:-4], refs[-4:]
    last = pl.num_programs(0) - 1

    @pl.when(pl.program_id(0) == 0)
    def _():
        for h in range(heads):
            ds_ref[h] = entering(near, h, ((0,), (0,)))
        for ref in (rim_ref, dtaps_ref):
            ref[...] = jnp.zeros_like(ref)

    @pl.when(pl.program_id(0) == last)
    def _():
        rim_back(first_ref, taps_ref, dall_ref, 0, dtaps_ref, rim_ref)
        dall_ref[:RIM, 2 * heads * DV:] = jnp.zeros((RIM, heads * DV), BF)

    @pl.when(pl.program_id(0) < last)
    def _():
        rows, cols = square_index()
        dall_ref[:, 2 * heads * DV:] = dgate_ref[...]
        for h in range(heads):
            ds = ds_ref[h]
            s = s_ref[0, h]
            do = do_ref[:, h * DV:(h + 1) * DV]
            q = q_ref[:, h * DK:(h + 1) * DK]
            k = k_ref[:, h * DK:(h + 1) * DK]
            gcol = gcol_ref[:, h:h + 1]
            beta = gcol_ref[:, heads + h:heads + h + 1]
            grow = grow_ref[0, h:h + 1, :]
            glast = grow[:, CH - 1:CH]
            ratio = jnp.exp(jnp.where(rows >= cols, gcol - grow, -1e30))
            eg = jnp.exp(gcol)
            el = jnp.exp(glast - gcol)
            u = uv_ref[:, h * DV:(h + 1) * DV] - mm(w_ref[:, h * DK:(h + 1) * DK], s)
            du = mm(a_ref[0, h], do, TL) + el * mm(k, ds)
            da = ratio * mm(do, u, TT)
            drv = mm(tinv_ref[0, h], du, TL)
            drk = mm(drv, s, TT)
            dl = jnp.where(rows > cols, (-beta) * ratio * mm(drv, u, TT), 0.0)
            dq = eg * mm(do, s, TT) + mm(da, k)
            dk = el * mm(u, ds, TT) + mm(da, q, TL) - (beta * eg) * drk + mm(dl, k) + mm(dl, k, TL)
            ds_ref[h] = mm(m_ref[0, h], ds, TL) + dc_ref[0, h]
            summed = sum_ref[:, 2 * h * DK:2 * (h + 1) * DK]
            act = summed * sigmoid(summed)
            dact = jnp.concatenate([normed_pull(act[:, :DK], dq, DK ** -0.5), normed_pull(act[:, DK:], dk, 1.0)], 1)
            conv_back(dact, 2 * h * DK, 2 * DK, sum_ref, p_ref, taps_ref, dall_ref, dtaps_ref, rim_ref)
            conv_back(beta * drv, (heads + h) * DV, DV, sum_ref, p_ref, taps_ref, dall_ref, dtaps_ref, rim_ref)


def delta_inputs_back(near, dc, m, s, do, uv, w, a, tinv, q, k, summed, p, dgate, first, taps, gcol, grow,
                      tokens, heads):
    n = tokens // CH

    def at(c):
        return jnp.maximum(n - 1 - c, 0)

    def rows(width):
        return pl.BlockSpec((CH, width), lambda c: (at(c), 0))

    def chunk(shape):
        return pl.BlockSpec((1,) + shape, lambda c: (at(c),) + (0,) * len(shape))

    width = heads * DV
    wide, key = rows(width), rows(heads * DK)
    out = pl.BlockSpec((CH, 3 * width), lambda c: (jnp.where(c == n, n, n - 1 - c), 0))
    return call(
        functools.partial(inputs_back_kernel, heads), "delta_inputs_back", n + 1, 19 * tokens // 1024,
        [chunk((heads, DK, DV)), chunk((heads, DK, DK)), chunk((heads, DK, DV)),
         wide, wide, key, chunk((heads, CH, CH)), chunk((heads, CH, CH)), key, key,
         rows(2 * width), rows(2 * width), wide, whole(first.shape), whole(taps.shape), rows(gcol.shape[1]),
         chunk(grow.shape[1:])] + [whole(a.shape) for a in near],
        [(out, sds((tokens + RIM, 3 * width), BF)),
         (whole(taps.shape), sds(taps.shape))],
        [pltpu.VMEM((heads, DK, DV), F32), pltpu.VMEM((8, 2 * width), F32)],
        dc, m, s, do, uv, w, a, tinv, q, k, summed, p, dgate, first, taps, gcol, grow, *near,
    )


def as_column(row):
    size = row.shape[1]
    found = []
    for at in range(0, size, CH):
        part = row[:, at:min(at + CH, size)]
        if part.shape[1] < CH:
            part = jnp.concatenate([part, jnp.zeros((1, CH - part.shape[1]), F32)], 1)
        found.append(jnp.broadcast_to(part, (CH, CH)).T[:min(CH, size - at), 0:1])
    return jnp.concatenate(found, 0)


def moments_kernel(plan, over_head_ref, over_seq_ref, old_ref, carried_ref, place_ref, conv_second_ref,
                   both_ref, go_ref, outg_ref, ex_ref, sh_ref, *outs):
    beta_two = 1.0 - STEP ** (-0.8)
    (in_rows, in_cols, out_rows, out_cols, ex_rows, ex_cols, sh_rows, sh_cols, late_ref, kernel_ref, second_ref, update_ref,
     in_row, in_col, out_row, out_col, ex_row, ex_col, sh_row, sh_col) = outs
    heads = in_cols.shape[0]
    span = in_rows.shape[1]
    place = lax.broadcasted_iota(jnp.int32, (1, 128), 1)
    sums = carried_ref[...]
    sources = {"head": over_head_ref, "seq": over_seq_ref}

    def moment(name, old_at):
        axis, start, size, over = plan["cells"][name]
        old = old_ref[:, old_at:old_at + size]
        new = beta_two * old + (1.0 - beta_two) * (sources[axis][:, start:start + size] * (1.0 / over) + 1e-30)
        return new, lax.rsqrt(new)

    parts = {
        "in": (both_ref[:span], both_ref[span:], go_ref[:span]),
        "out": (outg_ref[...],),
        "expand": (ex_ref[...].astype(F32),),
        "shrink": (sh_ref[...].astype(F32),),
    }
    refs = {
        "in": (in_rows, in_cols, in_row, in_col), "out": (out_rows, out_cols, out_row, out_col),
        "expand": (ex_rows, ex_cols, ex_row, ex_col), "shrink": (sh_rows, sh_cols, sh_row, sh_col),
    }
    for slot, name in enumerate(parts):
        rows_new, row_root = moment(name + "_rows", plan["old"][name + "_rows"])
        cols_new, col_root = moment(name + "_cols", plan["old"][name + "_cols"])
        rows_ref, cols_ref, row_ref, col_ref = refs[name]
        column = as_column(row_root)
        row_ref[...] = column
        col_ref[...] = col_root
        total, start = 0.0, 0
        for part in parts[name]:
            size = part.shape[1]
            update = part * column * col_root[:, start:start + size]
            total = total + jnp.sum(update * update, axis=(0, 1), keepdims=True)
            start += size
        sums = sums + jnp.where(place == slot, total, 0.0)
        row_total = jnp.sum(rows_new, axis=(0, 1), keepdims=True) * (1.0 / plan["copies"][name])
        sums = sums + jnp.where(place == 4 + slot, row_total, 0.0)
        if name == "in":
            rows_ref[...] = rows_new
            width = heads * DV
            for h in range(heads):
                for i in range(3):
                    cols_ref[h:h + 1, i * DV:(i + 1) * DV] = cols_new[:, i * width + h * DV:i * width + (h + 1) * DV]
        elif name == "out":
            cols_ref[...] = cols_new
            for h in range(heads):
                rows_ref[h:h + 1] = rows_new[:, h * DV:(h + 1) * DV]
        elif name == "expand":
            rows_ref[...] = rows_new
            size = cols_ref.shape[1]
            for i in range(2):
                cols_ref[i:i + 1] = cols_new[:, i * size:(i + 1) * size]
        else:
            rows_ref[...] = rows_new
            cols_ref[...] = cols_new
    axis, start, _, _ = plan["cells"]["taps"]
    cut, width = kernel_ref.shape[2], heads * DV
    total = 0.0
    for j in range(KC):
        for h in range(heads):
            grad = jnp.zeros((1, cut), F32)
            for c in range(CW // cut):
                at = start + j * 2 * width + (c * cut) // DV * width + h * DV + (c * cut) % DV
                grad = grad + place_ref[0:1, c:c + 1] * sources[axis][:, at:at + cut]
            second = beta_two * conv_second_ref[j, h:h + 1, :] + (1.0 - beta_two) * (grad * grad + 1e-30)
            update = grad * lax.rsqrt(second)
            kernel_ref[j, h:h + 1, :] = grad
            second_ref[j, h:h + 1, :] = second
            update_ref[j, h:h + 1, :] = update
            total = total + jnp.sum(update * update, axis=(0, 1), keepdims=True)
    late_ref[:, :128] = sums + jnp.where(place == 13, total, 0.0)
    share = 1.0 / plan["head_count"]
    for name, at in (("gain_two", 128), ("head_gain", 128 + D)):
        axis, start, size, _ = plan["cells"][name]
        late_ref[:, at:at + size] = sources[axis][:, start:start + size] * share


def new_moments(plan, outs, operands):
    return pl.pallas_call(
        functools.partial(moments_kernel, plan),
        out_shape=[sds(a) for a in outs],
        compiler_params=pltpu.CompilerParams(vmem_limit_bytes=56 * 1024 * 1024),
        name="new_moments",
    )(*operands)


def cast_kernel(heads, in_ref, kv_ref, gate_ref):
    width = heads * DV
    for h in range(heads):
        at = slice(h * DV, (h + 1) * DV)
        kv_ref[:, at] = in_ref[:, h, :DV].astype(BF)
        kv_ref[:, width + h * DV:width + (h + 1) * DV] = in_ref[:, h, DV:2 * DV].astype(BF)
        gate_ref[:, at] = in_ref[:, h, 2 * DV:].astype(BF)


def cast_columns(weight, steps=4):
    heads, span = weight.shape[1], weight.shape[0] // steps
    width = heads * DV
    return call(
        functools.partial(cast_kernel, heads), "cast_columns", steps, 3,
        [pl.BlockSpec((span, heads, HC), lambda c: (c, 0, 0))],
        [(pl.BlockSpec((span, size), lambda c: (c, 0)), sds((weight.shape[0], size), BF)) for size in (2 * width, width)],
        [],
        weight,
    )


def joined_kernel(heads, keys_ref, vals_ref, gate_ref, out_ref):
    for h in range(heads):
        at = slice(h * DV, (h + 1) * DV)
        for i, ref in enumerate((keys_ref, vals_ref, gate_ref)):
            out_ref[:, h, i * DV:(i + 1) * DV] = ref[:, at]


def joined_columns(both, go, heads, steps=4):
    span, width = both.shape[0] // (2 * steps), both.shape[1]
    first = pl.BlockSpec((span, width), lambda c: (c, 0))
    return call(
        functools.partial(joined_kernel, heads), "joined_columns", steps, 3,
        [first, pl.BlockSpec((span, width), lambda c: (c + steps, 0)), first],
        [(pl.BlockSpec((span, heads, HC), lambda c: (c, 0, 0)), sds((both.shape[0] // 2, heads, HC)))],
        [],
        both, both, go,
    )[0]


def split_kernel(grad_ref, out_ref):
    size = out_ref.shape[2]
    for i in range(2):
        out_ref[:, i, :] = grad_ref[:, i * size:(i + 1) * size].astype(F32)


def split_columns(grad, steps=4):
    span, size = grad.shape[0] // steps, grad.shape[1] // 2
    return call(
        split_kernel, "split_columns", steps, 3,
        [pl.BlockSpec((span, 2 * size), lambda c: (c, 0))],
        [(pl.BlockSpec((span, 2, size), lambda c: (c, 0, 0)), sds((grad.shape[0], 2, size)))],
        [],
        grad,
    )[0]


def small_step(weight, gradient, second_old, beta_two):
    second_new = beta_two * second_old + (1.0 - beta_two) * (gradient * gradient + 1e-30)
    update = gradient * lax.rsqrt(second_new)
    root = jnp.sqrt(jnp.mean(update * update, axis=-1, keepdims=True))
    scale = 0.3 * jnp.maximum(0.001, jnp.sqrt(jnp.mean(weight * weight, axis=-1, keepdims=True)))
    return second_new, weight - scale * (update / jnp.maximum(1.0, root))


def weights_kernel(heads, late_ref, gains_ref, gains_second_ref, head_ref, head_second_ref, conv_ref, conv_update_ref,
                   in_ref, keys_ref, vals_ref, gate_ref, in_row, in_col, out_ref, outg_ref, out_row, out_col,
                   ex_ref, exg_ref, ex_row, ex_col, sh_ref, shg_ref, sh_row, sh_col,
                   gains_grad, gains_second_new, gains_new, head_grad, head_second_new, head_new, conv_new,
                   in_new, out_new, ex_new, sh_new):
    beta_two = 1.0 - STEP ** (-0.8)
    counts = ((D, HEAD_TOTAL * HC), (HEAD_TOTAL * DV, D), (D, 2 * FF), (FF, D))

    def cell(at):
        return late_ref[0:1, at:at + 1]

    def size_of(weight, entries):
        return 0.3 * jnp.maximum(0.001, jnp.sqrt(weight * (1.0 / entries)))

    def scale(slot):
        mean, entries = cell(4 + slot) * (1.0 / counts[slot][0]), counts[slot][0] * counts[slot][1]
        root = jnp.sqrt(cell(slot) * mean * (1.0 / entries))
        return size_of(cell(8 + slot), entries) * jnp.sqrt(mean) / jnp.maximum(1.0, root)

    scales = [scale(slot) for slot in range(4)]

    @pl.when(pl.program_id(0) == 0)
    def _():
        for row in range(2):
            first = 128 if row else 128 + D + DV
            grad = late_ref[0:1, first:first + D]
            at = slice(row, row + 1)
            gains_grad[at] = grad
            gains_second_new[at], gains_new[at] = small_step(gains_ref[at], grad, gains_second_ref[at], beta_two)
        grad = late_ref[0:1, 128 + D:128 + D + DV]
        head_grad[...] = grad
        head_second_new[...], head_new[...] = small_step(head_ref[...], grad, head_second_ref[...], beta_two)
        entries = KC * HEAD_TOTAL * CW
        factor = size_of(cell(12), entries) / jnp.maximum(1.0, jnp.sqrt(cell(13) * (1.0 / entries)))
        conv_new[...] = conv_ref[...] - conv_update_ref[...] * factor[None]

    def stepped(weight, grad, rows, cols, slot):
        return weight - (grad.astype(F32) * cols) * (rows * scales[slot])

    width = heads * DV
    for h in range(heads):
        for i, ref in enumerate((keys_ref, vals_ref, gate_ref)):
            col = in_col[:, i * width + h * DV:i * width + (h + 1) * DV]
            at = slice(i * DV, (i + 1) * DV)
            in_new[:, h, at] = stepped(in_ref[:, h, at], ref[:, h * DV:(h + 1) * DV], in_row[...], col, 0)
    out_new[...] = stepped(out_ref[...], outg_ref[...], out_row[...], out_col[...], 1)
    size = ex_ref.shape[2]
    for i in range(2):
        at = slice(i * size, (i + 1) * size)
        ex_new[:, i, :] = stepped(ex_ref[:, i, :], exg_ref[:, at], ex_row[...], ex_col[:, at], 2)
    sh_new[...] = stepped(sh_ref[...], shg_ref[...], sh_row[...], sh_col[...], 3)


def new_weights(heads, small, groups):
    ins, operands = [whole(a.shape) for a in small], list(small)
    late, gains, _, head = small[:4]
    outs = [(whole(a.shape), sds(a.shape)) for a in (gains, gains, gains, head, head, head, small[5])]
    steps = 8 if groups[3][0].shape[0] % 128 == 0 else 4

    def blocked(a, span, first=0):
        tail = a.shape[1:]
        return pl.BlockSpec((span,) + tail, lambda c: (c + first,) + (0,) * len(tail))

    for weight, parts, rows, cols in groups:
        span = weight.shape[0] // steps
        for i, a in enumerate((weight, *parts, rows)):
            ins.append(blocked(a, span, steps if len(parts) == 3 and i == 2 else 0))
            operands.append(a)
        ins.append(whole(cols.shape))
        operands.append(cols)
        outs.append((blocked(weight, span), sds(weight.shape)))
    return call(functools.partial(weights_kernel, heads), "new_weights", steps, 10, ins, outs, [], *operands, room=56)


def ring(x, by=1):
    n = lax.axis_size("seq")
    return lax.ppermute(x, "seq", [(i, (i + by) % n) for i in range(n)])


def ahead(x, by):
    n = lax.axis_size("seq")
    return lax.ppermute(x, "seq", [(i, i + by) for i in range(n) if 0 <= i + by < n])


def after(x, *others):
    return lax.optimization_barrier((x,) + others)[0]


def ring_gather(x, hold=None):
    slots = [x]
    for k in range(1, lax.axis_size("seq")):
        slots.append(ring(after(slots[-1], *(hold or {}).get(k, ()))))
    return slots


def vector_of(scalars, size, first=0):
    place = lax.broadcasted_iota(jnp.int32, (1, size), 1)
    return sum(jnp.where(place == first + i, a, 0.0) for i, a in enumerate(scalars))


def ring_scatter(part, hold=None):
    n = lax.axis_size("seq")
    total, totals = part(1).astype(BF), []
    for k in range(1, n):
        held = hold(k) if hold else ()
        total = ring(after(total, *held) if held else total).astype(F32) + part((k + 1) % n).astype(F32)
        total = total if k == n - 1 else total.astype(BF)
        totals.append(total)
    return total, totals


def seq_slot(x, k, axis=0):
    n, z = lax.axis_size("seq"), lax.axis_index("seq")
    span = x.shape[axis] // n
    return lax.dynamic_slice_in_dim(x, lax.rem(z - k + n, n) * span, span, axis)


def in_order(slots, axis=0):
    n, z = lax.axis_size("seq"), lax.axis_index("seq")
    span = slots[0].shape[axis]
    turned = jnp.concatenate(slots[::-1] + slots[:0:-1], axis)
    return lax.dynamic_slice_in_dim(turned, (n - 1 - z) * span, n * span, axis)


def gather_head(x, axis=0):
    return lax.all_gather(x, "head", axis=axis, tiled=True)


def scatter_head(x, axis=0):
    return lax.psum_scatter(x, "head", scatter_dimension=axis, tiled=True)


def total_over(axis, x):
    n = lax.axis_size(axis)
    if n & (n - 1):
        return lax.psum(x, axis)
    step = 1
    while step < n:
        x = x + lax.ppermute(x, axis, [(i, i ^ step) for i in range(n)])
        step *= 2
    return x


def dot(a, b, dims=((1,), (0,)), out=F32):
    return lax.dot_general(a, b, (dims, ((), ())), preferred_element_type=out)


def norm_rows(entries, scale_row):
    return entries * lax.rsqrt(jnp.mean(entries * entries, axis=-1, keepdims=True) + 1e-06) * scale_row


def nearby(last, backward):
    n, sign = lax.axis_size("seq"), -1 if backward else 1
    near = [ahead(last, sign * k) for k in range(1, n - 1)]
    return near + [ahead(last[..., DK:], sign * (n - 1))]


def local(
    hidden_in,
    out_grad,
    decays,
    strength,
    mixer_in,
    mixer_in_rows,
    mixer_in_cols,
    mixer_out,
    mixer_out_rows,
    mixer_out_cols,
    feed_in,
    feed_in_rows,
    feed_in_cols,
    feed_out,
    feed_out_rows,
    feed_out_cols,
    conv_kernel,
    conv_second,
    norm_gains,
    gains_second,
    head_gain,
    head_gain_second,
):
    beta_two = 1.0 - STEP ** (-0.8)
    n = lax.axis_size("seq")
    seq_count, head_count = n, lax.axis_size("head")
    tokens, heads = decays.shape
    blocks = tokens // CH
    in_span = mixer_in.shape[0]
    out_span = mixer_out.shape[2]
    feed_span, hidden_span = feed_in.shape[0], feed_in.shape[2]
    width = heads * DV

    def padded(pieces):
        found, cells, at = [], {}, 0
        for name, piece in pieces.items():
            piece = piece.reshape(1, -1)
            size = piece.shape[1]
            room = -(-size // 128) * 128
            found.append(jnp.pad(piece, ((0, 0), (0, room - size))))
            cells[name] = (at, size)
            at += room
        return jnp.concatenate(found, 1), cells

    old_moments, old_cells = padded(
        {
            "in_rows": mixer_in_rows,
            "in_cols": jnp.stack([mixer_in_cols[:, i * DV : (i + 1) * DV] for i in range(3)]),
            "out_rows": mixer_out_rows,
            "out_cols": mixer_out_cols,
            "expand_rows": feed_in_rows,
            "expand_cols": feed_in_cols,
            "shrink_rows": feed_out_rows,
            "shrink_cols": feed_out_cols,
        }
    )
    over_counts = {
        "in_rows": HEAD_TOTAL * HC, "in_cols": D, "out_rows": D, "out_cols": HEAD_TOTAL * DV,
        "expand_rows": 2 * FF, "expand_cols": D, "shrink_rows": D, "shrink_cols": FF,
    }
    place = jnp.where(lax.broadcasted_iota(jnp.int32, (1, 128), 1) == lax.axis_index("seq"), 1.0, 0.0)

    x = hidden_in.astype(F32)
    rows_all = gather_head(norm_rows(x, norm_gains[0]).astype(BF))
    kv_own, gate_own = cast_columns(mixer_in)
    taps_mine = conv_kernel.astype(BF).reshape(KC, heads * conv_kernel.shape[2])
    taps_slots = [taps_mine] + [ring(taps_mine, k) for k in range(1, n)]
    kv_slots = ring_gather(kv_own, {2: taps_slots[1:]})[:3]
    rim = ahead(rows_all[tokens - RIM :], 1)
    taps = in_order([t[None] for t in taps_slots]).reshape(n, KC, heads, -1)
    taps = jnp.moveaxis(taps, 0, 2).reshape(KC, heads, CW).astype(F32)
    taps = jnp.concatenate([taps[:, :, : 2 * DK].reshape(KC, width), taps[:, :, 2 * DK :].reshape(KC, width)], 1)

    lower = jnp.tril(jnp.ones((CH, CH), F32))
    log_sum = jnp.einsum(
        "ij,bjh->bih", lower, jnp.log(decays).reshape(blocks, CH, heads), precision=lax.Precision.HIGHEST
    )
    gcol = jnp.concatenate([log_sum.reshape(tokens, heads), strength, jnp.zeros((tokens, 8 - 2 * heads), F32)], 1)
    grow = jnp.concatenate([jnp.swapaxes(log_sum, 1, 2), jnp.zeros((blocks, 8 - heads, CH), F32)], 1)
    gain_row = head_gain[None]
    row_slots = [seq_slot(rows_all, k, 1) for k in range(n)]

    def projected(parts, slots, total=None):
        for part, slot in zip(parts, slots):
            found = dot(part, slot)
            total = found if total is None else total + found
        return total

    expand = gather_head(after(feed_in.astype(BF).reshape(feed_span, 2 * hidden_span), rows_all, kv_slots[1]))
    p_start = projected(row_slots[:2], kv_slots[:2])
    kv_held, p_start, rim = lax.optimization_barrier((kv_slots[2], p_start, rim))
    kv_slots[2] = kv_held
    for _ in range(3, n):
        kv_slots.append(ring(kv_slots[-1]))
    rim_slots = [seq_slot(rim, k, 1) for k in range(n)]
    p_kv, r_kv = projected(row_slots[2:], kv_slots[2:], p_start), projected(rim_slots, kv_slots)
    go_own = jnp.concatenate([gate_own, mixer_out.astype(BF).reshape(width, out_span).T], 0)
    go_slots = ring_gather(go_own, {1: (kv_slots[-1],)})[:2]
    (summed, q, k, tinv, scores, w, uv, qe, oz, m, pre, last) = delta_parts(
        p_kv, r_kv, taps, gcol, grow, tokens, heads
    )
    last, go_one, go_zero, expand = lax.optimization_barrier((last, go_slots[1], go_slots[0], expand))
    go_slots = [go_zero, go_one]
    for _ in range(2, n):
        go_slots.append(ring(go_slots[-1]))
    shrink = gather_head(after(feed_out.astype(BF), expand, last, go_slots[2]), 1)
    p_gate = projected(row_slots, [a[:in_span] for a in go_slots])
    states, o, gated, mixed = delta_outputs(
        nearby(last, False), go_slots, pre, qe, oz, p_gate, gain_row, in_span, tokens, heads
    )
    grad_slots = ring_gather(out_grad, {1: (go_slots[-1],)})
    grad_rows = jnp.concatenate(grad_slots, 0)
    mixed = scatter_head(after(mixed, shrink)).astype(F32)
    mixed = in_order([mixed[:, i * out_span : (i + 1) * out_span] for i in range(n)], 1)
    residual = x + mixed
    out_t = in_order([a[in_span:] for a in go_slots])
    w_all = in_order([jnp.concatenate([a, b[:in_span]], 1) for a, b in zip(kv_slots, go_slots)])
    weights_then = lax.optimization_barrier((mixer_in, mixer_out, feed_in, feed_out, gated))[:4]
    weight_sums = vector_of([jnp.sum(a * a) for a in (*weights_then, conv_kernel)], 128, 8)

    normed_two, norm_two_pull = jax.vjp(norm_rows, residual, norm_gains[1])
    d_hidden = lax.optimization_barrier(dot(grad_rows, shrink, ((1,), (1,))))
    feed_held, out_t, w_all, weight_sums, old_moments = lax.optimization_barrier(
        (normed_two.astype(BF), out_t, w_all, weight_sums, old_moments)
    )
    feed_slots = ring_gather(feed_held, {1: (grad_slots[-1],), 2: (d_hidden,)})
    feed_rows = jnp.concatenate(feed_slots, 0)
    gate_up = dot(feed_rows, expand)
    gate, up = gate_up[:, :hidden_span], gate_up[:, hidden_span:]
    sig = sigmoid(gate)
    silu = gate * sig
    hidden = (silu * up).astype(BF)
    d_gate_up = jnp.concatenate(
        [d_hidden * up * (sig * (1.0 + gate * (1.0 - sig))), d_hidden * silu], 1
    ).astype(BF)
    rows_here = hidden_in.shape[0]

    def slot_rows(a, k):
        return a[k * rows_here : (k + 1) * rows_here]

    d_feed_rows = dot(d_gate_up, expand, ((1,), (1,)))
    d_normed_two, _ = ring_scatter(lambda k: slot_rows(d_feed_rows, k))
    d_residual_part, d_gain_two = norm_two_pull(d_normed_two)
    d_residual = out_grad.astype(F32) + d_residual_part
    d_residual_low = d_residual.astype(BF)
    d_rows = gather_head(d_residual_low)
    hidden_then, feed_rows_then, _ = lax.optimization_barrier((hidden, feed_rows, d_residual_low))
    shrink_part = dot(hidden_then, grad_rows, ((0,), (0,)), BF)
    feed_part = dot(hidden_then, shrink, out=BF)
    feed_part = in_order([slot_rows(feed_part, i) for i in range(n)])
    expand_part = dot(feed_rows_then, d_gate_up, ((0,), (0,)), BF)
    shrink_part, expand_part, feed_part, d_rows = lax.optimization_barrier(
        (shrink_part, expand_part, feed_part, d_rows)
    )
    shrink_low = scatter_head(shrink_part, 1)

    do, d_gate, dc, d_last, d_head_gain = delta_states_back(d_rows, out_t, o, p_gate, gain_row, qe, m, last, tokens, heads)
    near = nearby(d_last, True)
    gate_then, d_rows_then, _ = lax.optimization_barrier((d_gate, d_rows, d_last))

    def go_part(k, out=F32, rows=d_rows_then):
        d_slot = seq_slot(rows, k, 1)
        return jnp.concatenate([dot(row_slots[k], gate_then, TL, out), dot(d_slot, gated, TL, out)], 0)

    def added(arrived, part):
        return arrived.astype(F32) + part.astype(F32)

    go, go_next = lax.optimization_barrier((go_part(1, BF), go_part(2 % n), *near))[:2]
    sent = ring(go)
    d_all, d_taps = delta_inputs_back(
        near, dc, m, states, do, uv, w, scores, tinv, q, k, summed, p_kv, d_gate, r_kv, taps, gcol, grow, tokens, heads
    )
    d_all, sent, go_next, gate_then, d_rows_then, shrink_low = lax.optimization_barrier(
        (d_all, sent, go_next, gate_then, d_rows_then, shrink_low)
    )
    more_slots = [jnp.concatenate([a, b], 0) for a, b in zip(row_slots, rim_slots)]
    expand_low = scatter_head(after(expand_part, shrink_low, d_all))
    shrink_g, expand_g = shrink_low.astype(F32), expand_low.astype(F32)

    def both_part(k, out=F32):
        found = [dot(more_slots[k], d_all[:, i * width : (i + 1) * width], TL, out) for i in range(2)]
        return jnp.concatenate(found, 0)

    go = added(sent, go_next).astype(BF)
    both = both_part(1, BF)
    sent = ring(jnp.concatenate([go, both], 0))
    d_rows_more = dot(after(d_all, both), w_all, ((1,), (1,)), BF)
    parts = [jnp.concatenate([go_part((step + 1) % n, F32, d_rows_then), both_part(step)], 0) for step in range(2, n)]
    rim_rows, last_part, *parts = lax.optimization_barrier((d_rows_more[tokens:], both_part(0), *parts))
    rim_back = ahead(rim_rows, -1)
    d_rows_in = jnp.concatenate([d_rows_more[: tokens - RIM], d_rows_more[tokens - RIM : tokens] + rim_back], 0)
    feed_sums = (jnp.sum(expand_g * expand_g, 0), jnp.sum(shrink_g * shrink_g, 1))
    feed_sums += (jnp.sum(expand_g * expand_g, 1), jnp.sum(shrink_g * shrink_g, 0))
    for step in range(2, n):
        total = added(sent, parts[step - 2])
        if step < n - 1:
            sent = ring(total.astype(BF))
    d_normed_low = scatter_head(after(d_rows_in, expand_low, sent))
    go, both = total[: 2 * in_span], total[2 * in_span :].astype(BF)
    both, *feed_sums = lax.optimization_barrier((both, *feed_sums))
    both_grad = added(ring(both), last_part)
    go = lax.optimization_barrier(go)
    out_g = lax.optimization_barrier(go[in_span:].T)
    d_normed = d_normed_low.astype(F32)

    _, norm_one_pull = jax.vjp(norm_rows, x, norm_gains[0])
    d_residual_one, d_gain_one = norm_one_pull(d_normed)
    input_grad = d_residual + d_residual_one


    out_sq, both_sq, gate_sq = out_g * out_g, both_grad * both_grad, go[:in_span] * go[:in_span]
    over_head, head_cells = padded(
        {
            "expand_cols": feed_sums[0],
            "shrink_rows": feed_sums[1],
            "gain_two": d_gain_two,
            "head_gain": d_head_gain,
            "out_cols": jnp.sum(out_sq, 0),
            "in_rows": jnp.sum(both_sq[:in_span], 1) + jnp.sum(both_sq[in_span:], 1) + jnp.sum(gate_sq, 1),
        }
    )
    over_seq, seq_cells = padded(
        {
            "expand_rows": feed_sums[2],
            "shrink_cols": feed_sums[3],
            "taps": d_taps,
            "out_rows": jnp.sum(out_sq, 1),
            "in_cols": jnp.concatenate([jnp.sum(a, 0) for a in (both_sq[:in_span], both_sq[in_span:], gate_sq)]),
        }
    )
    both_then, over_head, over_seq = lax.optimization_barrier((both_grad, over_head, over_seq))
    in_grad = joined_columns(both_then, go, heads)
    expand_out = split_columns(expand_low)
    over_head, over_seq = total_over("head", over_head), total_over("seq", over_seq)

    cells = {}
    for axis, found in (("head", head_cells), ("seq", seq_cells)):
        for name, (at, size) in found.items():
            cells[name] = (axis, at, size, over_counts.get(name))
    plan = {
        "cells": cells,
        "old": {name: at for name, (at, _) in old_cells.items()},
        "copies": {"in": head_count, "out": seq_count, "expand": seq_count, "shrink": head_count},
        "head_count": head_count,
    }
    shape = {name: (1, size) for name, (_, _, size, _) in cells.items()}
    conv_shape = conv_kernel.shape
    (in_rows_new, in_cols_new, out_rows_new, out_cols_new, expand_rows_new, expand_cols_new, shrink_rows_new,
     shrink_cols_new, late, kernel_grad, conv_second_new, conv_update, *roots) = new_moments(
        plan,
        [shape["in_rows"], (heads, HC), (heads, DV), shape["out_cols"], shape["expand_rows"], (2, hidden_span),
         shape["shrink_rows"], shape["shrink_cols"], (1, 128 + D + DV), conv_shape, conv_shape, conv_shape]
        + [a for name in ("in", "out", "expand", "shrink") for a in ((shape[name + "_rows"][1], 1), shape[name + "_cols"])],
        [over_head, over_seq, old_moments, weight_sums, place, conv_second,
         both_grad, go, out_g, expand_low, shrink_low],
    )
    feed_sum = lax.psum_scatter(after(feed_part, d_normed_low, late), "seq", scatter_dimension=0, tiled=True).astype(F32)
    block_out = (residual + feed_sum).astype(BF)

    late = total_over("seq", total_over("head", jnp.concatenate([late, d_gain_one[None]], 1)))
    (gains_grad, gains_second_new, gains_new, head_gain_grad, head_second_new, head_new, conv_new,
     in_new, out_new, expand_new, shrink_new) = new_weights(
        heads,
        (late, norm_gains, gains_second, head_gain[None], head_gain_second[None], conv_kernel, conv_update),
        [
            (mixer_in, (both_grad, both_grad, go), *roots[0:2]),
            (mixer_out.reshape(width, out_span), (out_g,), *roots[2:4]),
            (feed_in, (expand_low,), *roots[4:6]),
            (feed_out, (shrink_low,), *roots[6:8]),
        ],
    )
    return (
        block_out,
        input_grad,
        in_grad,
        in_rows_new.reshape(-1),
        in_cols_new,
        in_new,
        out_g.reshape(mixer_out.shape),
        out_rows_new,
        out_cols_new.reshape(-1),
        out_new.reshape(mixer_out.shape),
        expand_out,
        expand_rows_new.reshape(-1),
        expand_cols_new,
        expand_new,
        shrink_g,
        shrink_rows_new.reshape(-1),
        shrink_cols_new.reshape(-1),
        shrink_new,
        kernel_grad,
        conv_second_new,
        conv_new,
        gains_grad,
        gains_second_new,
        gains_new,
        head_gain_grad.reshape(-1),
        head_second_new.reshape(-1),
        head_new.reshape(-1),
    )


def solution(mesh):
    return jax.shard_map(
        local,
        mesh=mesh,
        in_specs=(
            P(("seq", "head"), None),
            P(("seq", "head"), None),
            P("seq", "head"),
            P("seq", "head"),
            P("seq", "head", None),
            P("seq"),
            P("head", None),
            P("head", None, "seq"),
            P("head", None),
            P("seq"),
            P("head", None, "seq"),
            P("head"),
            P(None, "seq"),
            P("seq", "head"),
            P("seq"),
            P("head"),
            P(None, "head", "seq"),
            P(None, "head", "seq"),
            P(),
            P(),
            P(),
            P(),
        ),
        out_specs=(
            P(("seq", "head"), None),
            P(("seq", "head"), None),
            P("seq", "head", None),
            P("seq"),
            P("head", None),
            P("seq", "head", None),
            P("head", None, "seq"),
            P("head", None),
            P("seq"),
            P("head", None, "seq"),
            P("head", None, "seq"),
            P("head"),
            P(None, "seq"),
            P("head", None, "seq"),
            P("seq", "head"),
            P("seq"),
            P("head"),
            P("seq", "head"),
            P(None, "head", "seq"),
            P(None, "head", "seq"),
            P(None, "head", "seq"),
            P(),
            P(),
            P(),
            P(),
            P(),
            P(),
        ),
        check_vma=False,
    )
```

time: 1260 us -> 704 us (0.56)
  waiting for transfers between devices: 702 us -> 339 us
  blocking collectives: 132 us -> 0 us
  other arithmetic: 123 us -> 60.6 us
  starting transfers between devices: 4.38 us -> 43.9 us
  matrix products: 114 us -> 84.6 us
  between operations: 28.8 us -> 15.9 us
    reduce_scatter x8 -> x5, waiting for transfers between devices: 381 us -> 8.21 us  [the longest x4 7.01 us: scatter_head(): return lax.psum_scatter(x, 'head', scatter_dimension=axis, tiled=True)]
    ppermute x2 -> x40, waiting for transfers between devices: 7.21 us -> 317 us  [the longest x22 238 us: ring(): return lax.ppermute(x, 'seq', [(i, (i + by) % n) for i in range(n)])]
    all_gather x4 -> x0, waiting for transfers between devices: 170 us -> none  [gather_seq(): return lax.all_gather(x, 'seq', axis=axis, tiled=True)]
    all_gather x4, waiting for transfers between devices: 143 us -> 13.2 us  [gather_head(): return lax.all_gather(x, 'head', axis=axis, tiled=True)]
    psum x4 -> x0, blocking collectives: 85.3 us -> none  [the longest x2 40.6 us: local(): late = lax.psum(lax.psum(late, 'head'), 'seq')]
    all_gather x3 -> x0, blocking collectives: 47 us -> none  [the longest x1 17.9 us: local(): all_last = lax.all_gather(last.astype(BF), 'seq', axis=0)]
    ppermute x2 -> x40, starting transfers between devices: 2.57 us -> 42.6 us  [the longest x22 17.9 us: ring(): return lax.ppermute(x, 'seq', [(i, (i + by) % n) for i in range(n)])]
    reduce_sum x19 -> x9, other arithmetic: 38.4 us -> 12.1 us  [the longest x5 9.83 us: local(): jnp.sum(a * a)]
  transfers between devices with their start and end apart: 19 -> 49, of which waited for: 13 -> 31; matrix products, arithmetic and copies ran while one was open for 14% -> 22% of each run, Pallas kernels for 7% -> 13%
where the time goes in v2:
time: 704 us; the launch traced here: 696 us
  waiting for transfers between devices  339 us (48%)
  Pallas kernels  92.8 us (13%)
  matrix products  84.6 us (12%)
  other arithmetic  60.6 us (9%)
  local copies, waits for them, and re-layouts  59.2 us (8%)
  starting transfers between devices  43.9 us (6%)
  between operations  15.9 us (2%)
    ppermute x22, waiting for transfers between devices, ring(): return lax.ppermute(x, 'seq', [(i, (i + by) % n) for i in range(n)])  238 us
    pallas_call x8, Pallas kernels, call(): pl.pallas_call(kernel, grid=(n,), in_specs=ins, out_specs=[spec for spec,...  86.2 us
    dot_general x35, matrix products, dot(): return lax.dot_general(a, b, (dims, ((), ())), preferred_element_type=out)  84.5 us
    ppermute x8, waiting for transfers between devices, ahead(): lax.ppermute(x, 'seq', [(i, i + by) for i in range(n) if 0 <= i + by < n])  63.9 us
    unnamed x247, local copies, waits for them, and re-layouts  36.8 us
    ppermute x22, starting transfers between devices, ring(): return lax.ppermute(x, 'seq', [(i, (i + by) % n) for i in range(n)])  17.9 us
    ppermute x8, starting transfers between devices, ahead(): lax.ppermute(x, 'seq', [(i, i + by) for i in range(n) if 0 <= i + by < n])  17.4 us
    ppermute x10, waiting for transfers between devices, total_over(): x = x + lax.ppermute(x, axis, [(i, i ^ step) for i in range(n)])  15.5 us
  transfers between devices with their start and end apart: 49, of which 31 were waited for; matrix products, arithmetic and copies ran while one was open for 22% of the time, Pallas kernels for 13%

profile of v2, /device:TPU:0, one launch (start us, length us, event | category | flops | bytes accessed | tf_op | source)
XLA Modules:
  0.0 696.2 jit_solution(2387101292217010081)
XLA Ops:
  22.9 23.0 %collective-permute-done = bf16[512,1024]{1,0:T(8,128)(2,1)} collective-permute-done((bf16[512,1024]{1,0:T(8,128)(2,1)S(1)}, bf16[512,1024]{1,0:T(8,128)(2,1)}, u32[]{:S(2)}, u32[]{:S(2)}) %collective-permute-start) | collective-permute-done | bytes 1048608 | tf_op jit(solution)/shard_map/ppermute | solution.py:622
  71.5 16.2 %collective-permute-done.4 = bf16[512,1024]{1,0:T(8,128)(2,1)S(1)} collective-permute-done((bf16[512,1024]{1,0:T(8,128)(2,1)}, bf16[512,1024]{1,0:T(8,128)(2,1)S(1)}, u32[]{:S(2)}, u32[]{:S(2)}) %collective-permute-start.4) | collective-permute-done | bytes 1048608 | tf_op jit(solution)/shard_map/ppermute | solution.py:622
  91.2 21.8 %collective-permute-done.6 = bf16[512,1024]{1,0:T(8,128)(2,1)S(1)} collective-permute-done((bf16[512,1024]{1,0:T(8,128)(2,1)S(1)}, bf16[512,1024]{1,0:T(8,128)(2,1)S(1)}, u32[]{:S(2)}, u32[]{:S(2)}) %collective-permute-start.6) | collective-permute-done | bytes 1048608 | tf_op jit(solution)/shard_map/ppermute | solution.py:622
  117.2 22.3 %delta_parts.1 = (f32[1024,1024]{1,0:T(8,128)}, bf16[1024,256]{1,0:T(8,128)(2,1)S(1)}, bf16[1024,256]{1,0:T(8,128)(2,1)S(1)}, bf16[8,2,128,128]{3,2,1,0:T(8,128)...) custom-call(f32[1024,1024]{1,0:T(8,128)} %add_add_fusion.p_ref.halo_, ...), custom_call_target="tpu_custom_call" | custom-call | flops 3500000 | bytes 35000 | tf_op jit(solution)/shard_map/delta_parts/pallas_call | solution.py:139
  146.7 22.2 %collective-permute-done.8.refs_5_ = bf16[1024,512]{1,0:T(8,128)(2,1)} collective-permute-done((bf16[1024,512]{1,0:T(8,128)(2,1)S(1)}, bf16[1024,512]{1,0:T(8,128)(2,1)}, u32[]{:S(2)}, u32[]{:S(2)}) %collective-permute-start.8) | collective-permute-done | bytes 1048608 | tf_op jit(solution)/shard_map/ppermute | solution.py:622
  177.9 6.2 collective-permute-start.11
  190.4 8.7 %collective-permute-done.9.refs_6_ = bf16[1024,512]{1,0:T(8,128)(2,1)S(1)} collective-permute-done((bf16[1024,512]{1,0:T(8,128)(2,1)}, bf16[1024,512]{1,0:T(8,128)(2,1)S(1)}, u32[]{:S(2)}, u32[]{:S(2)}) %collective-permute-start.9) | collective-permute-done | bytes 1048608 | tf_op jit(solution)/shard_map/ppermute | solution.py:622
  206.1 13.1 %delta_outputs.1 = (bf16[8,2,128,256]{3,2,1,0:T(8,128)(2,1)S(1)}, f32[1024,512]{1,0:T(8,128)}, bf16[1024,512]{1,0:T(8,128)(2,1)S(1)}, bf16[1024,2048]{1,0:T(8,128)(2,1)}) custom-call(f32[8,2,128,384]{3,2,1,0:T(8,128)} %get-tuple-element.143.pre_ref, bf16[1024,256]{1,0:T(8,128)(2,1)S(1)} %copy-done.9, f32[1024,512]{1,0:T(8,128)} %get-tuple-element.145.oz_ref, ...), custom_call_target="tpu_custom_call" | custom-call | flops 700000 | bytes 7000 | tf_op jit(solution)/shard_map/delta_outputs/pallas_call | solution.py:139
  250.4 13.1 %collective-permute-done.14 = bf16[128,2048]{1,0:T(8,128)(2,1)S(1)} collective-permute-done((bf16[128,2048]{1,0:T(8,128)(2,1)}, bf16[128,2048]{1,0:T(8,128)(2,1)S(1)}, u32[]{:S(2)}, u32[]{:S(2)}) %collective-permute-start.14) | collective-permute-done | bytes 524320 | tf_op jit(solution)/shard_map/ppermute | solution.py:622
  280.9 6.6 fusion.97
  287.5 7.4 %collective-permute-done.16 = bf16[128,2048]{1,0:T(8,128)(2,1)S(1)} collective-permute-done((bf16[128,2048]{1,0:T(8,128)(2,1)S(1)}, bf16[128,2048]{1,0:T(8,128)(2,1)S(1)}, u32[]{:S(2)}, u32[]{:S(2)}) %collective-permute-start.16) | collective-permute-done | bytes 524320 | tf_op jit(solution)/shard_map/ppermute | solution.py:622
  294.9 14.6 %collective-permute-done.17 = bf16[128,2048]{1,0:T(8,128)(2,1)S(1)} collective-permute-done((bf16[128,2048]{1,0:T(8,128)(2,1)S(1)}, bf16[128,2048]{1,0:T(8,128)(2,1)S(1)}, u32[]{:S(2)}, u32[]{:S(2)}) %collective-permute-start.17) | collective-permute-done | bytes 524320 | tf_op jit(solution)/shard_map/ppermute | solution.py:622
  309.8 13.5 %collective-permute-done.18 = bf16[128,2048]{1,0:T(8,128)(2,1)S(1)} collective-permute-done((bf16[128,2048]{1,0:T(8,128)(2,1)S(1)}, bf16[128,2048]{1,0:T(8,128)(2,1)S(1)}, u32[]{:S(2)}, u32[]{:S(2)}) %collective-permute-start.18) | collective-permute-done | bytes 524320 | tf_op jit(solution)/shard_map/ppermute | solution.py:622
  323.4 6.1 fusion.98
  332.3 6.1 fusion.4
  338.6 12.7 %collective-permute-done.19 = bf16[128,2048]{1,0:T(8,128)(2,1)S(1)} collective-permute-done((bf16[128,2048]{1,0:T(8,128)(2,1)S(1)}, bf16[128,2048]{1,0:T(8,128)(2,1)S(1)}, u32[]{:S(2)}, u32[]{:S(2)}) %collective-permute-start.19) | collective-permute-done | bytes 524320 | tf_op jit(solution)/shard_map/ppermute | solution.py:622
  351.5 11.9 %collective-permute-done.20 = bf16[128,2048]{1,0:T(8,128)(2,1)S(1)} collective-permute-done((bf16[128,2048]{1,0:T(8,128)(2,1)S(1)}, bf16[128,2048]{1,0:T(8,128)(2,1)S(1)}, u32[]{:S(2)}, u32[]{:S(2)}) %collective-permute-start.20) | collective-permute-done | bytes 524320 | tf_op jit(solution)/shard_map/ppermute | solution.py:622
  363.6 11.0 %collective-permute-done.21 = bf16[128,2048]{1,0:T(8,128)(2,1)S(1)} collective-permute-done((bf16[128,2048]{1,0:T(8,128)(2,1)S(1)}, bf16[128,2048]{1,0:T(8,128)(2,1)S(1)}, u32[]{:S(2)}, u32[]{:S(2)}) %collective-permute-start.21) | collective-permute-done | bytes 524320 | tf_op jit(solution)/shard_map/ppermute | solution.py:622
  378.0 6.5 fusion.100
  386.5 7.7 %fusion.99 = bf16[1408,2048]{1,0:T(8,128)(2,1)} fusion(bf16[512,1408]{1,0:T(8,128)(2,1)} %get-tuple-element.166, bf16[512,2048]{1,0:T(8,128)(2,1)} %copy-done.73), kind=kOutput, calls=%fused_computation.259 | convolution fusion | flops 2952790016 | bytes 9306112 | tf_op jit(solution)/shard_map/dot_general | solution.py:690
  394.1 10.6 %fusion.3 = bf16[2048,2816]{1,0:T(8,128)(2,1)} fusion(bf16[512,2048]{1,0:T(8,128)(2,1)} %copy-done.74, bf16[512,1408]{1,0:T(8,128)(2,1)} %copy-done.69, bf16[512,1408]{1,0:T(8,128)(2,1)S(1)} %get-tuple-element.272), kind=kOutput, calls=%fused_computation.30 | convolution fusion | flops 5911347200 | bytes 16515072 | tf_op jit(solution)/shard_map/dot_general | solution.py:690
  404.8 7.1 %all-gather.11.cloned.1.call-done.drows_ref = bf16[1024,2048]{1,0:T(8,128)(2,1)} async-done(((bf16[128,2048]{1,0:T(8,128)(2,1)}), bf16[1024,2048]{1,0:T(8,128)(2,1)}) %all-gather.11.cloned.1.call-update) | async-done | bytes 4194320 | tf_op jit(solution)/shard_map/all_gather | solution.py:671
  411.9 10.5 %delta_states_back.1 = (bf16[1024,512]{1,0:T(8,128)(2,1)S(1)}, bf16[1024,512]{1,0:T(8,128)(2,1)S(1)}, f32[8,2,128,256]{3,2,1,0:T(8,128)S(1)}, bf16[2,128,384]{2,1,0:T(8,128)(2,1)S(1)}, f32[1,256]{1,0:T(1,128)S(1)}) custom-call(bf16[1024,2048]{1,0:T(8,128)(2,1)} %all-gather.11.cloned.1.call-done.drows_ref, ...), custom_call_target="tpu_custom_call" | custom-call | flops 700000 | bytes 7000 | tf_op jit(solution)/shard_map/delta_states_back/pallas_call | solution.py:139
  432.6 7.6 %collective-permute-done.24.refs_2_ = bf16[2,128,256]{2,1,0:T(8,128)(2,1)S(1)} collective-permute-done((bf16[2,128,256]{2,1,0:T(8,128)(2,1)S(1)}, bf16[2,128,256]{2,1,0:T(8,128)(2,1)S(1)}, u32[]{:S(2)}, u32[]{:S(2)}) %collective-permute-start.24) | collective-permute-done | bytes 131104 | tf_op jit(solution)/shard_map/ppermute | solution.py:627
  443.4 19.2 %delta_inputs_back.1 = (bf16[1040,1536]{1,0:T(8,128)(2,1)}, f32[4,1024]{1,0:T(4,128)S(1)}) custom-call(f32[8,2,128,256]{3,2,1,0:T(8,128)} %copy-done.11, bf16[8,2,128,128]{3,2,1,0:T(8,128)(2,1)S(1)} %get-tuple-element.172.m_ref, bf16[8,2,128,256]{3,2,1,0:T(8,128)(2,1)S(1)} %copy-done.13, bf16[1024,512]{1,0:T(8,128)(2,1)} %copy-done.16, ...), custom_call_target="tpu_custom_call" | custom-call | flops 1900000 | bytes 19000 | tf_op jit(solution)/shard_map/delta_inputs_back/pallas_call | solution.py:139
  462.7 7.2 %collective-permute-done.25 = bf16[1024,512]{0,1:T(8,128)(2,1)} collective-permute-done((bf16[1024,512]{0,1:T(8,128)(2,1)S(1)}, bf16[1024,512]{0,1:T(8,128)(2,1)}, u32[]{:S(2)}, u32[]{:S(2)}) %collective-permute-start.25) | collective-permute-done | bytes 1048608 | tf_op jit(solution)/shard_map/ppermute | solution.py:622
  488.7 8.8 %fusion.103 = bf16[1040,2048]{1,0:T(8,128)(2,1)S(1)} fusion(bf16[1040,1536]{1,0:T(8,128)(2,1)} %get-tuple-element.191, bf16[2048,1536]{1,0:T(8,128)(2,1)S(1)} %bitcast.139), kind=kOutput, calls=%fused_computation.263 | convolution fusion | flops 6543114240 | bytes 13746176 | tf_op jit(solution)/shard_map/dot_general | solution.py:690
  508.2 22.9 %collective-permute-done.27 = bf16[2048,512]{0,1:T(8,128)(2,1)S(1)} collective-permute-done((bf16[2048,512]{0,1:T(8,128)(2,1)S(1)}, bf16[2048,512]{0,1:T(8,128)(2,1)S(1)}, u32[]{:S(2)}, u32[]{:S(2)}) %collective-permute-start.27) | collective-permute-done | bytes 2097184 | tf_op jit(solution)/shard_map/ppermute | solution.py:622
  534.8 48.2 %collective-permute-done.26 = bf16[16,2048]{1,0:T(8,128)(2,1)S(1)} collective-permute-done((bf16[16,2048]{1,0:T(8,128)(2,1)S(1)}, bf16[16,2048]{1,0:T(8,128)(2,1)S(1)}, u32[]{:S(2)}, u32[]{:S(2)}) %collective-permute-start.26) | collective-permute-done | bytes 65568 | tf_op jit(solution)/shard_map/ppermute | solution.py:627
  595.6 26.0 %collective-permute-done.29 = bf16[1024,512]{0,1:T(8,128)(2,1)S(1)} collective-permute-done((bf16[1024,512]{0,1:T(8,128)(2,1)S(1)}, bf16[1024,512]{0,1:T(8,128)(2,1)S(1)}, u32[]{:S(2)}, u32[]{:S(2)}) %collective-permute-start.29) | collective-permute-done | bytes 1048608 | tf_op jit(solution)/shard_map/ppermute | solution.py:622
  636.3 6.6 new_moments.1
  673.3 13.0 %new_weights.1 = (f32[2,2048]{1,0:T(2,128)}, f32[2,2048]{1,0:T(2,128)}, f32[2,2048]{1,0:T(2,128)}, f32[1,256]{1,0:T(1,128)}, f32[1,256]{1,0:T(1,128)}, /*index=5...) custom-call(f32[1,4480]{1,0:T(1,128)} %add.313.late_ref, ...), custom_call_target="tpu_custom_call" | custom-call | flops 1000000 | bytes 10000 | tf_op jit(solution)/shard_map/new_weights/pallas_call | solution.py:139
  (480 shorter events, 241.8 us)
Async XLA Ops:
  7.2 44.8 %all-gather.5.cloned.1.call-start = ((), (), s32[]{:S(2)}) async-start(), calls=%async_computation.5 | async-start | bytes 4718592 | tf_op jit(solution)/shard_map/all_gather | solution.py:671
  12.4 132.0 %all-gather.7.cloned.1.call-start = ((), (), s32[]{:S(2)}) async-start(), calls=%async_computation.6 | async-start | bytes 12976128 | tf_op jit(solution)/shard_map/all_gather | solution.py:671
  17.5 28.4 %collective-permute-start = (bf16[512,1024]{1,0:T(8,128)(2,1)S(1)}, bf16[512,1024]{1,0:T(8,128)(2,1)}, u32[]{:S(2)}, u32[]{:S(2)}) collective-permute-start(bf16[512,1024]{1,0:T(8,128)(2,1)S(1)} %get-tuple-element.138), channel_id=1, source_target_pairs={{0,8},{8,16},{16,24},{24,0},{1,9},{9,17},{17,25},{25,1},{2,10},{10... | collective-permute-start | bytes 3145736 | tf_op jit(solution)/shard_map/ppermute | solution.py:622
  52.0 173.1 %all-gather.9.cloned.1.call-start = ((), (), s32[]{:S(2)}) async-start(), calls=%async_computation.7 | async-start | bytes 6488064 | tf_op jit(solution)/shard_map/all_gather | solution.py:671
  61.1 26.5 %collective-permute-start.4 = (bf16[512,1024]{1,0:T(8,128)(2,1)}, bf16[512,1024]{1,0:T(8,128)(2,1)S(1)}, u32[]{:S(2)}, u32[]{:S(2)}) collective-permute-start(bf16[512,1024]{1,0:T(8,128)(2,1)} %collective-permute-done), channel_id=1, source_target_pairs={{0,8},{8,16},{16,24},{24,0},{1,9},{9,17},{17,25},{25,1},{2,10},{10... | collective-permute-start | bytes 3145736 | tf_op jit(solution)/shard_map/ppermute | solution.py:622
  62.6 25.1 %collective-permute-start.5 = (bf16[16,2048]{1,0:T(8,128)(2,1)S(1)}, bf16[16,2048]{1,0:T(8,128)(2,1)S(1)}, u32[]{:S(2)}, u32[]{:S(2)}) collective-permute-start(bf16[16,2048]{1,0:T(8,128)(2,1)S(1)} %slice.188), channel_id=1, source_target_pairs={{0,8},{8,16},{16,24},{1,9},{9,17},{17,25},{2,10},{10,18},{18,26},{... | collective-permute-start | bytes 196616 | tf_op jit(solution)/shard_map/ppermute | solution.py:627
  87.7 25.4 %collective-permute-start.6 = (bf16[512,1024]{1,0:T(8,128)(2,1)S(1)}, bf16[512,1024]{1,0:T(8,128)(2,1)S(1)}, u32[]{:S(2)}, u32[]{:S(2)}) collective-permute-start(bf16[512,1024]{1,0:T(8,128)(2,1)S(1)} %collective-permute-done.4), channel_id=1, source_target_pairs={{0,8},{8,16},{16,24},{24,0},{1,9},{9,17},{17,25},{25,1},{2,10},{10... | collective-permute-start | bytes 3145736 | tf_op jit(solution)/shard_map/ppermute | solution.py:622
  113.0 31.3 %collective-permute-start.7 = (bf16[1024,512]{1,0:T(8,128)(2,1)S(1)}, bf16[1024,512]{1,0:T(8,128)(2,1)S(1)}, u32[]{:S(2)}, u32[]{:S(2)}) collective-permute-start(bf16[1024,512]{1,0:T(8,128)(2,1)S(1)} %pad_maximum_fusion.16.refs_3_), channel_id=1, source_target_pairs={{0,8},{8,16},{16,24},{24,0},{1,9},{9,17},{17,25},{25,1},{2,10},{10... | collective-permute-start | bytes 3145736 | tf_op jit(solution)/shard_map/ppermute | solution.py:622
  144.4 24.6 %collective-permute-start.8 = (bf16[1024,512]{1,0:T(8,128)(2,1)S(1)}, bf16[1024,512]{1,0:T(8,128)(2,1)}, u32[]{:S(2)}, u32[]{:S(2)}) collective-permute-start(bf16[1024,512]{1,0:T(8,128)(2,1)S(1)} %collective-permute-done.7.refs_4_), channel_id=1, source_target_pairs={{0,8},{8,16},{16,24},{24,0},{1,9},{9,17},{17,25},{25,1},{2,10},{10... | collective-permute-start | bytes 3145736 | tf_op jit(solution)/shard_map/ppermute | solution.py:622
  169.0 107.7 %reduce-scatter.6.cloned.1.call-start = ((), (), s32[]{:S(2)}) async-start(), calls=%async_computation.8 | async-start | bytes 4718592 | tf_op jit(solution)/shard_map/reduce_scatter | solution.py:675
  175.1 23.9 %collective-permute-start.9 = (bf16[1024,512]{1,0:T(8,128)(2,1)}, bf16[1024,512]{1,0:T(8,128)(2,1)S(1)}, u32[]{:S(2)}, u32[]{:S(2)}) collective-permute-start(bf16[1024,512]{1,0:T(8,128)(2,1)} %collective-permute-done.8.refs_5_), channel_id=1, source_target_pairs={{0,8},{8,16},{16,24},{24,0},{1,9},{9,17},{17,25},{25,1},{2,10},{10... | collective-permute-start | bytes 3145736 | tf_op jit(solution)/shard_map/ppermute | solution.py:622
  175.9 30.2 %collective-permute-start.10 = (bf16[2,128,384]{2,1,0:T(8,128)(2,1)S(1)}, bf16[2,128,384]{2,1,0:T(8,128)(2,1)S(1)}, u32[]{:S(2)}, u32[]{:S(2)}) collective-permute-start(bf16[2,128,384]{2,1,0:T(8,128)(2,1)S(1)} %get-tuple-element.152.map_ref), channel_id=1, source_target_pairs={{0,8},{8,16},{16,24},{1,9},{9,17},{17,25},{2,10},{10,18},{18,26},{... | collective-permute-start | bytes 589832 | tf_op jit(solution)/shard_map/ppermute | solution.py:627
  177.9 28.3 %collective-permute-start.11 = (bf16[2,128,384]{2,1,0:T(8,128)(2,1)S(1)}, bf16[2,128,384]{2,1,0:T(8,128)(2,1)S(1)}, u32[]{:S(2)}, u32[]{:S(2)}) collective-permute-start(bf16[2,128,384]{2,1,0:T(8,128)(2,1)S(1)} %get-tuple-element.152.map_ref), channel_id=1, source_target_pairs={{0,16},{8,24},{1,17},{9,25},{2,18},{10,26},{3,19},{11,27},{4,20},{... | collective-permute-start | bytes 589832 | tf_op jit(solution)/shard_map/ppermute | solution.py:627
  184.1 22.0 %collective-permute-start.12 = (bf16[2,128,256]{2,1,0:T(8,128)(2,1)S(1)}, bf16[2,128,256]{2,1,0:T(8,128)(2,1)S(1)}, u32[]{:S(2)}, u32[]{:S(2)}) collective-permute-start(bf16[2,128,256]{2,1,0:T(8,128)(2,1)S(1)} %slice.153), channel_id=1, source_target_pairs={{0,24},{1,25},{2,26},{3,27},{4,28},{5,29},{6,30},{7,31}} | collective-permute-start | bytes 393224 | tf_op jit(solution)/shard_map/ppermute | solution.py:627
  221.3 26.1 %collective-permute-start.13 = (bf16[128,2048]{1,0:T(8,128)(2,1)}, bf16[128,2048]{1,0:T(8,128)(2,1)}, u32[]{:S(2)}, u32[]{:S(2)}) collective-permute-start(bf16[128,2048]{1,0:T(8,128)(2,1)} %param.23), channel_id=1, source_target_pairs={{0,8},{8,16},{16,24},{24,0},{1,9},{9,17},{17,25},{25,1},{2,10},{10... | collective-permute-start | bytes 1572872 | tf_op jit(solution)/shard_map/ppermute | solution.py:622
  225.1 186.7 %all-gather.11.cloned.1.call-start = ((), (), s32[]{:S(2)}) async-start(), calls=%async_computation.9 | async-start | bytes 4718592 | tf_op jit(solution)/shard_map/all_gather | solution.py:671
  247.4 16.1 %collective-permute-start.14 = (bf16[128,2048]{1,0:T(8,128)(2,1)}, bf16[128,2048]{1,0:T(8,128)(2,1)S(1)}, u32[]{:S(2)}, u32[]{:S(2)}) collective-permute-start(bf16[128,2048]{1,0:T(8,128)(2,1)} %collective-permute-done.13), channel_id=1, source_target_pairs={{0,8},{8,16},{16,24},{24,0},{1,9},{9,17},{17,25},{25,1},{2,10},{10... | collective-permute-start | bytes 1572872 | tf_op jit(solution)/shard_map/ppermute | solution.py:622
  279.4 15.5 %collective-permute-start.16 = (bf16[128,2048]{1,0:T(8,128)(2,1)S(1)}, bf16[128,2048]{1,0:T(8,128)(2,1)S(1)}, u32[]{:S(2)}, u32[]{:S(2)}) collective-permute-start(bf16[128,2048]{1,0:T(8,128)(2,1)S(1)} %multiply_convert_fusion.3), channel_id=1, source_target_pairs={{0,8},{8,16},{16,24},{24,0},{1,9},{9,17},{17,25},{25,1},{2,10},{10... | collective-permute-start | bytes 1572872 | tf_op jit(solution)/shard_map/ppermute | solution.py:622
  294.9 14.6 %collective-permute-start.17 = (bf16[128,2048]{1,0:T(8,128)(2,1)S(1)}, bf16[128,2048]{1,0:T(8,128)(2,1)S(1)}, u32[]{:S(2)}, u32[]{:S(2)}) collective-permute-start(bf16[128,2048]{1,0:T(8,128)(2,1)S(1)} %collective-permute-done.16), channel_id=1, source_target_pairs={{0,8},{8,16},{16,24},{24,0},{1,9},{9,17},{17,25},{25,1},{2,10},{10... | collective-permute-start | bytes 1572872 | tf_op jit(solution)/shard_map/ppermute | solution.py:622
  309.5 13.8 %collective-permute-start.18 = (bf16[128,2048]{1,0:T(8,128)(2,1)S(1)}, bf16[128,2048]{1,0:T(8,128)(2,1)S(1)}, u32[]{:S(2)}, u32[]{:S(2)}) collective-permute-start(bf16[128,2048]{1,0:T(8,128)(2,1)S(1)} %collective-permute-done.17), channel_id=1, source_target_pairs={{0,8},{8,16},{16,24},{24,0},{1,9},{9,17},{17,25},{25,1},{2,10},{10... | collective-permute-start | bytes 1572872 | tf_op jit(solution)/shard_map/ppermute | solution.py:622
  377.7 96.8 %reduce-scatter.8.cloned.1.call-start = ((), (), s32[]{:S(2)}) async-start(), calls=%async_computation.10 | async-start | bytes 6488064 | tf_op jit(solution)/shard_map/reduce_scatter | solution.py:675
  411.9 173.3 %reduce-scatter.10.cloned.1.call-start = ((), (), s32[]{:S(2)}) async-start(), calls=%async_computation.11 | async-start | bytes 12976128 | tf_op jit(solution)/shard_map/reduce_scatter | solution.py:675
  422.5 17.7 %collective-permute-start.22 = (bf16[2,128,384]{2,1,0:T(8,128)(2,1)S(1)}, bf16[2,128,384]{2,1,0:T(8,128)(2,1)S(1)}, u32[]{:S(2)}, u32[]{:S(2)}) collective-permute-start(bf16[2,128,384]{2,1,0:T(8,128)(2,1)S(1)} %get-tuple-element.184), channel_id=1, source_target_pairs={{8,0},{16,8},{24,16},{9,1},{17,9},{25,17},{10,2},{18,10},{26,18},{... | collective-permute-start | bytes 589832 | tf_op jit(solution)/shard_map/ppermute | solution.py:627
  423.8 19.6 %collective-permute-start.23 = (bf16[2,128,384]{2,1,0:T(8,128)(2,1)S(1)}, bf16[2,128,384]{2,1,0:T(8,128)(2,1)S(1)}, u32[]{:S(2)}, u32[]{:S(2)}) collective-permute-start(bf16[2,128,384]{2,1,0:T(8,128)(2,1)S(1)} %get-tuple-element.184), channel_id=1, source_target_pairs={{16,0},{24,8},{17,1},{25,9},{18,2},{26,10},{19,3},{27,11},{20,4},{... | collective-permute-start | bytes 589832 | tf_op jit(solution)/shard_map/ppermute | solution.py:627
  425.1 15.1 %collective-permute-start.24 = (bf16[2,128,256]{2,1,0:T(8,128)(2,1)S(1)}, bf16[2,128,256]{2,1,0:T(8,128)(2,1)S(1)}, u32[]{:S(2)}, u32[]{:S(2)}) collective-permute-start(bf16[2,128,256]{2,1,0:T(8,128)(2,1)S(1)} %slice.176), channel_id=1, source_target_pairs={{24,0},{25,1},{26,2},{27,3},{28,4},{29,5},{30,6},{31,7}} | collective-permute-start | bytes 393224 | tf_op jit(solution)/shard_map/ppermute | solution.py:627
  443.4 26.5 %collective-permute-start.25 = (bf16[1024,512]{0,1:T(8,128)(2,1)S(1)}, bf16[1024,512]{0,1:T(8,128)(2,1)}, u32[]{:S(2)}, u32[]{:S(2)}) collective-permute-start(bf16[1024,512]{0,1:T(8,128)(2,1)S(1)} %pad_maximum_fusion.17), channel_id=1, source_target_pairs={{0,8},{8,16},{16,24},{24,0},{1,9},{9,17},{17,25},{25,1},{2,10},{10... | collective-permute-start | bytes 3145736 | tf_op jit(solution)/shard_map/ppermute | solution.py:622
  474.6 168.3 %reduce-scatter.12.cloned.1.call-start = ((), (), s32[]{:S(2)}) async-start(), calls=%async_computation.12 | async-start | bytes 4718592 | tf_op jit(solution)/shard_map/reduce_scatter | solution.py:675
  481.7 49.4 %collective-permute-start.27 = (bf16[2048,512]{0,1:T(8,128)(2,1)S(1)}, bf16[2048,512]{0,1:T(8,128)(2,1)S(1)}, u32[]{:S(2)}, u32[]{:S(2)}) collective-permute-start(bf16[2048,512]{0,1:T(8,128)(2,1)S(1)} %pad_maximum_fusion.6), channel_id=1, source_target_pairs={{0,8},{8,16},{16,24},{24,0},{1,9},{9,17},{17,25},{25,1},{2,10},{10... | collective-permute-start | bytes 6291464 | tf_op jit(solution)/shard_map/ppermute | solution.py:622
  533.2 52.0 %collective-permute-start.28 = (bf16[2048,512]{0,1:T(8,128)(2,1)}, bf16[2048,512]{0,1:T(8,128)(2,1)}, u32[]{:S(2)}, u32[]{:S(2)}) collective-permute-start(bf16[2048,512]{0,1:T(8,128)(2,1)} %add_convert_fusion), channel_id=1, source_target_pairs={{0,8},{8,16},{16,24},{24,0},{1,9},{9,17},{17,25},{25,1},{2,10},{10... | collective-permute-start | bytes 6291464 | tf_op jit(solution)/shard_map/ppermute | solution.py:622
  533.2 49.8 %collective-permute-start.26 = (bf16[16,2048]{1,0:T(8,128)(2,1)S(1)}, bf16[16,2048]{1,0:T(8,128)(2,1)S(1)}, u32[]{:S(2)}, u32[]{:S(2)}) collective-permute-start(bf16[16,2048]{1,0:T(8,128)(2,1)S(1)} %slice.211), channel_id=1, source_target_pairs={{8,0},{16,8},{24,16},{9,1},{17,9},{25,17},{10,2},{18,10},{26,18},{... | collective-permute-start | bytes 196616 | tf_op jit(solution)/shard_map/ppermute | solution.py:627
  585.2 102.3 %reduce-scatter.14.cloned.1.call-start = ((), (), s32[]{:S(2)}) async-start(), calls=%async_computation.13 | async-start | bytes 2621440 | tf_op jit(solution)/shard_map/reduce_scatter | solution.py:960
  594.7 27.0 %collective-permute-start.29 = (bf16[1024,512]{0,1:T(8,128)(2,1)S(1)}, bf16[1024,512]{0,1:T(8,128)(2,1)S(1)}, u32[]{:S(2)}, u32[]{:S(2)}) collective-permute-start(bf16[1024,512]{0,1:T(8,128)(2,1)S(1)} %slice.302), channel_id=1, source_target_pairs={{0,8},{8,16},{16,24},{24,0},{1,9},{9,17},{17,25},{25,1},{2,10},{10... | collective-permute-start | bytes 3145736 | tf_op jit(solution)/shard_map/ppermute | solution.py:622
  (114 other events, 1155.2 us)
Sparse Core Ops, SparseCore 0:
  12.5 39.4 all-gather.4
  54.4 67.6 all-gather.6
  169.1 42.5 all-gather.8
  225.3 51.4 reduce-scatter.5
  377.9 33.9 all-gather.10
  415.5 59.0 reduce-scatter.7
  478.1 86.7 reduce-scatter.9
  585.3 49.2 reduce-scatter.11
  643.1 44.2 reduce-scatter.13

commit v3 on v2

--- a/solution.py
+++ b/solution.py
@@ -55,9 +55,6 @@
         xs = [x - mm3(y, x) for x, y in zip(xs, left)]
         size *= 2
     return xs
-
-
-PER = 2
 
 
 def parts_kernel(heads, p_ref, halo_ref, first_ref, taps_ref, gcol_ref, grow_ref,
@@ -122,13 +119,17 @@
     return pl.BlockSpec(shape, lambda c: (0,) * len(shape))
 
 
+PER = 2
+
+
 def by_rows(width, n, back=False):
-    return pl.BlockSpec((CH, width), (lambda c: (n - 1 - c, 0)) if back else (lambda c: (c, 0)))
+    last = n // PER - 1
+    return pl.BlockSpec((PER * CH, width), (lambda c: (last - c, 0)) if back else (lambda c: (c, 0)))
 
 
 def by_chunk(shape, n, back=False):
-    tail = (0,) * len(shape)
-    return pl.BlockSpec((1,) + shape, (lambda c: (n - 1 - c,) + tail) if back else (lambda c: (c,) + tail))
+    tail, last = (0,) * len(shape), n // PER - 1
+    return pl.BlockSpec((PER,) + shape, (lambda c: (last - c,) + tail) if back else (lambda c: (c,) + tail))
 
 
 def sds(shape, dt=F32):
@@ -173,10 +174,10 @@
     )
 
 
-def entering(near, h, dims):
-    state = near[-1][h].astype(F32)
-    for found in near[-2::-1]:
-        state = mm(found[h, :, :DK], state, dims) + found[h, :, DK:].astype(F32)
+def entering(maps, offsets, dims):
+    state = offsets[-1].astype(F32)
+    for found, offset in zip(maps[::-1], offsets[-2::-1]):
+        state = mm(found, state, dims) + offset.astype(F32)
     return state
 
 
@@ -186,14 +187,20 @@
     @pl.when(pl.program_id(0) == 0)
     def _():
         for h in range(heads):
-            start_ref[h] = entering(near, h, ((1,), (0,)))
+            maps = [a[h, :, :DK] for a in near[:-1]]
+            offsets = [a[h, :, DK:] for a in near[:-1]] + [near[-1][h]]
+            start_ref[h] = entering(maps, offsets, ((1,), (0,)))
 
     for h in range(heads):
         at = slice(h * DV, (h + 1) * DV)
-        pre = pre_ref[0, h]
-        s = mm(pre[:, :DK], start_ref[h]) + pre[:, DK:]
-        s_ref[0, h] = s.astype(BF)
-        o = mm(qe_ref[:, h * DK:(h + 1) * DK], s) + oz_ref[:, at]
+        found = []
+        for c in range(PER):
+            rows = slice(c * CH, (c + 1) * CH)
+            pre = pre_ref[c, h]
+            s = mm(pre[:, :DK], start_ref[h]) + pre[:, DK:]
+            s_ref[c, h] = s.astype(BF)
+            found.append(mm(qe_ref[rows, h * DK:(h + 1) * DK], s) + oz_ref[rows, at])
+        o = jnp.concatenate(found, 0)
         o_ref[:, at] = o
         gate = gate_ref[:, at]
         n = o * lax.rsqrt(jnp.mean(o * o, axis=-1, keepdims=True) + 1e-5)
@@ -209,7 +216,7 @@
     wide = by_rows(heads * DV, n)
     size = len(slots) * (slots[0].shape[0] - rows_before)
     return call(
-        functools.partial(outputs_kernel, heads, len(near), rows_before), "delta_outputs", n, 7 * tokens // 1024,
+        functools.partial(outputs_kernel, heads, len(near), rows_before), "delta_outputs", n // PER, 7 * tokens // 1024,
         [by_chunk((heads, DK, DK + DV), n), by_rows(heads * DK, n), wide, wide, whole((1, DV))]
         + [whole(a.shape) for a in (*near, *slots)],
         [(by_chunk((heads, DK, DV), n), sds((n, heads, DK, DV), BF)), (wide, sds((tokens, heads * DV))),
@@ -219,13 +226,12 @@
     )
 
 
-def states_back_kernel(heads, drows_ref, out_ref, o_ref, gate_ref, gain_ref, qe_ref, m_ref, map_ref,
+def states_back_kernel(heads, drows_ref, out_ref, o_ref, gate_ref, gain_ref, qe_ref, m_ref,
                        do_ref, dgate_ref, dc_ref, last_ref, dgain_ref, d_ref):
     @pl.when(pl.program_id(0) == 0)
     def _():
         d_ref[...] = jnp.zeros_like(d_ref)
         dgain_ref[...] = jnp.zeros_like(dgain_ref)
-        last_ref[:, :, :DK] = map_ref[:, :, :DK]
 
     dgated = mm(drows_ref[...], out_ref[...])
     for h in range(heads):
@@ -240,25 +246,27 @@
         dn = dg * gain * act
         do = rstd * (dn - n * jnp.mean(dn * n, axis=-1, keepdims=True))
         do_ref[:, at] = do.astype(BF)
-        dc = mm(qe_ref[:, h * DK:(h + 1) * DK], do, TL)
-        dc_ref[0, h] = dc
-        d = mm(m_ref[0, h], d_ref[h], TL) + dc
+        d = d_ref[h]
+        for c in reversed(range(PER)):
+            rows = slice(c * CH, (c + 1) * CH)
+            dc = mm(qe_ref[rows, h * DK:(h + 1) * DK], do[rows], TL)
+            dc_ref[c, h] = dc
+            d = mm(m_ref[c, h], d, TL) + dc
         d_ref[h] = d
-        last_ref[h, :, DK:] = d.astype(BF)
-
-
-def delta_states_back(drows, out_t, o, gate, gain, qe, m, last, tokens, heads):
+        last_ref[h] = d.astype(BF)
+
+
+def delta_states_back(drows, out_t, o, gate, gain, qe, m, tokens, heads):
     n = tokens // CH
     wide = by_rows(heads * DV, n, True)
     return call(
-        functools.partial(states_back_kernel, heads), "delta_states_back", n, 7 * tokens // 1024,
-        [by_rows(drows.shape[1], n, True), whole(out_t.shape), wide, wide, whole((1, DV)), by_rows(heads * DK, n, True), by_chunk((heads, DK, DK), n, True),
-         whole(last.shape)],
+        functools.partial(states_back_kernel, heads), "delta_states_back", n // PER, 7 * tokens // 1024,
+        [by_rows(drows.shape[1], n, True), whole(out_t.shape), wide, wide, whole((1, DV)), by_rows(heads * DK, n, True), by_chunk((heads, DK, DK), n, True)],
         [(wide, sds((tokens, heads * DV), BF)), (wide, sds((tokens, heads * DV), BF)),
          (by_chunk((heads, DK, DV), n, True), sds((n, heads, DK, DV))),
-         (whole(last.shape), sds(last.shape, BF)), (whole((1, DV)), sds((1, DV)))],
+         (whole((heads, DK, DV)), sds((heads, DK, DV), BF)), (whole((1, DV)), sds((1, DV)))],
         [pltpu.VMEM((heads, DK, DV), F32)],
-        drows, out_t, o, gate, gain, qe, m, last,
+        drows, out_t, o, gate, gain, qe, m,
     )
 
 
@@ -266,6 +274,9 @@
     r = lax.rsqrt(jnp.sum(raw * raw, axis=-1, keepdims=True) + 1e-6)
     n = raw * r
     return (scale * r) * (grad - n * jnp.sum(grad * n, axis=-1, keepdims=True))
+
+
+BACK = 1
 
 
 def conv_back(dact, at, width, sum_ref, in_ref, taps_ref, out_ref, dtaps_ref, rim_ref):
@@ -276,9 +287,9 @@
     ext = jnp.concatenate([dsum, rim_ref[:, where]], 0)
     rim_ref[:, where] = dsum[:8]
     conv_in = in_ref[:, where]
-    dconv = jnp.zeros((CH, width), F32)
+    dconv = jnp.zeros((BACK * CH, width), F32)
     for j in range(KC):
-        moved = ext[3 - j:3 - j + CH]
+        moved = ext[3 - j:3 - j + BACK * CH]
         dconv = dconv + taps_ref[j:j + 1, where] * moved
         dtaps_ref[j:j + 1, where] += jnp.sum(moved * conv_in, axis=0, keepdims=True)
     out_ref[:, where] = dconv.astype(BF)
@@ -304,7 +315,8 @@
     @pl.when(pl.program_id(0) == 0)
     def _():
         for h in range(heads):
-            ds_ref[h] = entering(near, h, ((0,), (0,)))
+            half = (len(near) - 1) // 2
+            ds_ref[h] = entering([a[h] for a in near[:half]], [a[h] for a in near[half:]], ((0,), (0,)))
         for ref in (rim_ref, dtaps_ref):
             ref[...] = jnp.zeros_like(ref)
 
@@ -319,31 +331,35 @@
         dall_ref[:, 2 * heads * DV:] = dgate_ref[...]
         for h in range(heads):
             ds = ds_ref[h]
-            s = s_ref[0, h]
-            do = do_ref[:, h * DV:(h + 1) * DV]
-            q = q_ref[:, h * DK:(h + 1) * DK]
-            k = k_ref[:, h * DK:(h + 1) * DK]
-            gcol = gcol_ref[:, h:h + 1]
-            beta = gcol_ref[:, heads + h:heads + h + 1]
-            grow = grow_ref[0, h:h + 1, :]
-            glast = grow[:, CH - 1:CH]
-            ratio = jnp.exp(jnp.where(rows >= cols, gcol - grow, -1e30))
-            eg = jnp.exp(gcol)
-            el = jnp.exp(glast - gcol)
-            u = uv_ref[:, h * DV:(h + 1) * DV] - mm(w_ref[:, h * DK:(h + 1) * DK], s)
-            du = mm(a_ref[0, h], do, TL) + el * mm(k, ds)
-            da = ratio * mm(do, u, TT)
-            drv = mm(tinv_ref[0, h], du, TL)
-            drk = mm(drv, s, TT)
-            dl = jnp.where(rows > cols, (-beta) * ratio * mm(drv, u, TT), 0.0)
-            dq = eg * mm(do, s, TT) + mm(da, k)
-            dk = el * mm(u, ds, TT) + mm(da, q, TL) - (beta * eg) * drk + mm(dl, k) + mm(dl, k, TL)
-            ds_ref[h] = mm(m_ref[0, h], ds, TL) + dc_ref[0, h]
+            key, val = slice(h * DK, (h + 1) * DK), slice(h * DV, (h + 1) * DV)
+            dqs, dks, dvs = [None] * BACK, [None] * BACK, [None] * BACK
+            for c in reversed(range(BACK)):
+                at = slice(c * CH, (c + 1) * CH)
+                s, do, q, k = s_ref[c, h], do_ref[at, val], q_ref[at, key], k_ref[at, key]
+                gcol, beta = gcol_ref[at, h:h + 1], gcol_ref[at, heads + h:heads + h + 1]
+                grow = grow_ref[c, h:h + 1, :]
+                glast = grow[:, CH - 1:CH]
+                ratio = jnp.exp(jnp.where(rows >= cols, gcol - grow, -1e30))
+                eg = jnp.exp(gcol)
+                el = jnp.exp(glast - gcol)
+                u = uv_ref[at, val] - mm(w_ref[at, key], s)
+                du = mm(a_ref[c, h], do, TL) + el * mm(k, ds)
+                da = ratio * mm(do, u, TT)
+                drv = mm(tinv_ref[c, h], du, TL)
+                dl = jnp.where(rows > cols, (-beta) * ratio * mm(drv, u, TT), 0.0)
+                dqs[c] = eg * mm(do, s, TT) + mm(da, k)
+                dks[c] = (
+                    el * mm(u, ds, TT) + mm(da, q, TL) - (beta * eg) * mm(drv, s, TT) + mm(dl, k) + mm(dl, k, TL)
+                )
+                dvs[c] = beta * drv
+                ds = mm(m_ref[c, h], ds, TL) + dc_ref[c, h]
+            ds_ref[h] = ds
             summed = sum_ref[:, 2 * h * DK:2 * (h + 1) * DK]
             act = summed * sigmoid(summed)
+            dq, dk, dv = (jnp.concatenate(a, 0) for a in (dqs, dks, dvs))
             dact = jnp.concatenate([normed_pull(act[:, :DK], dq, DK ** -0.5), normed_pull(act[:, DK:], dk, 1.0)], 1)
             conv_back(dact, 2 * h * DK, 2 * DK, sum_ref, p_ref, taps_ref, dall_ref, dtaps_ref, rim_ref)
-            conv_back(beta * drv, (heads + h) * DV, DV, sum_ref, p_ref, taps_ref, dall_ref, dtaps_ref, rim_ref)
+            conv_back(dv, (heads + h) * DV, DV, sum_ref, p_ref, taps_ref, dall_ref, dtaps_ref, rim_ref)
 
 
 def delta_inputs_back(near, dc, m, s, do, uv, w, a, tinv, q, k, summed, p, dgate, first, taps, gcol, grow,
@@ -351,19 +367,20 @@
     n = tokens // CH
 
     def at(c):
-        return jnp.maximum(n - 1 - c, 0)
+        return jnp.maximum(n // BACK - 1 - c, 0)
 
     def rows(width):
-        return pl.BlockSpec((CH, width), lambda c: (at(c), 0))
+        return pl.BlockSpec((BACK * CH, width), lambda c: (at(c), 0))
 
     def chunk(shape):
-        return pl.BlockSpec((1,) + shape, lambda c: (at(c),) + (0,) * len(shape))
+        return pl.BlockSpec((BACK,) + shape, lambda c: (at(c),) + (0,) * len(shape))
 
     width = heads * DV
     wide, key = rows(width), rows(heads * DK)
-    out = pl.BlockSpec((CH, 3 * width), lambda c: (jnp.where(c == n, n, n - 1 - c), 0))
+    steps = n // BACK
+    out = pl.BlockSpec((BACK * CH, 3 * width), lambda c: (jnp.where(c == steps, steps, steps - 1 - c), 0))
     return call(
-        functools.partial(inputs_back_kernel, heads), "delta_inputs_back", n + 1, 19 * tokens // 1024,
+        functools.partial(inputs_back_kernel, heads), "delta_inputs_back", steps + 1, 19 * tokens // 1024,
         [chunk((heads, DK, DV)), chunk((heads, DK, DK)), chunk((heads, DK, DV)),
          wide, wide, key, chunk((heads, CH, CH)), chunk((heads, CH, CH)), key, key,
          rows(2 * width), rows(2 * width), wide, whole(first.shape), whole(taps.shape), rows(gcol.shape[1]),
@@ -694,10 +711,9 @@
     return entries * lax.rsqrt(jnp.mean(entries * entries, axis=-1, keepdims=True) + 1e-06) * scale_row
 
 
-def nearby(last, backward):
-    n, sign = lax.axis_size("seq"), -1 if backward else 1
-    near = [ahead(last, sign * k) for k in range(1, n - 1)]
-    return near + [ahead(last[..., DK:], sign * (n - 1))]
+def nearby(last):
+    n = lax.axis_size("seq")
+    return [ahead(last, k) for k in range(1, n - 1)] + [ahead(last[..., DK:], n - 1)]
 
 
 def local(
@@ -768,7 +784,7 @@
     kv_own, gate_own = cast_columns(mixer_in)
     taps_mine = conv_kernel.astype(BF).reshape(KC, heads * conv_kernel.shape[2])
     taps_slots = [taps_mine] + [ring(taps_mine, k) for k in range(1, n)]
-    kv_slots = ring_gather(kv_own, {2: taps_slots[1:]})[:3]
+    kv_slots = ring_gather(kv_own, {1: taps_slots[1:]})[:3]
     rim = ahead(rows_all[tokens - RIM :], 1)
     taps = in_order([t[None] for t in taps_slots]).reshape(n, KC, heads, -1)
     taps = jnp.moveaxis(taps, 0, 2).reshape(KC, heads, CW).astype(F32)
@@ -809,9 +825,10 @@
     shrink = gather_head(after(feed_out.astype(BF), expand, last, go_slots[2]), 1)
     p_gate = projected(row_slots, [a[:in_span] for a in go_slots])
     states, o, gated, mixed = delta_outputs(
-        nearby(last, False), go_slots, pre, qe, oz, p_gate, gain_row, in_span, tokens, heads
-    )
-    grad_slots = ring_gather(out_grad, {1: (go_slots[-1],)})
+        nearby(last), go_slots, pre, qe, oz, p_gate, gain_row, in_span, tokens, heads
+    )
+    maps_after = [ahead(last[..., :DK], -k) for k in range(1, n - 1)]
+    grad_slots = ring_gather(out_grad, {1: (go_slots[-1],), 2: maps_after})
     grad_rows = jnp.concatenate(grad_slots, 0)
     mixed = scatter_head(after(mixed, shrink)).astype(F32)
     mixed = in_order([mixed[:, i * out_span : (i + 1) * out_span] for i in range(n)], 1)
@@ -826,23 +843,34 @@
     feed_held, out_t, w_all, weight_sums, old_moments = lax.optimization_barrier(
         (normed_two.astype(BF), out_t, w_all, weight_sums, old_moments)
     )
-    feed_slots = ring_gather(feed_held, {1: (grad_slots[-1],), 2: (d_hidden,)})
-    feed_rows = jnp.concatenate(feed_slots, 0)
-    gate_up = dot(feed_rows, expand)
-    gate, up = gate_up[:, :hidden_span], gate_up[:, hidden_span:]
-    sig = sigmoid(gate)
-    silu = gate * sig
-    hidden = (silu * up).astype(BF)
-    d_gate_up = jnp.concatenate(
-        [d_hidden * up * (sig * (1.0 + gate * (1.0 - sig))), d_hidden * silu], 1
-    ).astype(BF)
     rows_here = hidden_in.shape[0]
 
     def slot_rows(a, k):
         return a[k * rows_here : (k + 1) * rows_here]
 
-    d_feed_rows = dot(d_gate_up, expand, ((1,), (1,)))
-    d_normed_two, _ = ring_scatter(lambda k: slot_rows(d_feed_rows, k))
+    def fed(rows, first):
+        gate_up = dot(rows, expand)
+        gate, up = gate_up[:, :hidden_span], gate_up[:, hidden_span:]
+        d_here = d_hidden[first * rows_here : first * rows_here + rows.shape[0]]
+        sig = sigmoid(gate)
+        silu = gate * sig
+        d_gate_up = jnp.concatenate([d_here * up * (sig * (1.0 + gate * (1.0 - sig))), d_here * silu], 1).astype(BF)
+        return (silu * up).astype(BF), d_gate_up, dot(d_gate_up, expand, ((1,), (1,)))
+
+    feed_slots = ring_gather(feed_held, {1: (grad_slots[-1],), 2: (d_hidden,)})[:3]
+    hidden_one, d_gate_up_one, d_feed_one = fed(jnp.concatenate(feed_slots[:2], 0), 0)
+    feed_held, d_feed_one = lax.optimization_barrier((feed_slots[2], d_feed_one))
+    feed_slots[2] = feed_held
+    for _ in range(3, n):
+        feed_slots.append(ring(feed_slots[-1]))
+    shrink_sum = ring(slot_rows(d_feed_one, 1).astype(BF))
+    feed_rows = jnp.concatenate(feed_slots, 0)
+    hidden_two, d_gate_up_two, d_feed_two = fed(jnp.concatenate(feed_slots[2:], 0), 2)
+    hidden = jnp.concatenate([hidden_one, hidden_two], 0)
+    d_gate_up = jnp.concatenate([d_gate_up_one, d_gate_up_two], 0)
+    for step in range(2, n):
+        shrink_sum = ring((shrink_sum.astype(F32) + slot_rows(d_feed_two, step - 2)).astype(BF))
+    d_normed_two = shrink_sum.astype(F32) + slot_rows(d_feed_one, 0)
     d_residual_part, d_gain_two = norm_two_pull(d_normed_two)
     d_residual = out_grad.astype(F32) + d_residual_part
     d_residual_low = d_residual.astype(BF)
@@ -857,8 +885,8 @@
     )
     shrink_low = scatter_head(shrink_part, 1)
 
-    do, d_gate, dc, d_last, d_head_gain = delta_states_back(d_rows, out_t, o, p_gate, gain_row, qe, m, last, tokens, heads)
-    near = nearby(d_last, True)
+    do, d_gate, dc, d_last, d_head_gain = delta_states_back(d_rows, out_t, o, p_gate, gain_row, qe, m, tokens, heads)
+    near = maps_after + [ahead(d_last, -k) for k in range(1, n)]
     gate_then, d_rows_then, _ = lax.optimization_barrier((d_gate, d_rows, d_last))
 
     def go_part(k, out=F32, rows=d_rows_then):
@@ -873,21 +901,25 @@
     d_all, d_taps = delta_inputs_back(
         near, dc, m, states, do, uv, w, scores, tinv, q, k, summed, p_kv, d_gate, r_kv, taps, gcol, grow, tokens, heads
     )
-    d_all, sent, go_next, gate_then, d_rows_then, shrink_low = lax.optimization_barrier(
-        (d_all, sent, go_next, gate_then, d_rows_then, shrink_low)
+    d_all, sent, go_next, gate_then, d_rows_then = lax.optimization_barrier(
+        (d_all, sent, go_next, gate_then, d_rows_then)
     )
     more_slots = [jnp.concatenate([a, b], 0) for a, b in zip(row_slots, rim_slots)]
-    expand_low = scatter_head(after(expand_part, shrink_low, d_all))
+
+    def both_dots(k, out):
+        return [dot(more_slots[k], d_all[:, i * width : (i + 1) * width], TL, out) for i in range(2)]
+
+    def both_part(k, out=F32):
+        return jnp.concatenate(both_dots(k, out), 0)
+
+    first_dots = both_dots(1, BF)
+    go = added(sent, go_next).astype(BF)
+    sending = jnp.concatenate([go, *first_dots], 0)
+    d_all_then, sending = lax.optimization_barrier((d_all, sending))
+    sent = ring(sending)
+    d_rows_more = dot(d_all_then, w_all, ((1,), (1,)), BF)
+    expand_low = scatter_head(after(expand_part, shrink_low, sending))
     shrink_g, expand_g = shrink_low.astype(F32), expand_low.astype(F32)
-
-    def both_part(k, out=F32):
-        found = [dot(more_slots[k], d_all[:, i * width : (i + 1) * width], TL, out) for i in range(2)]
-        return jnp.concatenate(found, 0)
-
-    go = added(sent, go_next).astype(BF)
-    both = both_part(1, BF)
-    sent = ring(jnp.concatenate([go, both], 0))
-    d_rows_more = dot(after(d_all, both), w_all, ((1,), (1,)), BF)
     parts = [jnp.concatenate([go_part((step + 1) % n, F32, d_rows_then), both_part(step)], 0) for step in range(2, n)]
     rim_rows, last_part, *parts = lax.optimization_barrier((d_rows_more[tokens:], both_part(0), *parts))
     rim_back = ahead(rim_rows, -1)
@@ -895,13 +927,15 @@
     feed_sums = (jnp.sum(expand_g * expand_g, 0), jnp.sum(shrink_g * shrink_g, 1))
     feed_sums += (jnp.sum(expand_g * expand_g, 1), jnp.sum(shrink_g * shrink_g, 0))
     for step in range(2, n):
-        total = added(sent, parts[step - 2])
+        gone, part = sent, parts[step - 2]
         if step < n - 1:
-            sent = ring(total.astype(BF))
+            sent = ring(added(gone, part).astype(BF))
     d_normed_low = scatter_head(after(d_rows_in, expand_low, sent))
-    go, both = total[: 2 * in_span], total[2 * in_span :].astype(BF)
-    both, *feed_sums = lax.optimization_barrier((both, *feed_sums))
-    both_grad = added(ring(both), last_part)
+    both = added(gone[2 * in_span :], part[2 * in_span :]).astype(BF)
+    last_sent = ring(both)
+    go = added(gone[: 2 * in_span], part[: 2 * in_span])
+    go, last_sent, *feed_sums = lax.optimization_barrier((go, last_sent, *feed_sums))
+    both_grad = added(last_sent, last_part)
     go = lax.optimization_barrier(go)
     out_g = lax.optimization_barrier(go[in_span:].T)
     d_normed = d_normed_low.astype(F32)

time: 704 us -> 683 us (0.970)
  waiting for transfers between devices: 339 us -> 305 us
  matrix products: 84.6 us -> 93.4 us
  starting transfers between devices: 43.9 us -> 51.3 us
    ppermute x22, waiting for transfers between devices: 238 us -> 219 us  [ring(): return lax.ppermute(x, 'seq', [(i, (i + by) % n) for i in range(n)])]
    all_gather x4, waiting for transfers between devices: 13.2 us -> 3.33 us  [gather_head(): return lax.all_gather(x, 'head', axis=axis, tiled=True)]
    dot_general x35 -> x37, matrix products: 84.5 us -> 93.2 us  [dot(): return lax.dot_general(a, b, (dims, ((), ())), preferred_element_type=out)]
    ppermute x8 -> x10, waiting for transfers between devices: 63.9 us -> 56.8 us  [ahead(): lax.ppermute(x, 'seq', [(i, i + by) for i in range(n) if 0 <= i + by < n])]
    ppermute x8 -> x10, starting transfers between devices: 17.4 us -> 22.9 us  [ahead(): lax.ppermute(x, 'seq', [(i, i + by) for i in range(n) if 0 <= i + by < n])]
    unnamed x247 -> x266, local copies, waits for them, and re-layouts: 36.8 us -> 34 us
  transfers between devices with their start and end apart: 49 -> 51, of which waited for: 31 -> 29; matrix products, arithmetic and copies ran while one was open for 22% -> 26% of each run, Pallas kernels for 13% -> 13%
where the time goes in v3:
time: 683 us; the launch traced here: 675 us
  waiting for transfers between devices  305 us (45%)
  matrix products  93.4 us (14%)
  Pallas kernels  88.4 us (13%)
  other arithmetic  60.3 us (9%)
  local copies, waits for them, and re-layouts  60.1 us (9%)
  starting transfers between devices  51.3 us (8%)
  between operations  16.1 us (2%)
    ppermute x22, waiting for transfers between devices, ring(): return lax.ppermute(x, 'seq', [(i, (i + by) % n) for i in range(n)])  219 us
    dot_general x37, matrix products, dot(): return lax.dot_general(a, b, (dims, ((), ())), preferred_element_type=out)  93.2 us
    pallas_call x8, Pallas kernels, call(): pl.pallas_call(kernel, grid=(n,), in_specs=ins, out_specs=[spec for spec,...  81.8 us
    ppermute x10, waiting for transfers between devices, ahead(): lax.ppermute(x, 'seq', [(i, i + by) for i in range(n) if 0 <= i + by < n])  56.8 us
    unnamed x266, local copies, waits for them, and re-layouts  34 us
    ppermute x10, starting transfers between devices, ahead(): lax.ppermute(x, 'seq', [(i, i + by) for i in range(n) if 0 <= i + by < n])  22.9 us
    ppermute x22, starting transfers between devices, ring(): return lax.ppermute(x, 'seq', [(i, (i + by) % n) for i in range(n)])  19.7 us
    ppermute x10, waiting for transfers between devices, total_over(): x = x + lax.ppermute(x, axis, [(i, i ^ step) for i in range(n)])  16 us
  transfers between devices with their start and end apart: 51, of which 29 were waited for; matrix products, arithmetic and copies ran while one was open for 26% of the time, Pallas kernels for 13%

profile of v3, /device:TPU:0, one launch (start us, length us, event | category | flops | bytes accessed | tf_op | source)
XLA Modules:
  0.0 674.9 jit_solution(13719692272704525510)
XLA Ops:
  27.1 22.9 %collective-permute-done.3 = bf16[512,1024]{1,0:T(8,128)(2,1)S(1)} collective-permute-done((bf16[512,1024]{1,0:T(8,128)(2,1)S(1)}, bf16[512,1024]{1,0:T(8,128)(2,1)S(1)}, u32[]{:S(2)}, u32[]{:S(2)}) %collective-permute-start.3) | collective-permute-done | bytes 1048608 | tf_op jit(solution)/shard_map/ppermute | solution.py:639
  69.1 15.5 %collective-permute-done.4 = bf16[512,1024]{1,0:T(8,128)(2,1)S(1)} collective-permute-done((bf16[512,1024]{1,0:T(8,128)(2,1)}, bf16[512,1024]{1,0:T(8,128)(2,1)S(1)}, u32[]{:S(2)}, u32[]{:S(2)}) %collective-permute-start.4) | collective-permute-done | bytes 1048608 | tf_op jit(solution)/shard_map/ppermute | solution.py:639
  87.5 23.4 %collective-permute-done.6 = bf16[512,1024]{1,0:T(8,128)(2,1)S(1)} collective-permute-done((bf16[512,1024]{1,0:T(8,128)(2,1)S(1)}, bf16[512,1024]{1,0:T(8,128)(2,1)S(1)}, u32[]{:S(2)}, u32[]{:S(2)}) %collective-permute-start.6) | collective-permute-done | bytes 1048608 | tf_op jit(solution)/shard_map/ppermute | solution.py:639
  115.1 22.3 %delta_parts.1 = (f32[1024,1024]{1,0:T(8,128)}, bf16[1024,256]{1,0:T(8,128)(2,1)S(1)}, bf16[1024,256]{1,0:T(8,128)(2,1)S(1)}, bf16[8,2,128,128]{3,2,1,0:T(8,128)...) custom-call(f32[1024,1024]{1,0:T(8,128)} %add_add_fusion.p_ref.halo_, ...), custom_call_target="tpu_custom_call" | custom-call | flops 3500000 | bytes 35000 | tf_op jit(solution)/shard_map/delta_parts/pallas_call | solution.py:140
  145.1 22.7 %collective-permute-done.8.refs_5_ = bf16[1024,512]{1,0:T(8,128)(2,1)} collective-permute-done((bf16[1024,512]{1,0:T(8,128)(2,1)S(1)}, bf16[1024,512]{1,0:T(8,128)(2,1)}, u32[]{:S(2)}, u32[]{:S(2)}) %collective-permute-start.8) | collective-permute-done | bytes 1048608 | tf_op jit(solution)/shard_map/ppermute | solution.py:639
  174.0 6.3 collective-permute-start.11
  187.4 10.2 %collective-permute-done.9.refs_6_ = bf16[1024,512]{1,0:T(8,128)(2,1)S(1)} collective-permute-done((bf16[1024,512]{1,0:T(8,128)(2,1)}, bf16[1024,512]{1,0:T(8,128)(2,1)S(1)}, u32[]{:S(2)}, u32[]{:S(2)}) %collective-permute-start.9) | collective-permute-done | bytes 1048608 | tf_op jit(solution)/shard_map/ppermute | solution.py:639
  203.6 9.6 %delta_outputs.1 = (bf16[8,2,128,256]{3,2,1,0:T(8,128)(2,1)S(1)}, f32[1024,512]{1,0:T(8,128)}, bf16[1024,512]{1,0:T(8,128)(2,1)S(1)}, bf16[1024,2048]{1,0:T(8,128)(2,1)}) custom-call(f32[8,2,128,384]{3,2,1,0:T(8,128)} %get-tuple-element.148.pre_ref, bf16[1024,256]{1,0:T(8,128)(2,1)S(1)} %copy-done.9, f32[1024,512]{1,0:T(8,128)} %get-tuple-element.150.oz_ref, ...), custom_call_target="tpu_custom_call" | custom-call | flops 700000 | bytes 7000 | tf_op jit(solution)/shard_map/delta_outputs/pallas_call | solution.py:140
  242.5 11.4 %collective-permute-done.16 = bf16[128,2048]{1,0:T(8,128)(2,1)S(1)} collective-permute-done((bf16[128,2048]{1,0:T(8,128)(2,1)}, bf16[128,2048]{1,0:T(8,128)(2,1)S(1)}, u32[]{:S(2)}, u32[]{:S(2)}) %collective-permute-start.16) | collective-permute-done | bytes 524320 | tf_op jit(solution)/shard_map/ppermute | solution.py:639
  273.8 7.3 %fusion.123 = f32[512,1408]{1,0:T(8,128)S(1)} fusion(bf16[512,2048]{1,0:T(8,128)(2,1)} %constant_dynamic-update-slice_fusion.17, bf16[1408,2048]{1,0:T(8,128)(2,1)} %all-gather.9.cloned.1.call-done), kind=kOutput, calls=%fused_computation.284 | convolution fusion | flops 2952790016 | bytes 10747904 | tf_op jit(solution)/shard_map/dot_general | solution.py:707
  281.0 6.7 collective-permute-done.18
  292.2 6.3 fusion.10
  298.6 8.3 %collective-permute-done.19 = bf16[128,2048]{1,0:T(8,128)(2,1)S(1)} collective-permute-done((bf16[128,2048]{1,0:T(8,128)(2,1)S(1)}, bf16[128,2048]{1,0:T(8,128)(2,1)S(1)}, u32[]{:S(2)}, u32[]{:S(2)}) %collective-permute-start.19) | collective-permute-done | bytes 524320 | tf_op jit(solution)/shard_map/ppermute | solution.py:639
  307.0 16.5 %collective-permute-done.20 = bf16[128,2048]{1,0:T(8,128)(2,1)S(1)} collective-permute-done((bf16[128,2048]{1,0:T(8,128)(2,1)S(1)}, bf16[128,2048]{1,0:T(8,128)(2,1)S(1)}, u32[]{:S(2)}, u32[]{:S(2)}) %collective-permute-start.20) | collective-permute-done | bytes 524320 | tf_op jit(solution)/shard_map/ppermute | solution.py:639
  324.3 6.3 fusion.35
  332.3 6.6 fusion.14
  339.1 13.4 %collective-permute-done.22 = bf16[128,2048]{1,0:T(8,128)(2,1)S(1)} collective-permute-done((bf16[128,2048]{1,0:T(8,128)(2,1)S(1)}, bf16[128,2048]{1,0:T(8,128)(2,1)S(1)}, u32[]{:S(2)}, u32[]{:S(2)}) %collective-permute-start.22) | collective-permute-done | bytes 524320 | tf_op jit(solution)/shard_map/ppermute | solution.py:639
  352.6 11.0 %collective-permute-done.23 = bf16[128,2048]{1,0:T(8,128)(2,1)S(1)} collective-permute-done((bf16[128,2048]{1,0:T(8,128)(2,1)S(1)}, bf16[128,2048]{1,0:T(8,128)(2,1)S(1)}, u32[]{:S(2)}, u32[]{:S(2)}) %collective-permute-start.23) | collective-permute-done | bytes 524320 | tf_op jit(solution)/shard_map/ppermute | solution.py:639
  371.5 6.4 fusion.125
  379.8 7.7 %fusion.124 = bf16[1408,2048]{1,0:T(8,128)(2,1)} fusion(bf16[512,1408]{1,0:T(8,128)(2,1)} %copy-done.70, bf16[512,2048]{1,0:T(8,128)(2,1)} %constant_dynamic-update-slice_fusion.17), kind=kOutput, calls=%fused_computation.285 | convolution fusion | flops 2952790016 | bytes 9306112 | tf_op jit(solution)/shard_map/dot_general | solution.py:707
  387.6 10.8 %fusion = bf16[2048,2816]{1,0:T(8,128)(2,1)} fusion(bf16[512,2048]{1,0:T(8,128)(2,1)} %pad_maximum_fusion.3, bf16[256,1408]{1,0:T(8,128)(2,1)} %copy-done.75, bf16[256,1408]{1,0:T(8,128)(2,1)} %copy-done.74, bf16[256,1408]{1,0:T(8,128)(2,1)} %copy-done.73, bf16[256,1408]{1,0:T(8,128)(2,1)S(1)} %copy-done.72), kind=kOutput, calls=%fused_computation.6 | convolution fusion | flops 5917114368 | bytes 16515072 | tf_op jit(solution)/shard_map/dot_general | solution.py:707
  400.9 8.7 %delta_states_back.1 = (bf16[1024,512]{1,0:T(8,128)(2,1)S(1)}, bf16[1024,512]{1,0:T(8,128)(2,1)S(1)}, f32[8,2,128,256]{3,2,1,0:T(8,128)S(1)}, bf16[2,128,256]{2,1,0:T(8,128)(2,1)S(1)}, f32[1,256]{1,0:T(1,128)S(1)}) custom-call(bf16[1024,2048]{1,0:T(8,128)(2,1)} %all-gather.11.cloned.1.call-done.drows_ref, ...), custom_call_target="tpu_custom_call" | custom-call | flops 700000 | bytes 7000 | tf_op jit(solution)/shard_map/delta_states_back/pallas_call | solution.py:140
  418.4 8.2 %collective-permute-done.25.refs_3_ = bf16[2,128,256]{2,1,0:T(8,128)(2,1)S(1)} collective-permute-done((bf16[2,128,256]{2,1,0:T(8,128)(2,1)S(1)}, bf16[2,128,256]{2,1,0:T(8,128)(2,1)S(1)}, u32[]{:S(2)}, u32[]{:S(2)}) %collective-permute-start.25) | collective-permute-done | bytes 131104 | tf_op jit(solution)/shard_map/ppermute | solution.py:644
  426.6 20.3 %delta_inputs_back.1 = (bf16[1040,1536]{1,0:T(8,128)(2,1)}, f32[4,1024]{1,0:T(4,128)S(1)}) custom-call(f32[8,2,128,256]{3,2,1,0:T(8,128)} %copy-done.11, bf16[8,2,128,128]{3,2,1,0:T(8,128)(2,1)S(1)} %get-tuple-element.180.m_ref, bf16[8,2,128,256]{3,2,1,0:T(8,128)(2,1)S(1)} %copy-done.13, bf16[1024,512]{1,0:T(8,128)(2,1)} %copy-done.16, ...), custom_call_target="tpu_custom_call" | custom-call | flops 1900000 | bytes 19000 | tf_op jit(solution)/shard_map/delta_inputs_back/pallas_call | solution.py:140
  446.8 6.0 collective-permute-done.27
  471.0 7.1 %fusion.128 = bf16[1040,2048]{1,0:T(8,128)(2,1)S(1)} fusion(bf16[1040,1536]{1,0:T(8,128)(2,1)S(1)} %copy-done.102, bf16[2048,1536]{1,0:T(8,128)(2,1)S(1)} %bitcast.140), kind=kOutput, calls=%fused_computation.289 | convolution fusion | flops 6543114240 | bytes 13746176 | tf_op jit(solution)/shard_map/dot_general | solution.py:707
  489.3 24.2 %collective-permute-done.29 = bf16[2048,512]{0,1:T(8,128)(2,1)S(1)} collective-permute-done((bf16[2048,512]{0,1:T(8,128)(2,1)}, bf16[2048,512]{0,1:T(8,128)(2,1)S(1)}, u32[]{:S(2)}, u32[]{:S(2)}) %collective-permute-start.29) | collective-permute-done | bytes 2097184 | tf_op jit(solution)/shard_map/ppermute | solution.py:639
  517.1 48.2 %collective-permute-done.28 = bf16[16,2048]{1,0:T(8,128)(2,1)S(1)} collective-permute-done((bf16[16,2048]{1,0:T(8,128)(2,1)S(1)}, bf16[16,2048]{1,0:T(8,128)(2,1)S(1)}, u32[]{:S(2)}, u32[]{:S(2)}) %collective-permute-start.28) | collective-permute-done | bytes 65568 | tf_op jit(solution)/shard_map/ppermute | solution.py:644
  574.6 23.8 %collective-permute-done.31 = bf16[1024,512]{0,1:T(8,128)(2,1)S(1)} collective-permute-done((bf16[1024,512]{0,1:T(8,128)(2,1)S(1)}, bf16[1024,512]{0,1:T(8,128)(2,1)S(1)}, u32[]{:S(2)}, u32[]{:S(2)}) %collective-permute-start.31) | collective-permute-done | bytes 1048608 | tf_op jit(solution)/shard_map/ppermute | solution.py:639
  615.2 6.7 new_moments.1
  640.3 4.9 collective-permute-done.40
  652.1 13.0 %new_weights.1 = (f32[2,2048]{1,0:T(2,128)}, f32[2,2048]{1,0:T(2,128)}, f32[2,2048]{1,0:T(2,128)}, f32[1,256]{1,0:T(1,128)}, f32[1,256]{1,0:T(1,128)}, /*index=5...) custom-call(f32[1,4480]{1,0:T(1,128)} %add.325.late_ref, ...), custom_call_target="tpu_custom_call" | custom-call | flops 1000000 | bytes 10000 | tf_op jit(solution)/shard_map/new_weights/pallas_call | solution.py:140
  (505 shorter events, 236.3 us)
Async XLA Ops:
  7.2 43.7 %all-gather.5.cloned.1.call-start = ((), (), s32[]{:S(2)}) async-start(), calls=%async_computation.5 | async-start | bytes 4718592 | tf_op jit(solution)/shard_map/all_gather | solution.py:688
  11.4 130.9 %all-gather.7.cloned.1.call-start = ((), (), s32[]{:S(2)}) async-start(), calls=%async_computation.6 | async-start | bytes 12976128 | tf_op jit(solution)/shard_map/all_gather | solution.py:688
  24.2 25.8 %collective-permute-start.3 = (bf16[512,1024]{1,0:T(8,128)(2,1)S(1)}, bf16[512,1024]{1,0:T(8,128)(2,1)S(1)}, u32[]{:S(2)}, u32[]{:S(2)}) collective-permute-start(bf16[512,1024]{1,0:T(8,128)(2,1)S(1)} %get-tuple-element.144), channel_id=1, source_target_pairs={{0,8},{8,16},{16,24},{24,0},{1,9},{9,17},{17,25},{25,1},{2,10},{10... | collective-permute-start | bytes 3145736 | tf_op jit(solution)/shard_map/ppermute | solution.py:639
  51.0 167.1 %all-gather.9.cloned.1.call-start = ((), (), s32[]{:S(2)}) async-start(), calls=%async_computation.7 | async-start | bytes 6488064 | tf_op jit(solution)/shard_map/all_gather | solution.py:688
  57.2 27.4 %collective-permute-start.4 = (bf16[512,1024]{1,0:T(8,128)(2,1)}, bf16[512,1024]{1,0:T(8,128)(2,1)S(1)}, u32[]{:S(2)}, u32[]{:S(2)}) collective-permute-start(bf16[512,1024]{1,0:T(8,128)(2,1)} %copy-done.39), channel_id=1, source_target_pairs={{0,8},{8,16},{16,24},{24,0},{1,9},{9,17},{17,25},{25,1},{2,10},{10... | collective-permute-start | bytes 3145736 | tf_op jit(solution)/shard_map/ppermute | solution.py:639
  59.6 25.0 %collective-permute-start.5 = (bf16[16,2048]{1,0:T(8,128)(2,1)S(1)}, bf16[16,2048]{1,0:T(8,128)(2,1)S(1)}, u32[]{:S(2)}, u32[]{:S(2)}) collective-permute-start(bf16[16,2048]{1,0:T(8,128)(2,1)S(1)} %slice.212), channel_id=1, source_target_pairs={{0,8},{8,16},{16,24},{1,9},{9,17},{17,25},{2,10},{10,18},{18,26},{... | collective-permute-start | bytes 196616 | tf_op jit(solution)/shard_map/ppermute | solution.py:644
  84.6 26.3 %collective-permute-start.6 = (bf16[512,1024]{1,0:T(8,128)(2,1)S(1)}, bf16[512,1024]{1,0:T(8,128)(2,1)S(1)}, u32[]{:S(2)}, u32[]{:S(2)}) collective-permute-start(bf16[512,1024]{1,0:T(8,128)(2,1)S(1)} %collective-permute-done.4), channel_id=1, source_target_pairs={{0,8},{8,16},{16,24},{24,0},{1,9},{9,17},{17,25},{25,1},{2,10},{10... | collective-permute-start | bytes 3145736 | tf_op jit(solution)/shard_map/ppermute | solution.py:639
  110.9 31.3 %collective-permute-start.7 = (bf16[1024,512]{1,0:T(8,128)(2,1)S(1)}, bf16[1024,512]{1,0:T(8,128)(2,1)S(1)}, u32[]{:S(2)}, u32[]{:S(2)}) collective-permute-start(bf16[1024,512]{1,0:T(8,128)(2,1)S(1)} %pad_maximum_fusion.15.refs_3_), channel_id=1, source_target_pairs={{0,8},{8,16},{16,24},{24,0},{1,9},{9,17},{17,25},{25,1},{2,10},{10... | collective-permute-start | bytes 3145736 | tf_op jit(solution)/shard_map/ppermute | solution.py:639
  142.3 25.6 %collective-permute-start.8 = (bf16[1024,512]{1,0:T(8,128)(2,1)S(1)}, bf16[1024,512]{1,0:T(8,128)(2,1)}, u32[]{:S(2)}, u32[]{:S(2)}) collective-permute-start(bf16[1024,512]{1,0:T(8,128)(2,1)S(1)} %collective-permute-done.7.refs_4_), channel_id=1, source_target_pairs={{0,8},{8,16},{16,24},{24,0},{1,9},{9,17},{17,25},{25,1},{2,10},{10... | collective-permute-start | bytes 3145736 | tf_op jit(solution)/shard_map/ppermute | solution.py:639
  167.8 101.8 %reduce-scatter.6.cloned.1.call-start = ((), (), s32[]{:S(2)}) async-start(), calls=%async_computation.8 | async-start | bytes 4718592 | tf_op jit(solution)/shard_map/reduce_scatter | solution.py:692
  171.4 26.2 %collective-permute-start.9 = (bf16[1024,512]{1,0:T(8,128)(2,1)}, bf16[1024,512]{1,0:T(8,128)(2,1)S(1)}, u32[]{:S(2)}, u32[]{:S(2)}) collective-permute-start(bf16[1024,512]{1,0:T(8,128)(2,1)} %collective-permute-done.8.refs_5_), channel_id=1, source_target_pairs={{0,8},{8,16},{16,24},{24,0},{1,9},{9,17},{17,25},{25,1},{2,10},{10... | collective-permute-start | bytes 3145736 | tf_op jit(solution)/shard_map/ppermute | solution.py:639
  172.2 31.4 %collective-permute-start.10 = (bf16[2,128,384]{2,1,0:T(8,128)(2,1)S(1)}, bf16[2,128,384]{2,1,0:T(8,128)(2,1)S(1)}, u32[]{:S(2)}, u32[]{:S(2)}) collective-permute-start(bf16[2,128,384]{2,1,0:T(8,128)(2,1)S(1)} %get-tuple-element.157), channel_id=1, source_target_pairs={{0,8},{8,16},{16,24},{1,9},{9,17},{17,25},{2,10},{10,18},{18,26},{... | collective-permute-start | bytes 589832 | tf_op jit(solution)/shard_map/ppermute | solution.py:644
  174.0 29.6 %collective-permute-start.11 = (bf16[2,128,384]{2,1,0:T(8,128)(2,1)S(1)}, bf16[2,128,384]{2,1,0:T(8,128)(2,1)S(1)}, u32[]{:S(2)}, u32[]{:S(2)}) collective-permute-start(bf16[2,128,384]{2,1,0:T(8,128)(2,1)S(1)} %get-tuple-element.157), channel_id=1, source_target_pairs={{0,16},{8,24},{1,17},{9,25},{2,18},{10,26},{3,19},{11,27},{4,20},{... | collective-permute-start | bytes 589832 | tf_op jit(solution)/shard_map/ppermute | solution.py:644
  181.0 58.3 %collective-permute-start.14 = (bf16[2,128,128]{2,1,0:T(8,128)(2,1)}, bf16[2,128,128]{2,1,0:T(8,128)(2,1)S(1)}, u32[]{:S(2)}, u32[]{:S(2)}) collective-permute-start(bf16[2,128,128]{2,1,0:T(8,128)(2,1)} %slice.184), channel_id=1, source_target_pairs={{8,0},{16,8},{24,16},{9,1},{17,9},{25,17},{10,2},{18,10},{26,18},{... | collective-permute-start | bytes 196616 | tf_op jit(solution)/shard_map/ppermute | solution.py:644
  182.3 57.0 %collective-permute-start.15 = (bf16[2,128,128]{2,1,0:T(8,128)(2,1)}, bf16[2,128,128]{2,1,0:T(8,128)(2,1)}, u32[]{:S(2)}, u32[]{:S(2)}) collective-permute-start(bf16[2,128,128]{2,1,0:T(8,128)(2,1)} %slice.184), channel_id=1, source_target_pairs={{16,0},{24,8},{17,1},{25,9},{18,2},{26,10},{19,3},{27,11},{20,4},{... | collective-permute-start | bytes 196616 | tf_op jit(solution)/shard_map/ppermute | solution.py:644
  215.2 24.2 %collective-permute-start.13 = (bf16[128,2048]{1,0:T(8,128)(2,1)}, bf16[128,2048]{1,0:T(8,128)(2,1)}, u32[]{:S(2)}, u32[]{:S(2)}) collective-permute-start(bf16[128,2048]{1,0:T(8,128)(2,1)} %param.23), channel_id=1, source_target_pairs={{0,8},{8,16},{16,24},{24,0},{1,9},{9,17},{17,25},{25,1},{2,10},{10... | collective-permute-start | bytes 1572872 | tf_op jit(solution)/shard_map/ppermute | solution.py:639
  218.1 182.7 %all-gather.11.cloned.1.call-start = ((), (), s32[]{:S(2)}) async-start(), calls=%async_computation.9 | async-start | bytes 4718592 | tf_op jit(solution)/shard_map/all_gather | solution.py:688
  239.3 14.6 %collective-permute-start.16 = (bf16[128,2048]{1,0:T(8,128)(2,1)}, bf16[128,2048]{1,0:T(8,128)(2,1)S(1)}, u32[]{:S(2)}, u32[]{:S(2)}) collective-permute-start(bf16[128,2048]{1,0:T(8,128)(2,1)} %collective-permute-done.13), channel_id=1, source_target_pairs={{0,8},{8,16},{16,24},{24,0},{1,9},{9,17},{17,25},{25,1},{2,10},{10... | collective-permute-start | bytes 1572872 | tf_op jit(solution)/shard_map/ppermute | solution.py:639
  272.3 15.5 %collective-permute-start.18 = (bf16[128,2048]{1,0:T(8,128)(2,1)S(1)}, bf16[128,2048]{1,0:T(8,128)(2,1)S(1)}, u32[]{:S(2)}, u32[]{:S(2)}) collective-permute-start(bf16[128,2048]{1,0:T(8,128)(2,1)S(1)} %multiply_convert_fusion.6), channel_id=1, source_target_pairs={{0,8},{8,16},{16,24},{24,0},{1,9},{9,17},{17,25},{25,1},{2,10},{10... | collective-permute-start | bytes 1572872 | tf_op jit(solution)/shard_map/ppermute | solution.py:639
  292.0 14.8 %collective-permute-start.19 = (bf16[128,2048]{1,0:T(8,128)(2,1)S(1)}, bf16[128,2048]{1,0:T(8,128)(2,1)S(1)}, u32[]{:S(2)}, u32[]{:S(2)}) collective-permute-start(bf16[128,2048]{1,0:T(8,128)(2,1)S(1)} %collective-permute-done.18), channel_id=1, source_target_pairs={{0,8},{8,16},{16,24},{24,0},{1,9},{9,17},{17,25},{25,1},{2,10},{10... | collective-permute-start | bytes 1572872 | tf_op jit(solution)/shard_map/ppermute | solution.py:639
  306.8 16.7 %collective-permute-start.20 = (bf16[128,2048]{1,0:T(8,128)(2,1)S(1)}, bf16[128,2048]{1,0:T(8,128)(2,1)S(1)}, u32[]{:S(2)}, u32[]{:S(2)}) collective-permute-start(bf16[128,2048]{1,0:T(8,128)(2,1)S(1)} %collective-permute-done.19), channel_id=1, source_target_pairs={{0,8},{8,16},{16,24},{24,0},{1,9},{9,17},{17,25},{25,1},{2,10},{10... | collective-permute-start | bytes 1572872 | tf_op jit(solution)/shard_map/ppermute | solution.py:639
  306.9 32.0 %collective-permute-start.21 = (bf16[128,2048]{1,0:T(8,128)(2,1)S(1)}, bf16[128,2048]{1,0:T(8,128)(2,1)S(1)}, u32[]{:S(2)}, u32[]{:S(2)}) collective-permute-start(bf16[128,2048]{1,0:T(8,128)(2,1)S(1)} %slice.344), channel_id=1, source_target_pairs={{0,8},{8,16},{16,24},{24,0},{1,9},{9,17},{17,25},{25,1},{2,10},{10... | collective-permute-start | bytes 1572872 | tf_op jit(solution)/shard_map/ppermute | solution.py:639
  366.7 96.9 %reduce-scatter.8.cloned.1.call-start = ((), (), s32[]{:S(2)}) async-start(), calls=%async_computation.10 | async-start | bytes 6488064 | tf_op jit(solution)/shard_map/reduce_scatter | solution.py:692
  400.8 166.8 %reduce-scatter.10.cloned.1.call-start = ((), (), s32[]{:S(2)}) async-start(), calls=%async_computation.11 | async-start | bytes 12976128 | tf_op jit(solution)/shard_map/reduce_scatter | solution.py:692
  410.9 15.6 %collective-permute-start.25 = (bf16[2,128,256]{2,1,0:T(8,128)(2,1)S(1)}, bf16[2,128,256]{2,1,0:T(8,128)(2,1)S(1)}, u32[]{:S(2)}, u32[]{:S(2)}) collective-permute-start(bf16[2,128,256]{2,1,0:T(8,128)(2,1)S(1)} %get-tuple-element.192), channel_id=1, source_target_pairs={{16,0},{24,8},{17,1},{25,9},{18,2},{26,10},{19,3},{27,11},{20,4},{... | collective-permute-start | bytes 393224 | tf_op jit(solution)/shard_map/ppermute | solution.py:644
  426.5 26.3 %collective-permute-start.27 = (bf16[1024,512]{0,1:T(8,128)(2,1)S(1)}, bf16[1024,512]{0,1:T(8,128)(2,1)S(1)}, u32[]{:S(2)}, u32[]{:S(2)}) collective-permute-start(bf16[1024,512]{0,1:T(8,128)(2,1)S(1)} %pad_maximum_fusion.16), channel_id=1, source_target_pairs={{0,8},{8,16},{16,24},{24,0},{1,9},{9,17},{17,25},{25,1},{2,10},{10... | collective-permute-start | bytes 3145736 | tf_op jit(solution)/shard_map/ppermute | solution.py:639
  463.6 158.3 %reduce-scatter.12.cloned.1.call-start = ((), (), s32[]{:S(2)}) async-start(), calls=%async_computation.12 | async-start | bytes 4718592 | tf_op jit(solution)/shard_map/reduce_scatter | solution.py:692
  463.7 49.8 %collective-permute-start.29 = (bf16[2048,512]{0,1:T(8,128)(2,1)}, bf16[2048,512]{0,1:T(8,128)(2,1)S(1)}, u32[]{:S(2)}, u32[]{:S(2)}) collective-permute-start(bf16[2048,512]{0,1:T(8,128)(2,1)} %pad_maximum_fusion.5), channel_id=1, source_target_pairs={{0,8},{8,16},{16,24},{24,0},{1,9},{9,17},{17,25},{25,1},{2,10},{10... | collective-permute-start | bytes 6291464 | tf_op jit(solution)/shard_map/ppermute | solution.py:639
  515.5 52.0 %collective-permute-start.30 = (bf16[2048,512]{0,1:T(8,128)(2,1)}, bf16[2048,512]{0,1:T(8,128)(2,1)}, u32[]{:S(2)}, u32[]{:S(2)}) collective-permute-start(bf16[2048,512]{0,1:T(8,128)(2,1)} %add_convert_fusion), channel_id=1, source_target_pairs={{0,8},{8,16},{16,24},{24,0},{1,9},{9,17},{17,25},{25,1},{2,10},{10... | collective-permute-start | bytes 6291464 | tf_op jit(solution)/shard_map/ppermute | solution.py:639
  515.5 49.8 %collective-permute-start.28 = (bf16[16,2048]{1,0:T(8,128)(2,1)S(1)}, bf16[16,2048]{1,0:T(8,128)(2,1)S(1)}, u32[]{:S(2)}, u32[]{:S(2)}) collective-permute-start(bf16[16,2048]{1,0:T(8,128)(2,1)S(1)} %slice.238), channel_id=1, source_target_pairs={{8,0},{16,8},{24,16},{9,1},{17,9},{25,17},{10,2},{18,10},{26,18},{... | collective-permute-start | bytes 196616 | tf_op jit(solution)/shard_map/ppermute | solution.py:644
  567.6 98.6 %reduce-scatter.14.cloned.1.call-start = ((), (), s32[]{:S(2)}) async-start(), calls=%async_computation.13 | async-start | bytes 2621440 | tf_op jit(solution)/shard_map/reduce_scatter | solution.py:994
  571.4 26.9 %collective-permute-start.31 = (bf16[1024,512]{0,1:T(8,128)(2,1)S(1)}, bf16[1024,512]{0,1:T(8,128)(2,1)S(1)}, u32[]{:S(2)}, u32[]{:S(2)}) collective-permute-start(bf16[1024,512]{0,1:T(8,128)(2,1)S(1)} %get-tuple-element.282), channel_id=1, source_target_pairs={{0,8},{8,16},{16,24},{24,0},{1,9},{9,17},{17,25},{25,1},{2,10},{10... | collective-permute-start | bytes 3145736 | tf_op jit(solution)/shard_map/ppermute | solution.py:639
  (127 other events, 1176.3 us)
Sparse Core Ops, SparseCore 0:
  11.5 39.4 all-gather.4
  53.4 67.6 all-gather.6
  168.0 42.4 all-gather.8
  218.2 51.3 reduce-scatter.5
  366.8 33.9 all-gather.10
  404.5 59.0 reduce-scatter.7
  467.1 86.7 reduce-scatter.9
  567.7 49.0 reduce-scatter.11
  622.1 44.1 reduce-scatter.13

commit v4 on v3

--- a/solution.py
+++ b/solution.py
@@ -71,9 +71,9 @@
     def convolved(at, size):
         before = jnp.where(pl.program_id(0) == 0, first_ref[RIM - 8:, at:at + size], halo_ref[:, at:at + size])
         ext = jnp.concatenate([before, p_ref[:, at:at + size]], 0)
-        summed = taps_ref[0:1, at:at + size] * ext[5:5 + PER * CH]
+        summed = taps_ref[0:1, at:at + size] * ext[5:5 + FRONT * CH]
         for j in range(1, KC):
-            summed = summed + taps_ref[j:j + 1, at:at + size] * ext[5 + j:5 + j + PER * CH]
+            summed = summed + taps_ref[j:j + 1, at:at + size] * ext[5 + j:5 + j + FRONT * CH]
         sum_ref[:, at:at + size] = summed
         return summed * sigmoid(summed)
 
@@ -81,7 +81,7 @@
     for h in range(heads):
         act = convolved(2 * h * DK, 2 * DK)
         values = convolved(width + h * DV, DV)
-        for c in range(PER):
+        for c in range(FRONT):
             at = slice(c * CH, (c + 1) * CH)
             q, k = act[at, :DK], act[at, DK:]
             q = q * (lax.rsqrt(jnp.sum(q * q, axis=-1, keepdims=True) + 1e-6) * DK ** -0.5)
@@ -120,6 +120,7 @@
 
 
 PER = 2
+FRONT = 4
 
 
 def by_rows(width, n, back=False):
@@ -153,18 +154,18 @@
 
 
 def delta_parts(p, first, taps, gcol, grow, tokens, heads):
-    n, span, width = tokens // CH, PER * CH, heads * DV
+    n, span, width = tokens // CH, FRONT * CH, heads * DV
 
     def rows(size, dt=F32):
         return pl.BlockSpec((span, size), lambda c: (c, 0)), sds((tokens, size), dt)
 
     def chunk(shape, dt=F32):
         tail = (0,) * len(shape)
-        return pl.BlockSpec((PER,) + shape, lambda c: (c,) + tail), sds((n,) + shape, dt)
+        return pl.BlockSpec((FRONT,) + shape, lambda c: (c,) + tail), sds((n,) + shape, dt)
 
     halo = pl.BlockSpec((8, 2 * width), lambda c: (jnp.maximum(c * (span // 8) - 1, 0), 0))
     return call(
-        functools.partial(parts_kernel, heads), "delta_parts", n // PER, 35 * tokens // 1024,
+        functools.partial(parts_kernel, heads), "delta_parts", n // FRONT, 35 * tokens // 1024,
         [rows(2 * width)[0], halo, whole(first.shape), whole(taps.shape), rows(gcol.shape[1])[0], chunk(grow.shape[1:])[0]],
         [rows(2 * width), rows(heads * DK, BF), rows(heads * DK, BF), chunk((heads, CH, CH), BF), chunk((heads, CH, CH), BF),
          rows(heads * DK, BF), rows(width), rows(heads * DK, BF), rows(width), chunk((heads, DK, DK), BF),
@@ -421,7 +422,7 @@
         return new, lax.rsqrt(new)
 
     parts = {
-        "in": (both_ref[:span], both_ref[span:], go_ref[:span]),
+        "in": (both_ref[:span], both_ref[span:], go_ref[...]),
         "out": (outg_ref[...],),
         "expand": (ex_ref[...].astype(F32),),
         "shrink": (sh_ref[...].astype(F32),),
@@ -516,25 +517,6 @@
     )
 
 
-def joined_kernel(heads, keys_ref, vals_ref, gate_ref, out_ref):
-    for h in range(heads):
-        at = slice(h * DV, (h + 1) * DV)
-        for i, ref in enumerate((keys_ref, vals_ref, gate_ref)):
-            out_ref[:, h, i * DV:(i + 1) * DV] = ref[:, at]
-
-
-def joined_columns(both, go, heads, steps=4):
-    span, width = both.shape[0] // (2 * steps), both.shape[1]
-    first = pl.BlockSpec((span, width), lambda c: (c, 0))
-    return call(
-        functools.partial(joined_kernel, heads), "joined_columns", steps, 3,
-        [first, pl.BlockSpec((span, width), lambda c: (c + steps, 0)), first],
-        [(pl.BlockSpec((span, heads, HC), lambda c: (c, 0, 0)), sds((both.shape[0] // 2, heads, HC)))],
-        [],
-        both, both, go,
-    )[0]
-
-
 def split_kernel(grad_ref, out_ref):
     size = out_ref.shape[2]
     for i in range(2):
@@ -564,7 +546,7 @@
                    in_ref, keys_ref, vals_ref, gate_ref, in_row, in_col, out_ref, outg_ref, out_row, out_col,
                    ex_ref, exg_ref, ex_row, ex_col, sh_ref, shg_ref, sh_row, sh_col,
                    gains_grad, gains_second_new, gains_new, head_grad, head_second_new, head_new, conv_new,
-                   in_new, out_new, ex_new, sh_new):
+                   in_new, out_new, ex_new, sh_new, in_grad):
     beta_two = 1.0 - STEP ** (-0.8)
     counts = ((D, HEAD_TOTAL * HC), (HEAD_TOTAL * DV, D), (D, 2 * FF), (FF, D))
 
@@ -604,7 +586,9 @@
         for i, ref in enumerate((keys_ref, vals_ref, gate_ref)):
             col = in_col[:, i * width + h * DV:i * width + (h + 1) * DV]
             at = slice(i * DV, (i + 1) * DV)
-            in_new[:, h, at] = stepped(in_ref[:, h, at], ref[:, h * DV:(h + 1) * DV], in_row[...], col, 0)
+            grad = ref[:, h * DV:(h + 1) * DV]
+            in_grad[:, h, at] = grad
+            in_new[:, h, at] = stepped(in_ref[:, h, at], grad, in_row[...], col, 0)
     out_new[...] = stepped(out_ref[...], outg_ref[...], out_row[...], out_col[...], 1)
     size = ex_ref.shape[2]
     for i in range(2):
@@ -631,6 +615,8 @@
         ins.append(whole(cols.shape))
         operands.append(cols)
         outs.append((blocked(weight, span), sds(weight.shape)))
+    weight = groups[0][0]
+    outs.append((blocked(weight, weight.shape[0] // steps), sds(weight.shape)))
     return call(functools.partial(weights_kernel, heads), "new_weights", steps, 10, ins, outs, [], *operands, room=56)
 
 
@@ -692,13 +678,16 @@
     return lax.psum_scatter(x, "head", scatter_dimension=axis, tiled=True)
 
 
-def total_over(axis, x):
+def total_over(axis, x, arrived=None):
     n = lax.axis_size(axis)
     if n & (n - 1):
         return lax.psum(x, axis)
     step = 1
     while step < n:
-        x = x + lax.ppermute(x, axis, [(i, i ^ step) for i in range(n)])
+        other = lax.ppermute(x, axis, [(i, i ^ step) for i in range(n)])
+        if arrived is not None:
+            arrived.append(other)
+        x = x + other
         step *= 2
     return x
 
@@ -926,18 +915,19 @@
     d_rows_in = jnp.concatenate([d_rows_more[: tokens - RIM], d_rows_more[tokens - RIM : tokens] + rim_back], 0)
     feed_sums = (jnp.sum(expand_g * expand_g, 0), jnp.sum(shrink_g * shrink_g, 1))
     feed_sums += (jnp.sum(expand_g * expand_g, 1), jnp.sum(shrink_g * shrink_g, 0))
-    for step in range(2, n):
-        gone, part = sent, parts[step - 2]
-        if step < n - 1:
-            sent = ring(added(gone, part).astype(BF))
+    for step in range(2, n - 1):
+        total = added(sent, parts[step - 2]).astype(BF)
+        if step < n - 2:
+            sent = ring(total)
+    gate_held, sent = total[:in_span], ring(total[in_span:])
     d_normed_low = scatter_head(after(d_rows_in, expand_low, sent))
-    both = added(gone[2 * in_span :], part[2 * in_span :]).astype(BF)
-    last_sent = ring(both)
-    go = added(gone[: 2 * in_span], part[: 2 * in_span])
-    go, last_sent, *feed_sums = lax.optimization_barrier((go, last_sent, *feed_sums))
-    both_grad = added(last_sent, last_part)
-    go = lax.optimization_barrier(go)
-    out_g = lax.optimization_barrier(go[in_span:].T)
+    part = parts[-1]
+    both = added(sent[in_span:], part[2 * in_span :]).astype(BF)
+    last_sent = ring(jnp.concatenate([gate_held, both], 0))
+    out_g = added(sent[:in_span], part[in_span : 2 * in_span])
+    expand_out = split_columns(expand_low)
+    out_g, last_sent, expand_out, *feed_sums = lax.optimization_barrier((out_g.T, last_sent, expand_out, *feed_sums))
+    both_grad, go = added(last_sent[in_span:], last_part), added(last_sent[:in_span], part[:in_span])
     d_normed = d_normed_low.astype(F32)
 
     _, norm_one_pull = jax.vjp(norm_rows, x, norm_gains[0])
@@ -945,7 +935,7 @@
     input_grad = d_residual + d_residual_one
 
 
-    out_sq, both_sq, gate_sq = out_g * out_g, both_grad * both_grad, go[:in_span] * go[:in_span]
+    out_sq, both_sq, gate_sq = out_g * out_g, both_grad * both_grad, go * go
     over_head, head_cells = padded(
         {
             "expand_cols": feed_sums[0],
@@ -965,10 +955,8 @@
             "in_cols": jnp.concatenate([jnp.sum(a, 0) for a in (both_sq[:in_span], both_sq[in_span:], gate_sq)]),
         }
     )
-    both_then, over_head, over_seq = lax.optimization_barrier((both_grad, over_head, over_seq))
-    in_grad = joined_columns(both_then, go, heads)
-    expand_out = split_columns(expand_low)
-    over_head, over_seq = total_over("head", over_head), total_over("seq", over_seq)
+    arrived = []
+    over_head, over_seq = total_over("head", over_head, arrived), total_over("seq", over_seq, arrived)
 
     cells = {}
     for axis, found in (("head", head_cells), ("seq", seq_cells)):
@@ -991,12 +979,12 @@
         [over_head, over_seq, old_moments, weight_sums, place, conv_second,
          both_grad, go, out_g, expand_low, shrink_low],
     )
-    feed_sum = lax.psum_scatter(after(feed_part, d_normed_low, late), "seq", scatter_dimension=0, tiled=True).astype(F32)
+    feed_sum = lax.psum_scatter(after(feed_part, d_normed_low, arrived[1], arrived[-1]), "seq", scatter_dimension=0, tiled=True).astype(F32)
     block_out = (residual + feed_sum).astype(BF)
 
     late = total_over("seq", total_over("head", jnp.concatenate([late, d_gain_one[None]], 1)))
     (gains_grad, gains_second_new, gains_new, head_gain_grad, head_second_new, head_new, conv_new,
-     in_new, out_new, expand_new, shrink_new) = new_weights(
+     in_new, out_new, expand_new, shrink_new, in_grad) = new_weights(
         heads,
         (late, norm_gains, gains_second, head_gain[None], head_gain_second[None], conv_kernel, conv_update),
         [

time: 683 us -> 673 us (0.985)
  local copies, waits for them, and re-layouts: 60.1 us -> 50 us
    ppermute x10, waiting for transfers between devices: 56.8 us -> 44.6 us  [ahead(): lax.ppermute(x, 'seq', [(i, i + by) for i in range(n) if 0 <= i + by < n])]
    unnamed x266 -> x272, local copies, waits for them, and re-layouts: 34 us -> 26.4 us
    pallas_call x8 -> x7, Pallas kernels: 81.8 us -> 78.7 us  [call(): pl.pallas_call(kernel, grid=(n,), in_specs=ins, out_specs=[spec for spec,...]
  transfers between devices with their start and end apart: 51 -> 51, of which waited for: 29 -> 30; matrix products, arithmetic and copies ran while one was open for 26% -> 26% of each run, Pallas kernels for 13% -> 13%
where the time goes in v4:
time: 673 us; the launch traced here: 666 us
  waiting for transfers between devices  304 us (45%)
  matrix products  96.6 us (14%)
  Pallas kernels  85.1 us (13%)
  other arithmetic  61.4 us (9%)
  starting transfers between devices  52.4 us (8%)
  local copies, waits for them, and re-layouts  50 us (7%)
  between operations  16.3 us (2%)
    ppermute x22, waiting for transfers between devices, ring(): return lax.ppermute(x, 'seq', [(i, (i + by) % n) for i in range(n)])  226 us
    dot_general x37, matrix products, dot(): return lax.dot_general(a, b, (dims, ((), ())), preferred_element_type=out)  96.4 us
    pallas_call x7, Pallas kernels, call(): pl.pallas_call(kernel, grid=(n,), in_specs=ins, out_specs=[spec for spec,...  78.7 us
    ppermute x10, waiting for transfers between devices, ahead(): lax.ppermute(x, 'seq', [(i, i + by) for i in range(n) if 0 <= i + by < n])  44.6 us
    unnamed x272, local copies, waits for them, and re-layouts  26.4 us
    ppermute x10, starting transfers between devices, ahead(): lax.ppermute(x, 'seq', [(i, i + by) for i in range(n) if 0 <= i + by < n])  23.8 us
    ppermute x10, waiting for transfers between devices, total_over(): other = lax.ppermute(x, axis, [(i, i ^ step) for i in range(n)])  21 us
    ppermute x22, starting transfers between devices, ring(): return lax.ppermute(x, 'seq', [(i, (i + by) % n) for i in range(n)])  20.1 us
  transfers between devices with their start and end apart: 51, of which 30 were waited for; matrix products, arithmetic and copies ran while one was open for 26% of the time, Pallas kernels for 13%

profile of v4, /device:TPU:0, one launch (start us, length us, event | category | flops | bytes accessed | tf_op | source)
XLA Modules:
  0.0 665.6 jit_solution(14565965062794213182)
XLA Ops:
  27.2 23.0 %collective-permute-done.3 = bf16[512,1024]{1,0:T(8,128)(2,1)} collective-permute-done((bf16[512,1024]{1,0:T(8,128)(2,1)S(1)}, bf16[512,1024]{1,0:T(8,128)(2,1)}, u32[]{:S(2)}, u32[]{:S(2)}) %collective-permute-start.3) | collective-permute-done | bytes 1048608 | tf_op jit(solution)/shard_map/ppermute | solution.py:625
  68.7 14.6 %collective-permute-done.4 = bf16[512,1024]{1,0:T(8,128)(2,1)S(1)} collective-permute-done((bf16[512,1024]{1,0:T(8,128)(2,1)}, bf16[512,1024]{1,0:T(8,128)(2,1)S(1)}, u32[]{:S(2)}, u32[]{:S(2)}) %collective-permute-start.4) | collective-permute-done | bytes 1048608 | tf_op jit(solution)/shard_map/ppermute | solution.py:625
  87.5 22.1 %collective-permute-done.6 = bf16[512,1024]{1,0:T(8,128)(2,1)S(1)} collective-permute-done((bf16[512,1024]{1,0:T(8,128)(2,1)S(1)}, bf16[512,1024]{1,0:T(8,128)(2,1)S(1)}, u32[]{:S(2)}, u32[]{:S(2)}) %collective-permute-start.6) | collective-permute-done | bytes 1048608 | tf_op jit(solution)/shard_map/ppermute | solution.py:625
  113.9 20.4 %delta_parts.1 = (f32[1024,1024]{1,0:T(8,128)}, bf16[1024,256]{1,0:T(8,128)(2,1)S(1)}, bf16[1024,256]{1,0:T(8,128)(2,1)S(1)}, bf16[8,2,128,128]{3,2,1,0:T(8,128)...) custom-call(f32[1024,1024]{1,0:T(8,128)} %add_add_fusion.p_ref.halo_, ...), custom_call_target="tpu_custom_call" | custom-call | flops 3500000 | bytes 35000 | tf_op jit(solution)/shard_map/delta_parts/pallas_call | solution.py:141
  142.1 22.6 %collective-permute-done.8.refs_5_ = bf16[1024,512]{1,0:T(8,128)(2,1)} collective-permute-done((bf16[1024,512]{1,0:T(8,128)(2,1)S(1)}, bf16[1024,512]{1,0:T(8,128)(2,1)}, u32[]{:S(2)}, u32[]{:S(2)}) %collective-permute-start.8) | collective-permute-done | bytes 1048608 | tf_op jit(solution)/shard_map/ppermute | solution.py:625
  169.0 6.2 collective-permute-start.11
  182.3 10.9 %collective-permute-done.9.refs_6_ = bf16[1024,512]{1,0:T(8,128)(2,1)S(1)} collective-permute-done((bf16[1024,512]{1,0:T(8,128)(2,1)}, bf16[1024,512]{1,0:T(8,128)(2,1)S(1)}, u32[]{:S(2)}, u32[]{:S(2)}) %collective-permute-start.9) | collective-permute-done | bytes 1048608 | tf_op jit(solution)/shard_map/ppermute | solution.py:625
  199.4 9.3 %delta_outputs.1 = (bf16[8,2,128,256]{3,2,1,0:T(8,128)(2,1)S(1)}, f32[1024,512]{1,0:T(8,128)}, bf16[1024,512]{1,0:T(8,128)(2,1)S(1)}, bf16[1024,2048]{1,0:T(8,128)(2,1)}) custom-call(f32[8,2,128,384]{3,2,1,0:T(8,128)} %get-tuple-element.147.pre_ref, bf16[1024,256]{1,0:T(8,128)(2,1)S(1)} %copy-done.6, f32[1024,512]{1,0:T(8,128)} %get-tuple-element.149.oz_ref, ...), custom_call_target="tpu_custom_call" | custom-call | flops 700000 | bytes 7000 | tf_op jit(solution)/shard_map/delta_outputs/pallas_call | solution.py:141
  238.6 11.5 %collective-permute-done.16 = bf16[128,2048]{1,0:T(8,128)(2,1)S(1)} collective-permute-done((bf16[128,2048]{1,0:T(8,128)(2,1)}, bf16[128,2048]{1,0:T(8,128)(2,1)S(1)}, u32[]{:S(2)}, u32[]{:S(2)}) %collective-permute-start.16) | collective-permute-done | bytes 524320 | tf_op jit(solution)/shard_map/ppermute | solution.py:625
  269.7 7.2 %fusion.121 = f32[512,1408]{1,0:T(8,128)S(1)} fusion(bf16[512,2048]{1,0:T(8,128)(2,1)} %constant_dynamic-update-slice_fusion.17, bf16[1408,2048]{1,0:T(8,128)(2,1)} %all-gather.9.cloned.1.call-done), kind=kOutput, calls=%fused_computation.284 | convolution fusion | flops 2952790016 | bytes 10747904 | tf_op jit(solution)/shard_map/dot_general | solution.py:696
  277.0 6.7 %collective-permute-done.18 = bf16[128,2048]{1,0:T(8,128)(2,1)S(1)} collective-permute-done((bf16[128,2048]{1,0:T(8,128)(2,1)S(1)}, bf16[128,2048]{1,0:T(8,128)(2,1)S(1)}, u32[]{:S(2)}, u32[]{:S(2)}) %collective-permute-start.18) | collective-permute-done | bytes 524320 | tf_op jit(solution)/shard_map/ppermute | solution.py:625
  288.0 6.5 fusion.10
  294.5 8.1 %collective-permute-done.19 = bf16[128,2048]{1,0:T(8,128)(2,1)S(1)} collective-permute-done((bf16[128,2048]{1,0:T(8,128)(2,1)S(1)}, bf16[128,2048]{1,0:T(8,128)(2,1)S(1)}, u32[]{:S(2)}, u32[]{:S(2)}) %collective-permute-start.19) | collective-permute-done | bytes 524320 | tf_op jit(solution)/shard_map/ppermute | solution.py:625
  302.7 16.5 %collective-permute-done.20 = bf16[128,2048]{1,0:T(8,128)(2,1)S(1)} collective-permute-done((bf16[128,2048]{1,0:T(8,128)(2,1)S(1)}, bf16[128,2048]{1,0:T(8,128)(2,1)S(1)}, u32[]{:S(2)}, u32[]{:S(2)}) %collective-permute-start.20) | collective-permute-done | bytes 524320 | tf_op jit(solution)/shard_map/ppermute | solution.py:625
  319.2 6.5 fusion.35
  326.7 6.6 fusion.14
  333.4 13.3 %collective-permute-done.22 = bf16[128,2048]{1,0:T(8,128)(2,1)S(1)} collective-permute-done((bf16[128,2048]{1,0:T(8,128)(2,1)S(1)}, bf16[128,2048]{1,0:T(8,128)(2,1)S(1)}, u32[]{:S(2)}, u32[]{:S(2)}) %collective-permute-start.22) | collective-permute-done | bytes 524320 | tf_op jit(solution)/shard_map/ppermute | solution.py:625
  347.0 11.0 %collective-permute-done.23 = bf16[128,2048]{1,0:T(8,128)(2,1)S(1)} collective-permute-done((bf16[128,2048]{1,0:T(8,128)(2,1)S(1)}, bf16[128,2048]{1,0:T(8,128)(2,1)S(1)}, u32[]{:S(2)}, u32[]{:S(2)}) %collective-permute-start.23) | collective-permute-done | bytes 524320 | tf_op jit(solution)/shard_map/ppermute | solution.py:625
  365.2 6.6 fusion.123
  373.9 7.9 %fusion.122 = bf16[1408,2048]{1,0:T(8,128)(2,1)} fusion(bf16[512,1408]{1,0:T(8,128)(2,1)} %copy-done.65, bf16[512,2048]{1,0:T(8,128)(2,1)} %constant_dynamic-update-slice_fusion.17), kind=kOutput, calls=%fused_computation.285 | convolution fusion | flops 2952790016 | bytes 9306112 | tf_op jit(solution)/shard_map/dot_general | solution.py:696
  381.9 10.6 %fusion = bf16[2048,2816]{1,0:T(8,128)(2,1)} fusion(bf16[512,2048]{1,0:T(8,128)(2,1)} %pad_maximum_fusion.3, bf16[256,1408]{1,0:T(8,128)(2,1)} %copy-done.71, bf16[256,1408]{1,0:T(8,128)(2,1)} %copy-done.70, bf16[256,1408]{1,0:T(8,128)(2,1)S(1)} %copy-done.69, bf16[256,1408]{1,0:T(8,128)(2,1)S(1)} %copy-done.67), kind=kOutput, calls=%fused_computation.6 | convolution fusion | flops 5917114368 | bytes 16515072 | tf_op jit(solution)/shard_map/dot_general | solution.py:696
  395.9 8.7 %delta_states_back.1 = (bf16[1024,512]{1,0:T(8,128)(2,1)S(1)}, bf16[1024,512]{1,0:T(8,128)(2,1)S(1)}, f32[8,2,128,256]{3,2,1,0:T(8,128)S(1)}, bf16[2,128,256]{2,1,0:T(8,128)(2,1)S(1)}, f32[1,256]{1,0:T(1,128)S(1)}) custom-call(bf16[1024,2048]{1,0:T(8,128)(2,1)} %all-gather.11.cloned.1.call-done.drows_ref, ...), custom_call_target="tpu_custom_call" | custom-call | flops 700000 | bytes 7000 | tf_op jit(solution)/shard_map/delta_states_back/pallas_call | solution.py:141
  413.6 7.9 %collective-permute-done.25.refs_3_ = bf16[2,128,256]{2,1,0:T(8,128)(2,1)S(1)} collective-permute-done((bf16[2,128,256]{2,1,0:T(8,128)(2,1)S(1)}, bf16[2,128,256]{2,1,0:T(8,128)(2,1)S(1)}, u32[]{:S(2)}, u32[]{:S(2)}) %collective-permute-start.25) | collective-permute-done | bytes 131104 | tf_op jit(solution)/shard_map/ppermute | solution.py:630
  421.6 20.2 %delta_inputs_back.1 = (bf16[1040,1536]{1,0:T(8,128)(2,1)}, f32[4,1024]{1,0:T(4,128)S(1)}) custom-call(f32[8,2,128,256]{3,2,1,0:T(8,128)} %copy-done.8, bf16[8,2,128,128]{3,2,1,0:T(8,128)(2,1)S(1)} %get-tuple-element.179.m_ref, bf16[8,2,128,256]{3,2,1,0:T(8,128)(2,1)S(1)} %copy-done.10, bf16[1024,512]{1,0:T(8,128)(2,1)} %copy-done.13, ...), custom_call_target="tpu_custom_call" | custom-call | flops 1900000 | bytes 19000 | tf_op jit(solution)/shard_map/delta_inputs_back/pallas_call | solution.py:141
  441.8 6.0 collective-permute-done.27
  465.8 7.1 %fusion.126 = bf16[1040,2048]{1,0:T(8,128)(2,1)S(1)} fusion(bf16[1040,1536]{1,0:T(8,128)(2,1)S(1)} %copy-done.105, bf16[2048,1536]{1,0:T(8,128)(2,1)S(1)} %bitcast.140), kind=kOutput, calls=%fused_computation.289 | convolution fusion | flops 6543114240 | bytes 13746176 | tf_op jit(solution)/shard_map/dot_general | solution.py:696
  484.2 24.0 %collective-permute-done.29 = bf16[2048,512]{0,1:T(8,128)(2,1)S(1)} collective-permute-done((bf16[2048,512]{0,1:T(8,128)(2,1)}, bf16[2048,512]{0,1:T(8,128)(2,1)S(1)}, u32[]{:S(2)}, u32[]{:S(2)}) %collective-permute-start.29) | collective-permute-done | bytes 2097184 | tf_op jit(solution)/shard_map/ppermute | solution.py:625
  512.4 36.7 %collective-permute-done.28 = bf16[16,2048]{1,0:T(8,128)(2,1)S(1)} collective-permute-done((bf16[16,2048]{1,0:T(8,128)(2,1)S(1)}, bf16[16,2048]{1,0:T(8,128)(2,1)S(1)}, u32[]{:S(2)}, u32[]{:S(2)}) %collective-permute-start.28) | collective-permute-done | bytes 65568 | tf_op jit(solution)/shard_map/ppermute | solution.py:630
  560.3 31.9 %collective-permute-done.31 = bf16[1536,512]{0,1:T(8,128)(2,1)S(1)} collective-permute-done((bf16[1536,512]{0,1:T(8,128)(2,1)S(1)}, bf16[1536,512]{0,1:T(8,128)(2,1)S(1)}, u32[]{:S(2)}, u32[]{:S(2)}) %collective-permute-start.31) | collective-permute-done | bytes 1572896 | tf_op jit(solution)/shard_map/ppermute | solution.py:625
  599.3 4.7 collective-permute-done.35
  611.8 6.5 new_moments.1
  642.2 14.6 %new_weights.1 = (f32[2,2048]{1,0:T(2,128)}, f32[2,2048]{1,0:T(2,128)}, f32[2,2048]{1,0:T(2,128)}, f32[1,256]{1,0:T(1,128)}, f32[1,256]{1,0:T(1,128)}, /*index=5...) custom-call(f32[1,4480]{1,0:T(1,128)} %add.329.late_ref, ...), custom_call_target="tpu_custom_call" | custom-call | flops 1000000 | bytes 10000 | tf_op jit(solution)/shard_map/new_weights/pallas_call | solution.py:141
  (514 shorter events, 232.6 us)
Async XLA Ops:
  7.2 43.7 %all-gather.5.cloned.1.call-start = ((), (), s32[]{:S(2)}) async-start(), calls=%async_computation.5 | async-start | bytes 4718592 | tf_op jit(solution)/shard_map/all_gather | solution.py:674
  11.4 127.8 %all-gather.7.cloned.1.call-start = ((), (), s32[]{:S(2)}) async-start(), calls=%async_computation.6 | async-start | bytes 12976128 | tf_op jit(solution)/shard_map/all_gather | solution.py:674
  24.2 25.9 %collective-permute-start.3 = (bf16[512,1024]{1,0:T(8,128)(2,1)S(1)}, bf16[512,1024]{1,0:T(8,128)(2,1)}, u32[]{:S(2)}, u32[]{:S(2)}) collective-permute-start(bf16[512,1024]{1,0:T(8,128)(2,1)S(1)} %get-tuple-element.143), channel_id=1, source_target_pairs={{0,8},{8,16},{16,24},{24,0},{1,9},{9,17},{17,25},{25,1},{2,10},{10... | collective-permute-start | bytes 3145736 | tf_op jit(solution)/shard_map/ppermute | solution.py:625
  51.0 162.8 %all-gather.9.cloned.1.call-start = ((), (), s32[]{:S(2)}) async-start(), calls=%async_computation.7 | async-start | bytes 6488064 | tf_op jit(solution)/shard_map/all_gather | solution.py:674
  56.0 27.4 %collective-permute-start.4 = (bf16[512,1024]{1,0:T(8,128)(2,1)}, bf16[512,1024]{1,0:T(8,128)(2,1)S(1)}, u32[]{:S(2)}, u32[]{:S(2)}) collective-permute-start(bf16[512,1024]{1,0:T(8,128)(2,1)} %collective-permute-done.3), channel_id=1, source_target_pairs={{0,8},{8,16},{16,24},{24,0},{1,9},{9,17},{17,25},{25,1},{2,10},{10... | collective-permute-start | bytes 3145736 | tf_op jit(solution)/shard_map/ppermute | solution.py:625
  58.4 25.0 %collective-permute-start.5 = (bf16[16,2048]{1,0:T(8,128)(2,1)S(1)}, bf16[16,2048]{1,0:T(8,128)(2,1)S(1)}, u32[]{:S(2)}, u32[]{:S(2)}) collective-permute-start(bf16[16,2048]{1,0:T(8,128)(2,1)S(1)} %slice.223), channel_id=1, source_target_pairs={{0,8},{8,16},{16,24},{1,9},{9,17},{17,25},{2,10},{10,18},{18,26},{... | collective-permute-start | bytes 196616 | tf_op jit(solution)/shard_map/ppermute | solution.py:630
  83.4 26.3 %collective-permute-start.6 = (bf16[512,1024]{1,0:T(8,128)(2,1)S(1)}, bf16[512,1024]{1,0:T(8,128)(2,1)S(1)}, u32[]{:S(2)}, u32[]{:S(2)}) collective-permute-start(bf16[512,1024]{1,0:T(8,128)(2,1)S(1)} %collective-permute-done.4), channel_id=1, source_target_pairs={{0,8},{8,16},{16,24},{24,0},{1,9},{9,17},{17,25},{25,1},{2,10},{10... | collective-permute-start | bytes 3145736 | tf_op jit(solution)/shard_map/ppermute | solution.py:625
  109.7 29.5 %collective-permute-start.7 = (bf16[1024,512]{1,0:T(8,128)(2,1)S(1)}, bf16[1024,512]{1,0:T(8,128)(2,1)S(1)}, u32[]{:S(2)}, u32[]{:S(2)}) collective-permute-start(bf16[1024,512]{1,0:T(8,128)(2,1)S(1)} %pad_maximum_fusion.16.refs_3_), channel_id=1, source_target_pairs={{0,8},{8,16},{16,24},{24,0},{1,9},{9,17},{17,25},{25,1},{2,10},{10... | collective-permute-start | bytes 3145736 | tf_op jit(solution)/shard_map/ppermute | solution.py:625
  139.2 25.5 %collective-permute-start.8 = (bf16[1024,512]{1,0:T(8,128)(2,1)S(1)}, bf16[1024,512]{1,0:T(8,128)(2,1)}, u32[]{:S(2)}, u32[]{:S(2)}) collective-permute-start(bf16[1024,512]{1,0:T(8,128)(2,1)S(1)} %collective-permute-done.7.refs_4_), channel_id=1, source_target_pairs={{0,8},{8,16},{16,24},{24,0},{1,9},{9,17},{17,25},{25,1},{2,10},{10... | collective-permute-start | bytes 3145736 | tf_op jit(solution)/shard_map/ppermute | solution.py:625
  164.7 100.6 %reduce-scatter.6.cloned.1.call-start = ((), (), s32[]{:S(2)}) async-start(), calls=%async_computation.8 | async-start | bytes 4718592 | tf_op jit(solution)/shard_map/reduce_scatter | solution.py:678
  167.0 26.2 %collective-permute-start.9 = (bf16[1024,512]{1,0:T(8,128)(2,1)}, bf16[1024,512]{1,0:T(8,128)(2,1)S(1)}, u32[]{:S(2)}, u32[]{:S(2)}) collective-permute-start(bf16[1024,512]{1,0:T(8,128)(2,1)} %collective-permute-done.8.refs_5_), channel_id=1, source_target_pairs={{0,8},{8,16},{16,24},{24,0},{1,9},{9,17},{17,25},{25,1},{2,10},{10... | collective-permute-start | bytes 3145736 | tf_op jit(solution)/shard_map/ppermute | solution.py:625
  167.0 32.3 %collective-permute-start.10 = (bf16[2,128,384]{2,1,0:T(8,128)(2,1)S(1)}, bf16[2,128,384]{2,1,0:T(8,128)(2,1)S(1)}, u32[]{:S(2)}, u32[]{:S(2)}) collective-permute-start(bf16[2,128,384]{2,1,0:T(8,128)(2,1)S(1)} %get-tuple-element.156), channel_id=1, source_target_pairs={{0,8},{8,16},{16,24},{1,9},{9,17},{17,25},{2,10},{10,18},{18,26},{... | collective-permute-start | bytes 589832 | tf_op jit(solution)/shard_map/ppermute | solution.py:630
  169.0 30.3 %collective-permute-start.11 = (bf16[2,128,384]{2,1,0:T(8,128)(2,1)S(1)}, bf16[2,128,384]{2,1,0:T(8,128)(2,1)S(1)}, u32[]{:S(2)}, u32[]{:S(2)}) collective-permute-start(bf16[2,128,384]{2,1,0:T(8,128)(2,1)S(1)} %get-tuple-element.156), channel_id=1, source_target_pairs={{0,16},{8,24},{1,17},{9,25},{2,18},{10,26},{3,19},{11,27},{4,20},{... | collective-permute-start | bytes 589832 | tf_op jit(solution)/shard_map/ppermute | solution.py:630
  175.9 59.5 %collective-permute-start.14 = (bf16[2,128,128]{2,1,0:T(8,128)(2,1)}, bf16[2,128,128]{2,1,0:T(8,128)(2,1)S(1)}, u32[]{:S(2)}, u32[]{:S(2)}) collective-permute-start(bf16[2,128,128]{2,1,0:T(8,128)(2,1)} %slice.192), channel_id=1, source_target_pairs={{8,0},{16,8},{24,16},{9,1},{17,9},{25,17},{10,2},{18,10},{26,18},{... | collective-permute-start | bytes 196616 | tf_op jit(solution)/shard_map/ppermute | solution.py:630
  177.2 58.2 %collective-permute-start.15 = (bf16[2,128,128]{2,1,0:T(8,128)(2,1)}, bf16[2,128,128]{2,1,0:T(8,128)(2,1)}, u32[]{:S(2)}, u32[]{:S(2)}) collective-permute-start(bf16[2,128,128]{2,1,0:T(8,128)(2,1)} %slice.192), channel_id=1, source_target_pairs={{16,0},{24,8},{17,1},{25,9},{18,2},{26,10},{19,3},{27,11},{20,4},{... | collective-permute-start | bytes 196616 | tf_op jit(solution)/shard_map/ppermute | solution.py:630
  210.7 24.8 %collective-permute-start.13 = (bf16[128,2048]{1,0:T(8,128)(2,1)}, bf16[128,2048]{1,0:T(8,128)(2,1)}, u32[]{:S(2)}, u32[]{:S(2)}) collective-permute-start(bf16[128,2048]{1,0:T(8,128)(2,1)} %param.23), channel_id=1, source_target_pairs={{0,8},{8,16},{16,24},{24,0},{1,9},{9,17},{17,25},{25,1},{2,10},{10... | collective-permute-start | bytes 1572872 | tf_op jit(solution)/shard_map/ppermute | solution.py:625
  213.8 181.9 %all-gather.11.cloned.1.call-start = ((), (), s32[]{:S(2)}) async-start(), calls=%async_computation.9 | async-start | bytes 4718592 | tf_op jit(solution)/shard_map/all_gather | solution.py:674
  235.4 14.6 %collective-permute-start.16 = (bf16[128,2048]{1,0:T(8,128)(2,1)}, bf16[128,2048]{1,0:T(8,128)(2,1)S(1)}, u32[]{:S(2)}, u32[]{:S(2)}) collective-permute-start(bf16[128,2048]{1,0:T(8,128)(2,1)} %collective-permute-done.13), channel_id=1, source_target_pairs={{0,8},{8,16},{16,24},{24,0},{1,9},{9,17},{17,25},{25,1},{2,10},{10... | collective-permute-start | bytes 1572872 | tf_op jit(solution)/shard_map/ppermute | solution.py:625
  268.0 15.7 %collective-permute-start.18 = (bf16[128,2048]{1,0:T(8,128)(2,1)S(1)}, bf16[128,2048]{1,0:T(8,128)(2,1)S(1)}, u32[]{:S(2)}, u32[]{:S(2)}) collective-permute-start(bf16[128,2048]{1,0:T(8,128)(2,1)S(1)} %multiply_convert_fusion.6), channel_id=1, source_target_pairs={{0,8},{8,16},{16,24},{24,0},{1,9},{9,17},{17,25},{25,1},{2,10},{10... | collective-permute-start | bytes 1572872 | tf_op jit(solution)/shard_map/ppermute | solution.py:625
  287.9 14.6 %collective-permute-start.19 = (bf16[128,2048]{1,0:T(8,128)(2,1)S(1)}, bf16[128,2048]{1,0:T(8,128)(2,1)S(1)}, u32[]{:S(2)}, u32[]{:S(2)}) collective-permute-start(bf16[128,2048]{1,0:T(8,128)(2,1)S(1)} %collective-permute-done.18), channel_id=1, source_target_pairs={{0,8},{8,16},{16,24},{24,0},{1,9},{9,17},{17,25},{25,1},{2,10},{10... | collective-permute-start | bytes 1572872 | tf_op jit(solution)/shard_map/ppermute | solution.py:625
  302.6 16.7 %collective-permute-start.20 = (bf16[128,2048]{1,0:T(8,128)(2,1)S(1)}, bf16[128,2048]{1,0:T(8,128)(2,1)S(1)}, u32[]{:S(2)}, u32[]{:S(2)}) collective-permute-start(bf16[128,2048]{1,0:T(8,128)(2,1)S(1)} %collective-permute-done.19), channel_id=1, source_target_pairs={{0,8},{8,16},{16,24},{24,0},{1,9},{9,17},{17,25},{25,1},{2,10},{10... | collective-permute-start | bytes 1572872 | tf_op jit(solution)/shard_map/ppermute | solution.py:625
  302.6 30.6 %collective-permute-start.21 = (bf16[128,2048]{1,0:T(8,128)(2,1)S(1)}, bf16[128,2048]{1,0:T(8,128)(2,1)S(1)}, u32[]{:S(2)}, u32[]{:S(2)}) collective-permute-start(bf16[128,2048]{1,0:T(8,128)(2,1)S(1)} %slice.352), channel_id=1, source_target_pairs={{0,8},{8,16},{16,24},{24,0},{1,9},{9,17},{17,25},{25,1},{2,10},{10... | collective-permute-start | bytes 1572872 | tf_op jit(solution)/shard_map/ppermute | solution.py:625
  361.6 96.9 %reduce-scatter.8.cloned.1.call-start = ((), (), s32[]{:S(2)}) async-start(), calls=%async_computation.10 | async-start | bytes 6488064 | tf_op jit(solution)/shard_map/reduce_scatter | solution.py:678
  395.8 155.6 %reduce-scatter.10.cloned.1.call-start = ((), (), s32[]{:S(2)}) async-start(), calls=%async_computation.11 | async-start | bytes 12976128 | tf_op jit(solution)/shard_map/reduce_scatter | solution.py:678
  405.9 15.6 %collective-permute-start.25 = (bf16[2,128,256]{2,1,0:T(8,128)(2,1)S(1)}, bf16[2,128,256]{2,1,0:T(8,128)(2,1)S(1)}, u32[]{:S(2)}, u32[]{:S(2)}) collective-permute-start(bf16[2,128,256]{2,1,0:T(8,128)(2,1)S(1)} %get-tuple-element.191), channel_id=1, source_target_pairs={{16,0},{24,8},{17,1},{25,9},{18,2},{26,10},{19,3},{27,11},{20,4},{... | collective-permute-start | bytes 393224 | tf_op jit(solution)/shard_map/ppermute | solution.py:630
  421.5 26.3 %collective-permute-start.27 = (bf16[1024,512]{0,1:T(8,128)(2,1)S(1)}, bf16[1024,512]{0,1:T(8,128)(2,1)S(1)}, u32[]{:S(2)}, u32[]{:S(2)}) collective-permute-start(bf16[1024,512]{0,1:T(8,128)(2,1)S(1)} %pad_maximum_fusion.17), channel_id=1, source_target_pairs={{0,8},{8,16},{16,24},{24,0},{1,9},{9,17},{17,25},{25,1},{2,10},{10... | collective-permute-start | bytes 3145736 | tf_op jit(solution)/shard_map/ppermute | solution.py:625
  458.6 145.6 %reduce-scatter.12.cloned.1.call-start = ((), (), s32[]{:S(2)}) async-start(), calls=%async_computation.12 | async-start | bytes 4718592 | tf_op jit(solution)/shard_map/reduce_scatter | solution.py:678
  458.6 49.6 %collective-permute-start.29 = (bf16[2048,512]{0,1:T(8,128)(2,1)}, bf16[2048,512]{0,1:T(8,128)(2,1)S(1)}, u32[]{:S(2)}, u32[]{:S(2)}) collective-permute-start(bf16[2048,512]{0,1:T(8,128)(2,1)} %pad_maximum_fusion.5), channel_id=1, source_target_pairs={{0,8},{8,16},{16,24},{24,0},{1,9},{9,17},{17,25},{25,1},{2,10},{10... | collective-permute-start | bytes 6291464 | tf_op jit(solution)/shard_map/ppermute | solution.py:625
  510.4 40.9 %collective-permute-start.30 = (bf16[1536,512]{0,1:T(8,128)(2,1)}, bf16[1536,512]{0,1:T(8,128)(2,1)}, u32[]{:S(2)}, u32[]{:S(2)}) collective-permute-start(bf16[1536,512]{0,1:T(8,128)(2,1)} %slice.250), channel_id=1, source_target_pairs={{0,8},{8,16},{16,24},{24,0},{1,9},{9,17},{17,25},{25,1},{2,10},{10... | collective-permute-start | bytes 4718600 | tf_op jit(solution)/shard_map/ppermute | solution.py:625
  510.8 38.3 %collective-permute-start.28 = (bf16[16,2048]{1,0:T(8,128)(2,1)S(1)}, bf16[16,2048]{1,0:T(8,128)(2,1)S(1)}, u32[]{:S(2)}, u32[]{:S(2)}) collective-permute-start(bf16[16,2048]{1,0:T(8,128)(2,1)S(1)} %slice.249), channel_id=1, source_target_pairs={{8,0},{16,8},{24,16},{9,1},{17,9},{25,17},{10,2},{18,10},{26,18},{... | collective-permute-start | bytes 196616 | tf_op jit(solution)/shard_map/ppermute | solution.py:630
  551.4 105.5 %reduce-scatter.14.cloned.1.call-start = ((), (), s32[]{:S(2)}) async-start(), calls=%async_computation.13 | async-start | bytes 2621440 | tf_op jit(solution)/shard_map/reduce_scatter | solution.py:982
  553.9 38.3 %collective-permute-start.31 = (bf16[1536,512]{0,1:T(8,128)(2,1)S(1)}, bf16[1536,512]{0,1:T(8,128)(2,1)S(1)}, u32[]{:S(2)}, u32[]{:S(2)}) collective-permute-start(bf16[1536,512]{0,1:T(8,128)(2,1)S(1)} %pad_maximum_fusion.10), channel_id=1, source_target_pairs={{0,8},{8,16},{16,24},{24,0},{1,9},{9,17},{17,25},{25,1},{2,10},{10... | collective-permute-start | bytes 4718600 | tf_op jit(solution)/shard_map/ppermute | solution.py:625
  (131 other events, 1408.8 us)
Sparse Core Ops, SparseCore 0:
  11.5 39.4 all-gather.4
  53.4 67.6 all-gather.6
  164.9 42.5 all-gather.8
  214.0 51.3 reduce-scatter.5
  361.8 33.9 all-gather.10
  399.4 59.0 reduce-scatter.7
  462.0 86.7 reduce-scatter.9
  552.2 51.8 reduce-scatter.11
  606.5 44.0 reduce-scatter.13
